TPU v7x, 256 devices: a whole 4x4x8 slice. The times are simulated.
256 devices in a mesh: macro: 32 (over z, y), pencil: 8 (over x, core).
Axes of the slice: x: 4, y: 4, z: 8, core: 2. Of those that a mesh axis runs over, the one named last changes fastest.
Arguments:
- voxel_material_ids: int32 [32, 128, 128, 128], P('macro', 'pencil'), may hold values from 0 to 2
- fiber_fraction: float32 [32, 128, 128, 128], P('macro', 'pencil'), may hold values from 0.5 to 18, as said below
- material_matrix_diffusivity: float32 [32, 3], P('macro'), may hold values from 0.2 to 5
- mesh_point_thermal_state: float32 [128], P('macro'), may hold values from 0.5 to 1.5
- element_corner_ids: int32 [32, 8], P('macro'), may hold values from 0 to 127, all different within a row
- global_entry_position: int32 [128], P('macro'), may hold values from 0 to 127, each once
- sample_choice_per_point: int32 [32], P('macro'), may hold values from 0 to 31, as said below
Outputs:
- qp_flux: float32 [32, 3], P('macro')
- nodal_flux: float32 [128], P('macro')
Inputs may be any that keep to these rules, and one draw needn't show every extreme that they name: `fiber_fraction`: positive. `sample_choice_per_point`: exactly 8 microstructures are used by 2 points each, 16 by 1 points each, and the rest by none.
All inputs are finite; a program needn't handle non-finite values.
Results may differ from a plain program's by a relative error of at most 0.0003.
Values sent between devices are 32-bit elements; how exact they have to be, the bound alone decides.
No kernel may reach another device: no remote copies, remote signals or barrier semaphores. Data moves between devices by JAX's collectives and lax.ppermute only.
A program may use at most 64 MiB of HBM per device.

v0:
```python
import math

import jax
import jax.numpy as jnp
from jax import lax
from jax.sharding import PartitionSpec as P

PHASES = 3
ITERS = 2


HIGHEST = lax.Precision.HIGHEST


def passed_along(array, axis, by):
    size = lax.axis_size(axis)
    return lax.ppermute(array, axis, [(i, (i + by) % size) for i in range(size)])


def corner_signs():
    table = [
        [2.0 * (corner >> device_axis & 1) - 1.0 for device_axis in range(3)] for corner in range(8)
    ]
    return jnp.array(table, dtype=jnp.float32)


def base_field(voxel_material_ids, fiber_fraction, phase_lookup_table):
    conduct = jnp.zeros(fiber_fraction.shape, jnp.float32)
    for phase in range(PHASES):
        conduct = conduct + jnp.where(voxel_material_ids == phase, phase_lookup_table[phase], 0.0)
    return conduct * fiber_fraction


def fourier_tables(length):
    index = jnp.arange(length, dtype=jnp.int32)
    product = index[:, None] * index[None, :] % length
    angle = 2.0 * math.pi / length * product.astype(jnp.float32)
    return (jnp.cos(angle), jnp.sin(angle))


def complex_transform_pass(real_part, imag_part, cosine, sine, form, sign):
    real_cos = jnp.einsum(form, real_part, cosine, precision=HIGHEST)
    real_sin = jnp.einsum(form, real_part, sine, precision=HIGHEST)
    imag_cos = jnp.einsum(form, imag_part, cosine, precision=HIGHEST)
    imag_sin = jnp.einsum(form, imag_part, sine, precision=HIGHEST)
    return (real_cos - sign * imag_sin, imag_cos + sign * real_sin)


def forward_spectrum(field, cosine, sine):
    real_part = jnp.dot(field, cosine, precision=HIGHEST)
    imag_part = -jnp.dot(field, sine, precision=HIGHEST)
    real_part, imag_part = complex_transform_pass(
        real_part, imag_part, cosine, sine, "ink,nm->imk", -1.0
    )
    return complex_transform_pass(
        lax.all_to_all(real_part, "pencil", split_axis=1, concat_axis=0, tiled=True),
        lax.all_to_all(imag_part, "pencil", split_axis=1, concat_axis=0, tiled=True),
        cosine,
        sine,
        "nbk,nm->mbk",
        -1.0,
    )


def inverse_field(real_part, imag_part, cosine, sine):
    real_part, imag_part = complex_transform_pass(
        real_part, imag_part, cosine, sine, "nbk,nm->mbk", 1.0
    )
    real_part, imag_part = complex_transform_pass(
        lax.all_to_all(real_part, "pencil", split_axis=0, concat_axis=1, tiled=True),
        lax.all_to_all(imag_part, "pencil", split_axis=0, concat_axis=1, tiled=True),
        cosine,
        sine,
        "ink,nm->imk",
        1.0,
    )
    return jnp.dot(real_part, cosine, precision=HIGHEST) - jnp.dot(
        imag_part, sine, precision=HIGHEST
    )


def divergence(field, reference_k, gradient_field):
    contrast = field - reference_k
    polar = [contrast * gradient_field[device_axis] for device_axis in range(3)]
    below = passed_along(polar[0][-1:], "pencil", 1)
    behind = jnp.concatenate([below, polar[0][:-1]], axis=0)
    first = polar[0] - behind
    second = polar[1] - jnp.roll(polar[1], 1, axis=1)
    third = polar[2] - jnp.roll(polar[2], 1, axis=2)
    return first + second + third


def on_device(
    voxel_material_ids,
    fiber_fraction,
    material_matrix_diffusivity,
    mesh_point_thermal_state,
    element_corner_ids,
    global_entry_position,
    sample_choice_per_point,
):
    macro_index = lax.axis_index("macro")
    pencil_index = lax.axis_index("pencil")
    slab = fiber_fraction.shape[1]
    width = fiber_fraction.shape[3]
    volume = float(width**3)
    per_device = element_corner_ids.shape[0]
    cosine, sine = fourier_tables(width)
    conduct = base_field(voxel_material_ids[0], fiber_fraction[0], material_matrix_diffusivity[0])
    totals = lax.psum((jnp.sum(conduct), jnp.sum(conduct * conduct)), "pencil")
    stats = jnp.stack(totals).reshape(1, 2)
    mesh_point_flux_result = lax.all_gather(mesh_point_thermal_state, "macro", axis=0, tiled=True)
    rows_all, assign_all = (
        lax.all_gather(global_entry_position, "macro", axis=0, tiled=True),
        lax.all_gather(sample_choice_per_point, "macro", axis=0, tiled=True),
    )
    nodes = mesh_point_flux_result.shape[0]
    node_ids = jnp.arange(nodes, dtype=jnp.int32)
    picks = element_corner_ids[:, :, None] == node_ids
    fourier_argument = jnp.sum(jnp.where(picks, mesh_point_flux_result, 0.0), axis=2)
    rows = jnp.sum(jnp.where(picks, rows_all, 0), axis=2)
    signs = corner_signs()
    gradient = jnp.dot(fourier_argument, signs, precision=HIGHEST) / 4.0
    heat = jnp.sum(fourier_argument, axis=1) / 8.0
    gradients_all, heat_all, stats_all = (
        lax.all_gather(gradient, "macro", axis=0, tiled=True),
        lax.all_gather(heat, "macro", axis=0, tiled=True),
        lax.all_gather(stats, "macro", axis=0, tiled=True),
    )
    points = assign_all.shape[0]
    point_ids = jnp.arange(points, dtype=jnp.int32)
    same_group = assign_all[:, None] == assign_all[None, :]
    earlier = point_ids[None, :] < point_ids[:, None]
    rank = jnp.sum((same_group & earlier).astype(jnp.int32), axis=1)
    slots = 2 * per_device
    source_stats = stats_all[macro_index]
    slot_ids = jnp.arange(slots, dtype=jnp.int32)
    select = (assign_all[None, :] == macro_index) & (rank[None, :] == slot_ids[:, None])
    slot_gradient = jnp.sum(jnp.where(select[:, :, None], gradients_all[None, :, :], 0.0), axis=1)
    slot_heat = jnp.sum(jnp.where(select, heat_all[None, :], 0.0), axis=1)
    line_angle = 2.0 * math.pi / width * jnp.arange(width, dtype=jnp.int32).astype(jnp.float32)
    block_modes = pencil_index * slab + jnp.arange(slab, dtype=jnp.int32)
    block_angle = 2.0 * math.pi / width * block_modes.astype(jnp.float32)
    line_cos = jnp.cos(line_angle)
    block_cos = jnp.cos(block_angle)
    eigen = (
        (2.0 - 2.0 * line_cos)[:, None, None]
        + (2.0 - 2.0 * block_cos)[None, :, None]
        + (2.0 - 2.0 * line_cos)[None, None, :]
    )
    positive = eigen > 0
    inverse_eigen = jnp.where(positive, 1.0 / (volume * jnp.where(positive, eigen, 1.0)), 0.0)

    def solve_slot(carry, packed):
        point_gradient, point_heat = packed
        radiative = point_heat**3
        field = conduct + radiative
        mean_square = (
            source_stats[1] + 2.0 * radiative * source_stats[0]
        ) / volume + radiative * radiative
        reference_k = jnp.sqrt(mean_square)
        weight = inverse_eigen / reference_k
        gradient_field = [
            point_gradient[device_axis] + jnp.zeros_like(field) for device_axis in range(3)
        ]
        for sweep in range(ITERS):
            spectrum = forward_spectrum(
                divergence(field, reference_k, gradient_field), cosine, sine
            )
            potential = inverse_field(spectrum[0] * weight, spectrum[1] * weight, cosine, sine)
            above = passed_along(potential[:1], "pencil", -1)
            ahead = jnp.concatenate([potential[1:], above], axis=0)
            gradient_field = [
                point_gradient[0] + ahead - potential,
                point_gradient[1] + jnp.roll(potential, -1, axis=1) - potential,
                point_gradient[2] + jnp.roll(potential, -1, axis=2) - potential,
            ]
        local = jnp.stack(
            [jnp.sum(field * gradient_field[device_axis]) for device_axis in range(3)]
        )
        flux = lax.psum(local, "pencil") / volume
        return (carry, flux)

    ignored, slot_flux = lax.scan(solve_slot, jnp.float32(0.0), (slot_gradient, slot_heat))
    flux_all = lax.all_gather(slot_flux, "macro", axis=0, tiled=True)
    flux_row = assign_all * slots + rank
    mine = lax.dynamic_slice_in_dim(flux_row, macro_index * per_device, per_device)
    catalog = jnp.arange(flux_all.shape[0], dtype=jnp.int32)
    qp_flux = jnp.sum(
        jnp.where((mine[:, None] == catalog[None, :])[:, :, None], flux_all[None, :, :], 0.0),
        axis=1,
    )
    residual = jnp.dot(qp_flux, signs.T, precision=HIGHEST) / 4.0
    hits = rows[:, :, None] == node_ids
    local_rows = jnp.sum(jnp.where(hits, residual[:, :, None], 0.0), axis=(0, 1))
    nodal_flux = lax.psum_scatter(local_rows, "macro", scatter_dimension=0, tiled=True)
    return (qp_flux, nodal_flux)


def solution(mesh):
    in_specs = (
        P("macro", "pencil", None, None),
        P("macro", "pencil", None, None),
        P("macro", None),
        P("macro"),
        P("macro", None),
        P("macro"),
        P("macro"),
    )
    out_specs = (P("macro", None), P("macro"))
    return jax.shard_map(
        on_device, mesh=mesh, in_specs=in_specs, out_specs=out_specs, check_vma=False
    )
```

profile of v0, /device:TPU:0, one launch (start us, length us, event | category | flops | bytes accessed | tf_op | source)
XLA Modules:
  0.0 937.2 jit_solution(7280020410338958855)
XLA Ops:
  6.5 21.8 %all-reduce.8 = (s32[32]{0:T(128)S(1)}, s32[128]{0:T(128)S(1)}) all-reduce(s32[32]{0:T(128)S(1)} %dynamic-update-slice, s32[128]{0:T(128)S(1)} %dynamic-update-slice.5), channel_id=1, replica_groups=mesh['macro'=32,'pencil'=8] {'macro'}, use_global_device_ids=true, to_apply=%add | all-reduce | flops 160 | bytes 1280
  32.4 70.3 %all-reduce.1 = f32[128]{0:T(128)S(1)} all-reduce(f32[128]{0:T(128)S(1)} %dynamic-update-slice.1), channel_id=1, replica_groups=mesh['macro'=32,'pencil'=8] {'macro'}, use_global_device_ids=true, to_apply=%add.1 | all-reduce | flops 128 | bytes 1024
  106.4 4.4 fusion.330
  111.7 13.1 %all-reduce.10 = (f32[1]{0:T(128)}, f32[1]{0:T(128)}) all-reduce(f32[1]{0:T(128)} %bitcast.13, f32[1]{0:T(128)} %bitcast.12), channel_id=1, replica_groups=mesh['macro'=32,'pencil'=8] {'pencil'}, use_global_device_ids=true, to_apply=%region_8.9 | all-reduce | flops 2 | bytes 16 | tf_op jit(solution)/shard_map/psum | solution.py:110
  126.3 139.0 %all-reduce.9 = (f32[32]{0:T(128)S(1)}, f32[96]{0:T(128)S(1)}, f32[32,2]{1,0:T(8,128)S(1)}) all-reduce(f32[32]{0:T(128)S(1)} %dynamic-update-slice.2, f32[96]{0:T(128)S(1)} %dynamic-update-slice.3, f32[32,2]{1,0:T(8,128)S(1)} %reshape.330), channel_id=1, replica_groups=mesh['macro'=32,'pencil'=8] {'macro'}, use_global_device_ids=true, to_apply=%add.2 | all-reduce | flops 192 | bytes 1536
  265.8 556.8 %while.12 = (s32[]{:T(128)}, f32[2,3]{1,0:T(2,128)S(1)}, f32[2]{0:T(128)S(1)}, f32[16,128,128]{2,1,0:T(8,128)S(1)}, f32[2,3]{1,0:T(2,128)S(1)}, /*index=5*/f32[2...) while((s32[]{:T(128)}, f32[2,3]{1,0:T(2,128)S(1)}, ...), condition=%wide.region_14.15_spmd.clone.clone, body=%wide.region_9.14_spmd.clone.clone.sunk | while | flops 16144400384 | bytes 237046800 | solution.py:184
  274.0 4.4 collective-permute-done
  297.4 11.4 %all-to-all-done = f32[16,128,128]{2,0,1:T(8,128)} async-done(((f32[16,128,128]{2,0,1:T(8,128)}), f32[16,128,128]{2,0,1:T(8,128)}, u32[]{:S(2)}, u32[]{:S(2)}) %all-to-all-start) | async-done | bytes 1048608 | tf_op jit(solution)/shard_map/while/body/eval_jaxpr/all_to_all | solution.py:56
  317.0 11.8 %all-to-all-done.1 = f32[16,128,128]{2,0,1:T(8,128)S(1)} async-done(((f32[16,128,128]{2,0,1:T(8,128)}), f32[16,128,128]{2,0,1:T(8,128)S(1)}, u32[]{:S(2)}, u32[]{:S(2)}) %all-to-all-start.1) | async-done | bytes 1048608 | tf_op jit(solution)/shard_map/while/body/eval_jaxpr/all_to_all | solution.py:57
  343.0 4.2 all-to-all-start.2
  351.1 12.1 %all-to-all-done.2 = f32[128,16,128]{2,1,0:T(8,128)} async-done(((f32[128,16,128]{2,1,0:T(8,128)}), f32[128,16,128]{2,1,0:T(8,128)}, u32[]{:S(2)}, u32[]{:S(2)}) %all-to-all-start.2) | async-done | bytes 1048608 | tf_op jit(solution)/shard_map/while/body/eval_jaxpr/all_to_all | solution.py:70
  368.3 14.4 %all-to-all-done.3 = f32[128,16,128]{2,1,0:T(8,128)S(1)} async-done(((f32[128,16,128]{2,1,0:T(8,128)}), f32[128,16,128]{2,1,0:T(8,128)S(1)}, u32[]{:S(2)}, u32[]{:S(2)}) %all-to-all-start.3) | async-done | bytes 1048608 | tf_op jit(solution)/shard_map/while/body/eval_jaxpr/all_to_all | solution.py:71
  415.0 4.2 all-to-all-start.4
  423.9 11.4 %all-to-all-done.4 = f32[16,128,128]{2,0,1:T(8,128)} async-done(((f32[16,128,128]{2,0,1:T(8,128)}), f32[16,128,128]{2,0,1:T(8,128)}, u32[]{:S(2)}, u32[]{:S(2)}) %all-to-all-start.4) | async-done | bytes 1048608 | tf_op jit(solution)/shard_map/while/body/eval_jaxpr/all_to_all | solution.py:56
  443.1 11.8 %all-to-all-done.5 = f32[16,128,128]{2,0,1:T(8,128)S(1)} async-done(((f32[16,128,128]{2,0,1:T(8,128)}), f32[16,128,128]{2,0,1:T(8,128)S(1)}, u32[]{:S(2)}, u32[]{:S(2)}) %all-to-all-start.5) | async-done | bytes 1048608 | tf_op jit(solution)/shard_map/while/body/eval_jaxpr/all_to_all | solution.py:57
  469.1 4.2 all-to-all-start.6
  477.2 12.1 %all-to-all-done.6 = f32[128,16,128]{2,1,0:T(8,128)} async-done(((f32[128,16,128]{2,1,0:T(8,128)}), f32[128,16,128]{2,1,0:T(8,128)}, u32[]{:S(2)}, u32[]{:S(2)}) %all-to-all-start.6) | async-done | bytes 1048608 | tf_op jit(solution)/shard_map/while/body/eval_jaxpr/all_to_all | solution.py:70
  494.6 14.1 %all-to-all-done.7 = f32[128,16,128]{2,1,0:T(8,128)S(1)} async-done(((f32[128,16,128]{2,1,0:T(8,128)}), f32[128,16,128]{2,1,0:T(8,128)S(1)}, u32[]{:S(2)}, u32[]{:S(2)}) %all-to-all-start.7) | async-done | bytes 1048608 | tf_op jit(solution)/shard_map/while/body/eval_jaxpr/all_to_all | solution.py:71
  528.2 15.4 %psum.26 = f32[3]{0:T(128)S(1)} all-reduce(f32[3]{0:T(128)S(1)} %pad_maximum_fusion.2), channel_id=1, replica_groups=mesh['macro'=32,'pencil'=8] {'pencil'}, use_global_device_ids=true, to_apply=%region_13.13 | all-reduce | flops 3 | bytes 24 | tf_op jit(solution)/shard_map/while/body/eval_jaxpr/psum | solution.py:181
  551.8 4.4 collective-permute-done
  566.4 4.2 all-to-all-start
  575.2 11.4 %all-to-all-done = f32[16,128,128]{2,0,1:T(8,128)} async-done(((f32[16,128,128]{2,0,1:T(8,128)}), f32[16,128,128]{2,0,1:T(8,128)}, u32[]{:S(2)}, u32[]{:S(2)}) %all-to-all-start) | async-done | bytes 1048608 | tf_op jit(solution)/shard_map/while/body/eval_jaxpr/all_to_all | solution.py:56
  594.7 11.8 %all-to-all-done.1 = f32[16,128,128]{2,0,1:T(8,128)S(1)} async-done(((f32[16,128,128]{2,0,1:T(8,128)}), f32[16,128,128]{2,0,1:T(8,128)S(1)}, u32[]{:S(2)}, u32[]{:S(2)}) %all-to-all-start.1) | async-done | bytes 1048608 | tf_op jit(solution)/shard_map/while/body/eval_jaxpr/all_to_all | solution.py:57
  628.8 12.1 %all-to-all-done.2 = f32[128,16,128]{2,1,0:T(8,128)} async-done(((f32[128,16,128]{2,1,0:T(8,128)}), f32[128,16,128]{2,1,0:T(8,128)}, u32[]{:S(2)}, u32[]{:S(2)}) %all-to-all-start.2) | async-done | bytes 1048608 | tf_op jit(solution)/shard_map/while/body/eval_jaxpr/all_to_all | solution.py:70
  646.0 14.4 %all-to-all-done.3 = f32[128,16,128]{2,1,0:T(8,128)S(1)} async-done(((f32[128,16,128]{2,1,0:T(8,128)}), f32[128,16,128]{2,1,0:T(8,128)S(1)}, u32[]{:S(2)}, u32[]{:S(2)}) %all-to-all-start.3) | async-done | bytes 1048608 | tf_op jit(solution)/shard_map/while/body/eval_jaxpr/all_to_all | solution.py:71
  701.5 11.4 %all-to-all-done.4 = f32[16,128,128]{2,0,1:T(8,128)} async-done(((f32[16,128,128]{2,0,1:T(8,128)}), f32[16,128,128]{2,0,1:T(8,128)}, u32[]{:S(2)}, u32[]{:S(2)}) %all-to-all-start.4) | async-done | bytes 1048608 | tf_op jit(solution)/shard_map/while/body/eval_jaxpr/all_to_all | solution.py:56
  720.8 11.8 %all-to-all-done.5 = f32[16,128,128]{2,0,1:T(8,128)S(1)} async-done(((f32[16,128,128]{2,0,1:T(8,128)}), f32[16,128,128]{2,0,1:T(8,128)S(1)}, u32[]{:S(2)}, u32[]{:S(2)}) %all-to-all-start.5) | async-done | bytes 1048608 | tf_op jit(solution)/shard_map/while/body/eval_jaxpr/all_to_all | solution.py:57
  754.9 12.1 %all-to-all-done.6 = f32[128,16,128]{2,1,0:T(8,128)} async-done(((f32[128,16,128]{2,1,0:T(8,128)}), f32[128,16,128]{2,1,0:T(8,128)}, u32[]{:S(2)}, u32[]{:S(2)}) %all-to-all-start.6) | async-done | bytes 1048608 | tf_op jit(solution)/shard_map/while/body/eval_jaxpr/all_to_all | solution.py:70
  772.3 14.1 %all-to-all-done.7 = f32[128,16,128]{2,1,0:T(8,128)S(1)} async-done(((f32[128,16,128]{2,1,0:T(8,128)}), f32[128,16,128]{2,1,0:T(8,128)S(1)}, u32[]{:S(2)}, u32[]{:S(2)}) %all-to-all-start.7) | async-done | bytes 1048608 | tf_op jit(solution)/shard_map/while/body/eval_jaxpr/all_to_all | solution.py:71
  805.8 15.4 %psum.26 = f32[3]{0:T(128)S(1)} all-reduce(f32[3]{0:T(128)S(1)} %pad_maximum_fusion.2), channel_id=1, replica_groups=mesh['macro'=32,'pencil'=8] {'pencil'}, use_global_device_ids=true, to_apply=%region_13.13 | all-reduce | flops 3 | bytes 24 | tf_op jit(solution)/shard_map/while/body/eval_jaxpr/psum | solution.py:181
  822.5 39.6 %all-gather.2 = f32[32,2,3]{2,1,0:T(2,128)S(1)} all-gather(f32[1,2,3]{2,1,0:T(2,128)S(1)} %bitcast.528), channel_id=1, replica_groups=mesh['macro'=32,'pencil'=8] {'macro'}, dimensions={0}, use_global_device_ids=true | all-gather | bytes 792 | tf_op jit(solution)/shard_map/all_gather | solution.py:185
  864.0 72.3 %all-reduce.7 = f32[128]{0:T(128)S(1)} all-reduce(f32[128]{0:T(128)S(1)} %select_reduce_fusion.3), channel_id=4, replica_groups=mesh['macro'=32,'pencil'=8] {'macro'}, use_global_device_ids=true, to_apply=%region_18.19.clone | all-reduce | flops 128 | bytes 1024
  (280 shorter events, 308.0 us)
Async XLA Ops:
  273.5 4.9 collective-permute-start
  288.6 20.2 %all-to-all-start = ((f32[16,128,128]{2,0,1:T(8,128)}), f32[16,128,128]{2,0,1:T(8,128)}, u32[]{:S(2)}, u32[]{:S(2)}) async-start(f32[16,128,128]{2,0,1:T(8,128)} %copy.194), calls=%async_computation | async-start | bytes 2097152 | tf_op jit(solution)/shard_map/while/body/eval_jaxpr/all_to_all | solution.py:56
  308.8 20.0 %all-to-all-start.1 = ((f32[16,128,128]{2,0,1:T(8,128)}), f32[16,128,128]{2,0,1:T(8,128)S(1)}, u32[]{:S(2)}, u32[]{:S(2)}) async-start(f32[16,128,128]{2,0,1:T(8,128)} %copy.197), calls=%async_computation.1 | async-start | bytes 2097152 | tf_op jit(solution)/shard_map/while/body/eval_jaxpr/all_to_all | solution.py:57
  331.7 1.2 copy-start.2
  334.1 1.4 copy-start.3
  343.0 20.2 %all-to-all-start.2 = ((f32[128,16,128]{2,1,0:T(8,128)}), f32[128,16,128]{2,1,0:T(8,128)}, u32[]{:S(2)}, u32[]{:S(2)}) async-start(f32[128,16,128]{2,1,0:T(8,128)} %copy.200), calls=%async_computation.2 | async-start | bytes 2097152 | tf_op jit(solution)/shard_map/while/body/eval_jaxpr/all_to_all | solution.py:70
  363.2 19.4 %all-to-all-start.3 = ((f32[128,16,128]{2,1,0:T(8,128)}), f32[128,16,128]{2,1,0:T(8,128)S(1)}, u32[]{:S(2)}, u32[]{:S(2)}) async-start(f32[128,16,128]{2,1,0:T(8,128)} %copy.202), calls=%async_computation.3 | async-start | bytes 2097152 | tf_op jit(solution)/shard_map/while/body/eval_jaxpr/all_to_all | solution.py:71
  394.9 2.3 collective-permute-start.1
  400.0 5.0 collective-permute-start.2
  415.0 20.2 %all-to-all-start.4 = ((f32[16,128,128]{2,0,1:T(8,128)}), f32[16,128,128]{2,0,1:T(8,128)}, u32[]{:S(2)}, u32[]{:S(2)}) async-start(f32[16,128,128]{2,0,1:T(8,128)} %copy.204), calls=%async_computation.4 | async-start | bytes 2097152 | tf_op jit(solution)/shard_map/while/body/eval_jaxpr/all_to_all | solution.py:56
  435.3 19.6 %all-to-all-start.5 = ((f32[16,128,128]{2,0,1:T(8,128)}), f32[16,128,128]{2,0,1:T(8,128)S(1)}, u32[]{:S(2)}, u32[]{:S(2)}) async-start(f32[16,128,128]{2,0,1:T(8,128)} %copy.207), calls=%async_computation.5 | async-start | bytes 2097152 | tf_op jit(solution)/shard_map/while/body/eval_jaxpr/all_to_all | solution.py:57
  457.8 1.2 copy-start
  460.2 1.4 copy-start.1
  469.1 20.2 %all-to-all-start.6 = ((f32[128,16,128]{2,1,0:T(8,128)}), f32[128,16,128]{2,1,0:T(8,128)}, u32[]{:S(2)}, u32[]{:S(2)}) async-start(f32[128,16,128]{2,1,0:T(8,128)} %copy.210), calls=%async_computation.6 | async-start | bytes 2097152 | tf_op jit(solution)/shard_map/while/body/eval_jaxpr/all_to_all | solution.py:70
  489.3 19.4 %all-to-all-start.7 = ((f32[128,16,128]{2,1,0:T(8,128)}), f32[128,16,128]{2,1,0:T(8,128)S(1)}, u32[]{:S(2)}, u32[]{:S(2)}) async-start(f32[128,16,128]{2,1,0:T(8,128)} %copy.212), calls=%async_computation.7 | async-start | bytes 2097152 | tf_op jit(solution)/shard_map/while/body/eval_jaxpr/all_to_all | solution.py:71
  520.6 2.3 collective-permute-start.3
  551.3 4.9 collective-permute-start
  566.4 20.2 %all-to-all-start = ((f32[16,128,128]{2,0,1:T(8,128)}), f32[16,128,128]{2,0,1:T(8,128)}, u32[]{:S(2)}, u32[]{:S(2)}) async-start(f32[16,128,128]{2,0,1:T(8,128)} %copy.194), calls=%async_computation | async-start | bytes 2097152 | tf_op jit(solution)/shard_map/while/body/eval_jaxpr/all_to_all | solution.py:56
  586.6 19.8 %all-to-all-start.1 = ((f32[16,128,128]{2,0,1:T(8,128)}), f32[16,128,128]{2,0,1:T(8,128)S(1)}, u32[]{:S(2)}, u32[]{:S(2)}) async-start(f32[16,128,128]{2,0,1:T(8,128)} %copy.197), calls=%async_computation.1 | async-start | bytes 2097152 | tf_op jit(solution)/shard_map/while/body/eval_jaxpr/all_to_all | solution.py:57
  609.3 1.2 copy-start.2
  611.8 1.4 copy-start.3
  620.7 20.2 %all-to-all-start.2 = ((f32[128,16,128]{2,1,0:T(8,128)}), f32[128,16,128]{2,1,0:T(8,128)}, u32[]{:S(2)}, u32[]{:S(2)}) async-start(f32[128,16,128]{2,1,0:T(8,128)} %copy.200), calls=%async_computation.2 | async-start | bytes 2097152 | tf_op jit(solution)/shard_map/while/body/eval_jaxpr/all_to_all | solution.py:70
  640.9 19.4 %all-to-all-start.3 = ((f32[128,16,128]{2,1,0:T(8,128)}), f32[128,16,128]{2,1,0:T(8,128)S(1)}, u32[]{:S(2)}, u32[]{:S(2)}) async-start(f32[128,16,128]{2,1,0:T(8,128)} %copy.202), calls=%async_computation.3 | async-start | bytes 2097152 | tf_op jit(solution)/shard_map/while/body/eval_jaxpr/all_to_all | solution.py:71
  672.5 2.3 collective-permute-start.1
  677.6 5.0 collective-permute-start.2
  692.7 20.2 %all-to-all-start.4 = ((f32[16,128,128]{2,0,1:T(8,128)}), f32[16,128,128]{2,0,1:T(8,128)}, u32[]{:S(2)}, u32[]{:S(2)}) async-start(f32[16,128,128]{2,0,1:T(8,128)} %copy.204), calls=%async_computation.4 | async-start | bytes 2097152 | tf_op jit(solution)/shard_map/while/body/eval_jaxpr/all_to_all | solution.py:56
  712.9 19.6 %all-to-all-start.5 = ((f32[16,128,128]{2,0,1:T(8,128)}), f32[16,128,128]{2,0,1:T(8,128)S(1)}, u32[]{:S(2)}, u32[]{:S(2)}) async-start(f32[16,128,128]{2,0,1:T(8,128)} %copy.207), calls=%async_computation.5 | async-start | bytes 2097152 | tf_op jit(solution)/shard_map/while/body/eval_jaxpr/all_to_all | solution.py:57
  735.4 1.2 copy-start
  737.9 1.4 copy-start.1
  746.8 20.2 %all-to-all-start.6 = ((f32[128,16,128]{2,1,0:T(8,128)}), f32[128,16,128]{2,1,0:T(8,128)}, u32[]{:S(2)}, u32[]{:S(2)}) async-start(f32[128,16,128]{2,1,0:T(8,128)} %copy.210), calls=%async_computation.6 | async-start | bytes 2097152 | tf_op jit(solution)/shard_map/while/body/eval_jaxpr/all_to_all | solution.py:70
  767.0 19.4 %all-to-all-start.7 = ((f32[128,16,128]{2,1,0:T(8,128)}), f32[128,16,128]{2,1,0:T(8,128)S(1)}, u32[]{:S(2)}, u32[]{:S(2)}) async-start(f32[128,16,128]{2,1,0:T(8,128)} %copy.212), calls=%async_computation.7 | async-start | bytes 2097152 | tf_op jit(solution)/shard_map/while/body/eval_jaxpr/all_to_all | solution.py:71
  798.2 2.3 collective-permute-start.3
  (10 other events, 6.4 us)
where the time goes:
time: 943 us; the launch traced here: 937 us
  blocking collectives  387 us (41%)
  waiting for transfers between devices  219 us (23%)
  matrix products  131 us (14%)
  local copies, waits for them, and re-layouts  83.2 us (9%)
  starting transfers between devices  68.6 us (7%)
  other arithmetic  33.8 us (4%)
  loops' own time  9.49 us (1%)
    unnamed x4, blocking collectives  303 us
    all_to_all x4, waiting for transfers between devices, inverse_field(): lax.all_to_all(imag_part, 'pencil', split_axis=0, concat_axis=1, tiled=True)  57 us
    all_to_all x4, waiting for transfers between devices, inverse_field(): lax.all_to_all(real_part, 'pencil', split_axis=0, concat_axis=1, tiled=True)  48.5 us
    all_to_all x4, waiting for transfers between devices, forward_spectrum(): lax.all_to_all(imag_part, 'pencil', split_axis=1, concat_axis=0, tiled=True)  47.1 us
    all_to_all x4, waiting for transfers between devices, forward_spectrum(): lax.all_to_all(real_part, 'pencil', split_axis=1, concat_axis=0, tiled=True)  45.6 us
    all_gather x1, blocking collectives, on_device(): flux_all = lax.all_gather(slot_flux, 'macro', axis=0, tiled=True)  39.6 us
    dot_general x16, matrix products, complex_transform_pass(): imag_sin = jnp.einsum(form, imag_part, sine, precision=HIGHEST)  34 us
    psum x2, blocking collectives, solve_slot(): flux = lax.psum(local, 'pencil') / volume  30.8 us
  transfers between devices with their start and end apart: 24, of which 24 were waited for; matrix products, arithmetic and copies ran while one was open for 6% of the time, Pallas kernels for 0%

commit v1 on v0

v1 whole, which is shorter than its diff:
```python
import math

import jax
import jax.numpy as jnp
import numpy as np
from jax import lax
from jax.sharding import PartitionSpec as P

PHASES = 3

HIGHEST = lax.Precision.HIGHEST


def mode_tables(width, slab):
    half = width // 2
    mode = np.arange(width)
    number = np.where(mode <= half, mode, mode - half)
    angle = 2.0 * np.pi * (number[:, None] * np.arange(width)[None, :] % width) / width
    basis = np.where((mode <= half)[:, None], np.cos(angle), np.sin(angle)) * math.sqrt(2.0 / width)
    basis[0] /= math.sqrt(2.0)
    basis[half] /= math.sqrt(2.0)
    line = 4.0 * np.sin(np.pi * number / width) ** 2
    plane = line[:, None] + line[None, :]
    rho = 1.0 + plane / 2.0 - np.sqrt(plane + plane * plane / 4.0)
    zero = plane == 0.0
    norm = np.where(zero, 0.0, 1.0 / np.where(zero, 1.0, 1.0 / rho - rho))
    step = rho**slab
    loop = rho**width
    keep = np.where(zero, 0.0, 1.0 - loop)
    scale = np.where(zero, 1.0, 1.0 / np.where(zero, 1.0, 1.0 - loop))
    f32 = lambda table: table.astype(np.float32)
    return f32(basis), f32(rho), f32(norm), f32(step), f32(keep), f32(scale)


def corner_signs():
    table = [
        [2.0 * (corner >> device_axis & 1) - 1.0 for device_axis in range(3)] for corner in range(8)
    ]
    return jnp.array(table, dtype=jnp.float32)


def base_field(voxel_material_ids, fiber_fraction, phase_lookup_table):
    conduct = jnp.zeros(fiber_fraction.shape, jnp.float32)
    for phase in range(PHASES):
        conduct = conduct + jnp.where(voxel_material_ids == phase, phase_lookup_table[phase], 0.0)
    return conduct * fiber_fraction


def spread_tails(tails, step, keep, scale):
    slabs = tails.shape[0]
    right = tails[0, 0]
    left = tails[slabs - 1, 1]
    for i in range(1, slabs):
        right = tails[i, 0] + step * right
        left = tails[slabs - 1 - i, 1] + step * left
    rights, lefts = [right], [left]
    for j in range(slabs - 1):
        rights.append(keep * tails[j, 0] + step * rights[-1])
        lefts.append(keep * tails[slabs - 1 - j, 1] + step * lefts[-1])
    return jnp.stack([jnp.stack([r, l]) for r, l in zip(rights, lefts[::-1])]) * scale


def on_device(
    voxel_material_ids,
    fiber_fraction,
    material_matrix_diffusivity,
    mesh_point_thermal_state,
    element_corner_ids,
    global_entry_position,
    sample_choice_per_point,
):
    macro_index = lax.axis_index("macro")
    pencil_index = lax.axis_index("pencil")
    slab = fiber_fraction.shape[1]
    width = fiber_fraction.shape[3]
    volume = float(width**3)
    slabs = width // slab
    per_device = element_corner_ids.shape[0]
    own_nodes = mesh_point_thermal_state.shape[0]
    basis, rho, norm, step, keep, scale = mode_tables(width, slab)

    packed = jnp.concatenate(
        [
            mesh_point_thermal_state,
            global_entry_position.astype(jnp.float32),
            sample_choice_per_point.astype(jnp.float32),
            element_corner_ids.reshape(-1).astype(jnp.float32),
        ]
    )
    gathered = lax.all_gather(packed, "macro", axis=0, tiled=False)

    conduct = base_field(voxel_material_ids[0], fiber_fraction[0], material_matrix_diffusivity[0])
    total = jnp.sum(conduct)
    total_square = jnp.sum(conduct * conduct)
    modes = jnp.einsum("xyz,bz->xyb", conduct, basis, precision=HIGHEST)
    modes = jnp.einsum("ay,xyb->xab", basis, modes, precision=HIGHEST) * norm
    right = modes[0]
    left = modes[slab - 1]
    for i in range(1, slab):
        right = modes[i] + rho * right
        left = modes[slab - 1 - i] + rho * left
    corner = (jnp.arange(width)[:, None] == 0) & (jnp.arange(width)[None, :] == 0)
    right = jnp.where(corner, total, right)
    left = jnp.where(corner, total_square, left)
    tails = lax.all_to_all(jnp.stack([right, left]), "pencil", 1, 0, tiled=True)
    rows = lambda table: lax.dynamic_slice_in_dim(jnp.asarray(table), pencil_index * slab, slab)
    tails = spread_tails(
        tails.reshape(slabs, 2, slab, width), rows(step), rows(keep), rows(scale)
    )
    tails = lax.all_to_all(tails.reshape(2 * slabs, slab, width), "pencil", 0, 1, tiled=True)
    mean = tails[0, 0, 0] / volume
    mean_square = tails[1, 0, 0] / volume
    before = jnp.where(corner, 0.0, tails[0])
    after = jnp.where(corner, 0.0, tails[1])
    ahead = [before]
    for i in range(slab):
        ahead.append(modes[i] + rho * ahead[-1])
    ahead.append(rho * ahead[-1])
    behind = [after, rho * after]
    for i in range(slab - 1, -1, -1):
        behind.append(rho * (modes[i] + behind[-1]))
    behind = behind[::-1]
    potential = jnp.stack([p + q for p, q in zip(ahead, behind)])
    rise = potential[1:-1] - potential[:-2]
    potential = potential[1:]
    shifted = jnp.asarray(basis.astype(np.float64) - np.roll(basis.astype(np.float64), 1, axis=1), jnp.float32)
    synth = lambda field, y, z: jnp.einsum(
        "ay,xaz->xyz", y, jnp.einsum("xab,bz->xaz", field, z, precision=HIGHEST), precision=HIGHEST
    )
    psi_x = synth(rise, basis, basis)
    psi_y = synth(potential, shifted, basis)
    psi_z = synth(potential, basis, shifted)
    next_y = lambda f: jnp.roll(f, -1, axis=1) - f
    next_z = lambda f: jnp.roll(f, -1, axis=2) - f
    here_y, here_z = psi_y[:-1], psi_z[:-1]
    e_xy, e_yy, e_zy = psi_y[1:] - here_y, next_y(here_y), next_z(here_y)
    e_xz, e_yz, e_zz = psi_z[1:] - here_z, next_y(here_z), next_z(here_z)
    e_yx, e_zx = next_y(psi_x), next_z(psi_x)
    e_xx = mean - conduct - e_yy - e_zz
    e = [[e_xx, e_yx, e_zx], [e_xy, e_yy, e_zy], [e_xz, e_yz, e_zz]]
    plain = [[None] * 3 for _ in range(3)]
    weighted = [[None] * 3 for _ in range(3)]
    for i in range(3):
        for j in range(i, 3):
            product = e[i][0] * e[j][0] + e[i][1] * e[j][1] + e[i][2] * e[j][2]
            plain[i][j] = plain[j][i] = jnp.sum(product) / volume
            weighted[i][j] = weighted[j][i] = jnp.sum(conduct * product) / volume
    plain = jnp.stack([jnp.stack(r) for r in plain])
    weighted = jnp.stack([jnp.stack(r) for r in weighted])

    points = gathered.shape[0]
    temperature = gathered[:, :own_nodes].reshape(-1)
    entry = gathered[:, own_nodes : 2 * own_nodes].reshape(-1)
    assign = gathered[:, 2 * own_nodes]
    corners = gathered[:, 2 * own_nodes + 1 :].reshape(points, 8)
    node_ids = jnp.arange(temperature.shape[0]).astype(jnp.float32)
    picks = corners[:, :, None] == node_ids
    theta = jnp.sum(jnp.where(picks, temperature, 0.0), axis=2)
    rows_of = jnp.sum(jnp.where(picks, entry, 0.0), axis=2)
    signs = corner_signs()
    gradient = jnp.dot(theta, signs, precision=HIGHEST) / 4.0
    heat = jnp.sum(theta, axis=1) / 8.0
    radiative = heat**3
    reference_k = jnp.sqrt(mean_square + 2.0 * radiative * mean + radiative * radiative)
    inverse_k = 1.0 / reference_k
    first = jnp.sum(plain[None] * gradient[:, None, :], axis=2)
    second = jnp.sum(weighted[None] * gradient[:, None, :], axis=2)
    flux = (
        second * (inverse_k * inverse_k)[:, None]
        - first * (inverse_k * (2.0 - radiative * inverse_k))[:, None]
    )
    share = gradient * (mean + radiative)[:, None] / float(slabs)
    here = assign == macro_index.astype(jnp.float32)
    flux = jnp.where(here[:, None], flux + share, 0.0)
    residual = jnp.dot(flux, signs.T, precision=HIGHEST) / 4.0
    nodal = jnp.sum(jnp.where(rows_of[:, :, None] == node_ids, residual[:, :, None], 0.0), axis=(0, 1))
    parts = jnp.concatenate([flux, nodal.reshape(points, own_nodes)], axis=1)
    parts = lax.psum(parts, ("macro", "pencil"))
    mine = lax.dynamic_slice_in_dim(parts, macro_index * per_device, per_device)
    return (mine[:, :3], mine[0, 3:])


def solution(mesh):
    in_specs = (
        P("macro", "pencil", None, None),
        P("macro", "pencil", None, None),
        P("macro", None),
        P("macro"),
        P("macro", None),
        P("macro"),
        P("macro"),
    )
    out_specs = (P("macro", None), P("macro"))
    return jax.shard_map(
        on_device, mesh=mesh, in_specs=in_specs, out_specs=out_specs, check_vma=False
    )
```

time: 943 us -> 227 us (0.24)
  the two profiles are of different devices: /device:TPU:0 before, /device:TPU:1 now
where the time goes in v1:
time: 227 us; the launch traced here: 226 us
  blocking collectives  135 us (59%)
  other arithmetic  31.1 us (14%)
  starting transfers between devices  25.5 us (11%)
  between operations  12.1 us (5%)
  matrix products  8.82 us (4%)
  local copies, waits for them, and re-layouts  8.4 us (4%)
  waiting for transfers between devices  4.78 us (2%)
    psum x1, blocking collectives, on_device(): parts = lax.psum(parts, ('macro', 'pencil'))  72.3 us
    unnamed x1, blocking collectives  63.1 us
    all_to_all x1, starting transfers between devices, on_device(): lax.all_to_all(tails.reshape(2 * slabs, slab, width), 'pencil', 0, 1, til...  18.9 us
    unnamed x31, other arithmetic  14 us
    all_to_all x1, starting transfers between devices, on_device(): tails = lax.all_to_all(jnp.stack([right, left]), 'pencil', 1, 0, tiled=True)  6.51 us
    all_to_all x1, waiting for transfers between devices, on_device(): lax.all_to_all(tails.reshape(2 * slabs, slab, width), 'pencil', 0, 1, til...  4.78 us
  transfers between devices with their start and end apart: 2, of which 1 were waited for; matrix products, arithmetic and copies ran while one was open for 1% of the time, Pallas kernels for 0%

profile of v1, /device:TPU:1, one launch (start us, length us, event | category | flops | bytes accessed | tf_op | source)
XLA Modules:
  0.0 226.0 jit_solution(16712668191866784900)
XLA Ops:
  0.7 1.6 copy.145
  3.3 3.0 %fusion.92 = (f32[]{:T(128)}, f32[1,16,128,128]{2,3,1,0:T(8,128)S(1)}) fusion(f32[1,16,128,128]{2,3,1,0:T(8,128)S(1)} %copy.145, f32[]{:T(128)} %bitcast.4, s32[1,16,128,128]{2,3,1,0:T(8,128)S(1)} %copy.142, f32[]{:T(128)} %bitcast.3, f32[]{:T(128)} %bitcast.2), kind=kLoop, calls=%fused_computation.310 | loop fusion | flops 2621439 | bytes 3145744 | tf_op jit(solution)/shard_map/reduce_sum | solution.py:93
  7.2 1.1 fusion.4
  8.3 1.0 fusion.1
  11.8 6.5 %all-to-all-start = ((f32[2,128,128]{2,0,1:T(2,128)}), f32[2,128,128]{2,0,1:T(2,128)S(1)}, u32[]{:S(2)}, u32[]{:S(2)}) async-start(f32[2,128,128]{2,0,1:T(2,128)} %copy.148), calls=%async_computation | async-start | bytes 262144 | tf_op jit(solution)/shard_map/all_to_all | solution.py:105
  20.5 63.1 %all-reduce = f32[544]{0:T(1024)S(1)} all-reduce(f32[544]{0:T(1024)S(1)} %maximum_dynamic-update-slice_fusion), channel_id=2, replica_groups=mesh['macro'=32,'pencil'=8] {'macro'}, use_global_device_ids=true, to_apply=%add | all-reduce | flops 544 | bytes 4352
  86.1 18.9 %all-to-all-start.1 = ((f32[16,16,128]{2,1,0:T(8,128)}), f32[16,16,128]{2,1,0:T(8,128)S(1)}, u32[]{:S(2)}, u32[]{:S(2)}) async-start(f32[16,16,128]{2,1,0:T(8,128)} %bitcast_multiply_fusion.7), calls=%async_computation.1 | async-start | bytes 262144 | tf_op jit(solution)/shard_map/all_to_all | solution.py:110
  105.5 4.8 %all-to-all-done.1 = f32[16,16,128]{2,1,0:T(8,128)S(1)} async-done(((f32[16,16,128]{2,1,0:T(8,128)}), f32[16,16,128]{2,1,0:T(8,128)S(1)}, u32[]{:S(2)}, u32[]{:S(2)}) %all-to-all-start.1) | async-done | bytes 131104 | tf_op jit(solution)/shard_map/all_to_all | solution.py:110
  111.6 0.9 constant_dynamic-update-slice_fusion.22
  112.5 0.9 constant_dynamic-update-slice_fusion.21
  113.4 0.9 constant_dynamic-update-slice_fusion.20
  115.2 0.9 constant_dynamic-update-slice_fusion.18
  116.1 0.9 constant_dynamic-update-slice_fusion.17
  117.0 0.9 constant_dynamic-update-slice_fusion.16
  117.9 0.9 constant_dynamic-update-slice_fusion.15
  118.8 0.9 constant_dynamic-update-slice_fusion.14
  120.6 0.9 constant_dynamic-update-slice_fusion.12
  121.5 0.9 constant_dynamic-update-slice_fusion.11
  122.4 0.9 constant_dynamic-update-slice_fusion.10
  123.3 1.0 constant_dynamic-update-slice_fusion.9
  124.5 0.9 constant_dynamic-update-slice_fusion.41
  125.5 1.1 fusion.99
  126.6 1.0 convolution_bitcast_fusion
  128.1 1.1 fusion.98
  129.2 1.0 convolution_bitcast_fusion.1
  131.0 1.1 fusion.15
  132.1 1.0 convolution_bitcast_fusion.2
  134.7 1.5 multiply_add_fusion.1
  136.3 1.2 multiply_add_fusion.3
  137.5 4.0 %fusion.10 = (f32[]{:T(128)}, f32[]{:T(128)}, f32[]{:T(128)}, f32[]{:T(128)}, f32[]{:T(128)}, /*index=5*/f32[]{:T(128)}, f32[]{:T(128)}, f32[]{:T(128)}, f32[]{:T(128)}, f32[]{:T(128)}, /*index=10*/f32[]{:T(128)}, f32[]{:T(128)}) fusion(f32[1,16,128,128]{2,3,1,0:T(8,128)S(1)} %get-tuple-element.92, f32[16,128,128]{1,2,0:T(8,128)S(1)} %get-tuple-element.40, ...), kind=kLoop, calls=%fused_computation.31 | loop fusion | flops 9961460 | bytes 12582960 | tf_op jit(solution)/shard_map/reduce_sum | solution.py:147
  151.1 1.2 fusion.97
  152.4 72.3 %psum.7 = f32[32,7]{0,1:T(8,128)S(1)} all-reduce(f32[32,7]{0,1:T(8,128)S(1)} %pad_maximum_fusion.1), channel_id=1, replica_groups=mesh['macro'=32,'pencil'=8] {'macro','pencil'}, use_global_device_ids=true, to_apply=%region_20.21 | all-reduce | flops 224 | bytes 1792 | tf_op jit(solution)/shard_map/psum | solution.py:178
  (121 shorter events, 15.5 us)
Async XLA Ops:
  0.6 1.7 copy-start.9
  0.6 2.4 %copy-start.3 = (s32[1,16,128,128]{3,2,1,0:T(8,128)S(1)}, s32[1,16,128,128]{3,2,1,0:T(8,128)}, u32[]{:S(2)}) copy-start(s32[1,16,128,128]{3,2,1,0:T(8,128)} %param.20) | copy-start | bytes 3145732
  3.3 3.9 %copy-start.2 = (f32[128,128,1]{1,0,2:T(8,128)S(1)}, f32[128,128,1]{1,0,2:T(8,128)}, u32[]{:S(2)}) copy-start(f32[128,128,1]{1,0,2:T(8,128)} %constant.98) | copy-start | bytes 196612
  7.2 1.1 copy-start.5
  8.3 1.0 copy-start.1
  9.3 101.2 %copy-start = (f32[16,128,128]{1,2,0:T(8,128)}, f32[16,128,128]{1,2,0:T(8,128)S(1)}, u32[]{:S(2)}) copy-start(f32[16,128,128]{1,2,0:T(8,128)S(1)} %fusion.1) | copy-start | bytes 3145732
  10.1 8.2 %copy-start.11 = (s32[1,8]{1,0:T(1,128)S(1)}, s32[1,8]{1,0:T(1,128)}, u32[]{:S(2)}) copy-start(s32[1,8]{1,0:T(1,128)} %param.24) | copy-start | bytes 100
  10.1 8.9 %copy-start.12 = (s32[4]{0:T(128)S(1)}, s32[4]{0:T(128)}, u32[]{:S(2)}) copy-start(s32[4]{0:T(128)} %param.25) | copy-start | bytes 52
  10.1 8.9 %copy-start.13 = (u32[256]{0:T(256)S(1)}, u32[256]{0:T(256)}, u32[]{:S(2)}) copy-start(u32[256]{0:T(256)} %constant.94) | copy-start | bytes 3076
  10.2 10.1 %copy-start.10 = (f32[4]{0:T(128)S(1)}, f32[4]{0:T(128)}, u32[]{:S(2)}) copy-start(f32[4]{0:T(128)} %param.23) | copy-start | bytes 52
  10.2 74.3 %copy-start.6 = (f32[128,128]{1,0:T(8,128)S(1)}, f32[128,128]{1,0:T(8,128)}, u32[]{:S(2)}) copy-start(f32[128,128]{1,0:T(8,128)} %constant.80.clone) | copy-start | bytes 196612
  10.2 74.3 %copy-start.7 = (f32[128,128]{1,0:T(8,128)S(1)}, f32[128,128]{1,0:T(8,128)}, u32[]{:S(2)}) copy-start(f32[128,128]{1,0:T(8,128)} %constant.81.clone) | copy-start | bytes 196612
  11.0 94.0 %copy-start.8 = (f32[8,3]{1,0:T(8,128)S(1)}, f32[8,3]{1,0:T(8,128)}, u32[]{:S(2)}) copy-start(f32[8,3]{1,0:T(8,128)} %constant.84.clone) | copy-start | bytes 292
  11.8 72.6 %all-to-all-start = ((f32[2,128,128]{2,0,1:T(2,128)}), f32[2,128,128]{2,0,1:T(2,128)S(1)}, u32[]{:S(2)}, u32[]{:S(2)}) async-start(f32[2,128,128]{2,0,1:T(2,128)} %copy.148), calls=%async_computation | async-start | bytes 262144 | tf_op jit(solution)/shard_map/all_to_all | solution.py:105
  86.1 24.2 %all-to-all-start.1 = ((f32[16,16,128]{2,1,0:T(8,128)}), f32[16,16,128]{2,1,0:T(8,128)S(1)}, u32[]{:S(2)}, u32[]{:S(2)}) async-start(f32[16,16,128]{2,1,0:T(8,128)} %bitcast_multiply_fusion.7), calls=%async_computation.1 | async-start | bytes 262144 | tf_op jit(solution)/shard_map/all_to_all | solution.py:110
  124.4 1.1 copy-start.4

commit v2 on v1

v2 whole, which is shorter than its diff:
```python
import math

import jax
import jax.numpy as jnp
import ml_dtypes
import numpy as np
from jax import lax
from jax.experimental import pallas as pl
from jax.experimental.pallas import tpu as pltpu
from jax.sharding import PartitionSpec as P

PHASES = 3
LANES = 128
ROWS = 8
VMEM_BYTES = 48 * 1024 * 1024

HIGHEST = lax.Precision.HIGHEST


def split_table(table):
    high = table.astype(ml_dtypes.bfloat16)
    low = (table - high.astype(np.float64)).astype(ml_dtypes.bfloat16)
    return high, low


def from_right(table):
    high, low = split_table(table)
    return np.block([[high, low], [high, low]])


def from_left(table):
    high, low = split_table(table)
    return np.block([[high, high], [low, low]])


def mode_tables(width, slab):
    half = width // 2
    mode = np.arange(width)
    number = np.where(mode <= half, mode, mode - half)
    angle = 2.0 * np.pi * (number[:, None] * np.arange(width)[None, :] % width) / width
    basis = np.where((mode <= half)[:, None], np.cos(angle), np.sin(angle)) * math.sqrt(2.0 / width)
    basis[0] /= math.sqrt(2.0)
    basis[half] /= math.sqrt(2.0)
    slope = basis - np.roll(basis, 1, axis=1)
    slope[0] = 0.0
    line = 4.0 * np.sin(np.pi * number / width) ** 2
    plane = line[:, None] + line[None, :]
    rho = 1.0 + plane / 2.0 - np.sqrt(plane + plane * plane / 4.0)
    zero = plane == 0.0
    norm = np.where(zero, 0.0, 1.0 / np.where(zero, 1.0, 1.0 / rho - rho))
    scale = np.where(zero, 1.0, 1.0 / np.where(zero, 1.0, 1.0 - rho**width))
    f32 = lambda table: table.astype(np.float32)
    return dict(
        basis=basis,
        slope=slope,
        rho=f32(rho),
        norm=f32(norm),
        step=f32(rho**slab),
        chip_step=f32(rho ** (2 * slab)),
        scale=f32(scale),
    )


def halves(data):
    high = data.astype(jnp.bfloat16)
    low = (data - high.astype(jnp.float32)).astype(jnp.bfloat16)
    return high, low


def beside(data):
    return jnp.concatenate(halves(data), axis=1)


def stacked(data):
    return jnp.concatenate(halves(data), axis=0)


def product(left, right):
    return jnp.dot(left, right, preferred_element_type=jnp.float32)


def corner_mask(shape):
    row = lax.broadcasted_iota(jnp.int32, shape, 0)
    lane = lax.broadcasted_iota(jnp.int32, shape, 1)
    return (row == 0) & (lane == 0)


def analyse_kernel(
    material_ref, ids_ref, fiber_ref, right_ref, left_ref, norm_ref, rho_ref,
    conduct_ref, modes_ref, keep_ref, give_ref, sums_ref,
):
    slab, width = fiber_ref.shape[1], fiber_ref.shape[3]
    odd = lax.rem(lax.axis_index("pencil"), 2) == 1
    sums_ref[...] = jnp.zeros_like(sums_ref)

    def pair(step, carry):
        planes = []
        for part in range(2):
            x = 2 * step + part
            ids = ids_ref[0, x]
            conduct = jnp.zeros((width, width), jnp.float32)
            for phase in range(PHASES):
                conduct = jnp.where(ids == phase, material_ref[0, phase], conduct)
            conduct = conduct * fiber_ref[0, x]
            conduct_ref[x] = conduct
            tiles = conduct.reshape(width // ROWS, ROWS, width)
            sums_ref[0] += jnp.sum(tiles, axis=0)
            sums_ref[1] += jnp.sum(tiles * tiles, axis=0)
            planes.append(beside(conduct))
        lines = product(jnp.concatenate(planes, axis=0), right_ref[...])
        lines = lines[:, :width] + lines[:, width:]
        lines = jnp.concatenate([lines[:width], lines[width:]], axis=1)
        modes = product(left_ref[...], stacked(lines))
        modes = modes[:width] + modes[width:]
        norm = norm_ref[...]
        modes_ref[2 * step] = modes[:, :width] * norm
        modes_ref[2 * step + 1] = modes[:, width:] * norm
        return carry

    lax.fori_loop(0, slab // 2, pair, 0)
    total = jnp.sum(sums_ref[0])
    total_square = jnp.sum(sums_ref[1])

    def chunk(index, carry):
        at = pl.ds(pl.multiple_of(index * ROWS, ROWS), ROWS)
        rho = rho_ref[at]
        right = modes_ref[0, at]
        left = modes_ref[slab - 1, at]
        for x in range(1, slab):
            right = modes_ref[x, at] + rho * right
            left = modes_ref[slab - 1 - x, at] + rho * left
        corner = corner_mask(right.shape) & (index == 0)
        right = jnp.where(corner, total, right)
        left = jnp.where(corner, total_square, left)
        keep_ref[at] = jnp.where(odd, left, right)
        give_ref[at] = jnp.where(odd, right, left)
        return carry

    lax.fori_loop(0, width // ROWS, chunk, 0)


def moments_kernel(
    conduct_ref, modes_ref, own_ref, other_ref, extra_ref, rho_ref,
    right_basis_ref, right_slope_ref, left_basis_ref, left_slope_ref,
    out_ref, potential_ref, rise_ref, px_ref, py_ref, pz_ref,
):
    slab, width = conduct_ref.shape[0], conduct_ref.shape[2]
    volume = float(width**3)
    pencil = lax.axis_index("pencil")
    odd = lax.rem(pencil, 2) == 1

    def sweep(index, carry):
        at = pl.ds(pl.multiple_of(index * ROWS, ROWS), ROWS)
        rho = rho_ref[at]
        corner = corner_mask(rho.shape) & (index == 0)
        own, other = own_ref[at], other_ref[at]
        before = jnp.where(corner, 0.0, jnp.where(odd, other, own))
        after = jnp.where(corner, 0.0, jnp.where(odd, own, other))
        behind = [after, rho * after]
        for x in range(slab - 1, -1, -1):
            behind.append(rho * (modes_ref[x, at] + behind[-1]))
        behind = behind[::-1]
        ahead = before
        last = ahead + behind[0]
        for x in range(slab + 1):
            ahead = rho * ahead
            if x < slab:
                ahead = ahead + modes_ref[x, at]
            here = ahead + behind[x + 1]
            potential_ref[x, at] = here
            rise_ref[x, at] = here - last
            last = here
        return carry

    lax.fori_loop(0, width // ROWS, sweep, 0)

    def put(ref, x, plane):
        ref[x, :width] = plane
        ref[x, width:] = plane[:ROWS]

    def synthesise(x):
        along = beside(potential_ref[x])
        rise = product(beside(rise_ref[x]), right_basis_ref[...])
        slope = product(along, right_slope_ref[...])
        plain = product(along, right_basis_ref[...])
        rise = rise[:, :width] + rise[:, width:]
        slope = slope[:, :width] + slope[:, width:]
        plain = plain[:, :width] + plain[:, width:]
        both = product(left_basis_ref[...], stacked(jnp.concatenate([slope, rise], axis=1)))
        both = both[:width] + both[width:]
        third = product(left_slope_ref[...], stacked(plain))
        third = third[:width] + third[width:]
        put(pz_ref, x, both[:, :width])
        put(px_ref, x, both[:, width:])
        put(py_ref, x, third)

    corner = corner_mask((ROWS, width))
    own = jnp.sum(jnp.where(corner, own_ref[:ROWS], 0.0))
    other = jnp.sum(jnp.where(corner, other_ref[:ROWS], 0.0))
    first = jnp.where(odd, other, own)
    second = jnp.where(odd, own, other)
    mean = first / volume

    def plane(step, totals):
        x = jnp.maximum(step - 2, 0)
        totals = list(totals)
        for chunk in range(width // ROWS):
            at = pl.ds(chunk * ROWS, ROWS)
            down = pl.ds(chunk * ROWS + 1, ROWS)
            conduct = conduct_ref[x, at]
            px, py, pz = px_ref[x, at], py_ref[x, at], pz_ref[x, at]
            turn = lambda field: pltpu.roll(field, width - 1, 1) - field
            e_yx, e_zx = px_ref[x, down] - px, turn(px)
            e_xy, e_yy, e_zy = py_ref[x + 1, at] - py, py_ref[x, down] - py, turn(py)
            e_xz, e_yz, e_zz = pz_ref[x + 1, at] - pz, pz_ref[x, down] - pz, turn(pz)
            e_xx = (mean - conduct) - (e_yy + e_zz)
            e = ((e_xx, e_yx, e_zx), (e_xy, e_yy, e_zy), (e_xz, e_yz, e_zz))
            at_entry = 0
            for i in range(3):
                for j in range(i, 3):
                    term = e[i][0] * e[j][0] + e[i][1] * e[j][1] + e[i][2] * e[j][2]
                    totals[at_entry] = totals[at_entry] + term
                    totals[6 + at_entry] = totals[6 + at_entry] + conduct * term
                    at_entry += 1
        synthesise(jnp.minimum(step, slab))
        return tuple(jnp.where(step < 2, 0.0, total) for total in totals)

    nothing = jnp.zeros((ROWS, width), jnp.float32)
    totals = lax.fori_loop(0, slab + 2, plane, (nothing,) * 12)
    lines = [jnp.sum(total, axis=0, keepdims=True) for total in totals]
    lines = jnp.concatenate(lines + [jnp.zeros((4, width), jnp.float32)], axis=0)
    column = jnp.sum(lines, axis=1, keepdims=True)
    row = lax.broadcasted_iota(jnp.int32, (16, width), 0)
    lane = lax.broadcasted_iota(jnp.int32, (16, width), 1)
    once = jnp.where(pencil == 0, 1.0, 0.0)
    column = jnp.where(row == 12, first * once, jnp.where(row == 13, second * once, column))
    out_ref[...] = jnp.sum(jnp.where(row == lane, column, 0.0), axis=0, keepdims=True) + extra_ref[...] * once


def close_kernel(nodes_own, volume, table_ref, flux_ref, nodal_ref):
    points = table_ref.shape[0]
    macro = lax.axis_index("macro")
    table = table_ref[...]
    lane = lax.broadcasted_iota(jnp.int32, (points, LANES), 1)
    row = lax.broadcasted_iota(jnp.int32, (points, LANES), 0)
    column = lambda index: table[:, index : index + 1]

    def along_lanes(start):
        spread = jnp.zeros((points, LANES), jnp.float32)
        for node in range(nodes_own):
            spread = jnp.where(lane == row * nodes_own + node, column(start + node), spread)
        return jnp.sum(spread, axis=0, keepdims=True)

    temperature = along_lanes(16)
    entry = along_lanes(16 + nodes_own)
    assign = column(16 + 2 * nodes_own)
    theta, rows = [], []
    for corner in range(8):
        pick = lane.astype(jnp.float32) == column(17 + 2 * nodes_own + corner)
        theta.append(jnp.sum(jnp.where(pick, temperature, 0.0), axis=1, keepdims=True))
        rows.append(jnp.sum(jnp.where(pick, entry, 0.0), axis=1, keepdims=True))
    sign = lambda corner, axis: 2.0 * (corner >> axis & 1) - 1.0
    gradient = [sum(sign(a, d) * theta[a] for a in range(8)) / 4.0 for d in range(3)]
    heat = sum(theta) / 8.0
    chosen = jnp.where(
        lax.broadcasted_iota(jnp.int32, (points, points), 1).astype(jnp.float32) == assign, 1.0, 0.0
    )
    moments = jnp.dot(chosen, table, precision=HIGHEST, preferred_element_type=jnp.float32) / volume
    moment = lambda index: moments[:, index : index + 1]
    mean, mean_square = moment(12), moment(13)
    radiative = heat * heat * heat
    inverse_k = lax.rsqrt(mean_square + 2.0 * radiative * mean + radiative * radiative)
    order = ((0, 1, 2), (1, 3, 4), (2, 4, 5))
    flux = []
    for d in range(3):
        plain = sum(moment(order[d][j]) * gradient[j] for j in range(3))
        weighted = sum(moment(6 + order[d][j]) * gradient[j] for j in range(3))
        flux.append(
            gradient[d] * (mean + radiative)
            + weighted * (inverse_k * inverse_k)
            - plain * (inverse_k * (2.0 - radiative * inverse_k))
        )
    spread = jnp.zeros((points, LANES), jnp.float32)
    for d in range(3):
        spread = jnp.where(lane == d, flux[d], spread)
    mine = jnp.sum(jnp.where(row == macro, spread, 0.0), axis=0, keepdims=True)
    flux_ref[...] = mine[:, :3]
    assembled = jnp.zeros((points, LANES), jnp.float32)
    for corner in range(8):
        residual = sum(sign(corner, d) * flux[d] for d in range(3)) / 4.0
        hit = lane.astype(jnp.float32) == rows[corner] - (macro * nodes_own).astype(jnp.float32)
        assembled = assembled + jnp.where(hit, residual, 0.0)
    nodal_ref[...] = jnp.sum(assembled, axis=0, keepdims=True)[:, :nodes_own]


def on_device(
    voxel_material_ids,
    fiber_fraction,
    material_matrix_diffusivity,
    mesh_point_thermal_state,
    element_corner_ids,
    global_entry_position,
    sample_choice_per_point,
):
    slab = fiber_fraction.shape[1]
    width = fiber_fraction.shape[3]
    volume = float(width**3)
    own_nodes = mesh_point_thermal_state.shape[0]
    pencils = lax.axis_size("pencil")
    chips = pencils // 2
    groups = lax.axis_size("macro")
    tables = mode_tables(width, slab)
    plane = jax.ShapeDtypeStruct((width, width), jnp.float32)
    block = jax.ShapeDtypeStruct((slab, width, width), jnp.float32)
    params = pltpu.CompilerParams(vmem_limit_bytes=VMEM_BYTES)
    vmem = pl.BlockSpec(memory_space=pltpu.VMEM)
    smem = pl.BlockSpec(memory_space=pltpu.SMEM)

    extra = jnp.concatenate(
        [
            mesh_point_thermal_state,
            global_entry_position.astype(jnp.float32),
            sample_choice_per_point.astype(jnp.float32),
            element_corner_ids.reshape(-1).astype(jnp.float32),
        ]
    )
    extra = jnp.pad(extra, (16, LANES - 16 - extra.shape[0])).reshape(1, LANES)

    conduct, modes, keep, give = pl.pallas_call(
        analyse_kernel,
        out_shape=(block, block, plane, plane),
        in_specs=[smem] + [vmem] * 6,
        out_specs=(vmem,) * 4,
        scratch_shapes=[pltpu.VMEM((2, ROWS, width), jnp.float32)],
        compiler_params=params,
        name="analyse",
    )(
        material_matrix_diffusivity,
        voxel_material_ids,
        fiber_fraction,
        from_right(tables["basis"].T),
        from_left(tables["basis"]),
        tables["norm"],
        tables["rho"],
    )

    swap = [(i, i ^ 1) for i in range(pencils)]

    def from_chip(array, away):
        perm = [(i, (i + (2 * away if i % 2 == 0 else -2 * away)) % pencils) for i in range(pencils)]
        return lax.ppermute(array, "pencil", perm)

    step, chip_step, scale = tables["step"], tables["chip_step"], tables["scale"]
    chip = lax.ppermute(give, "pencil", swap) + step * keep
    coming = [from_chip(chip, away) for away in range(1, chips)] + [chip]
    own = coming[-1]
    for tail in coming[-2::-1]:
        own = tail + chip_step * own
    own = own * scale
    corner = corner_mask((width, width))
    other = lax.ppermute(jnp.where(corner, 0.0, keep) + step * own, "pencil", swap)

    field = (slab + 1, width, width)
    padded = (slab + 1, width + ROWS, width)
    moments = pl.pallas_call(
        moments_kernel,
        out_shape=jax.ShapeDtypeStruct((1, LANES), jnp.float32),
        in_specs=[vmem] * 10,
        out_specs=vmem,
        scratch_shapes=[pltpu.VMEM(s, jnp.float32) for s in (field, field, padded, padded, padded)],
        compiler_params=params,
        name="moments",
    )(
        conduct,
        modes,
        own,
        other,
        extra,
        tables["rho"],
        from_right(tables["basis"]),
        from_right(tables["slope"]),
        from_left(tables["basis"].T),
        from_left(tables["slope"].T),
    )

    table = jnp.broadcast_to(moments, (pencils, LANES))
    table = jnp.sum(lax.all_to_all(table, "pencil", 0, 0, tiled=True), axis=0, keepdims=True)
    table = lax.all_to_all(jnp.broadcast_to(table, (groups, LANES)), "macro", 0, 0, tiled=True)
    flux, nodal = pl.pallas_call(
        lambda *refs: close_kernel(own_nodes, volume, *refs),
        out_shape=(
            jax.ShapeDtypeStruct((1, 3), jnp.float32),
            jax.ShapeDtypeStruct((1, own_nodes), jnp.float32),
        ),
        in_specs=[vmem],
        out_specs=(vmem, vmem),
        name="close",
    )(table)
    return (flux, nodal.reshape(own_nodes))


def solution(mesh):
    in_specs = (
        P("macro", "pencil", None, None),
        P("macro", "pencil", None, None),
        P("macro", None),
        P("macro"),
        P("macro", None),
        P("macro"),
        P("macro"),
    )
    out_specs = (P("macro", None), P("macro"))
    return jax.shard_map(
        on_device, mesh=mesh, in_specs=in_specs, out_specs=out_specs, check_vma=False
    )
```

time: 227 us -> 65.5 us (0.29)
  blocking collectives: 135 us -> 27.5 us
  other arithmetic: 31.1 us -> 0.22 us
  starting transfers between devices: 25.5 us -> 5.79 us
  Pallas kernels: 0 us -> 16.1 us
  between operations: 12.1 us -> 1.4 us
  matrix products: 8.82 us -> 0 us
    psum x1 -> x0, blocking collectives: 72.3 us -> none  [on_device(): parts = lax.psum(parts, ('macro', 'pencil'))]
    unnamed x1 -> x0, blocking collectives: 63.1 us -> none
    all_to_all x0 -> x2, blocking collectives: none -> 27.5 us  [the longest x1 19.2 us: on_device(): lax.all_to_all(jnp.broadcast_to(table, (groups, LANES)), 'macro', 0, 0, t...]
    all_to_all x2 -> x0, starting transfers between devices: 25.5 us -> none  [the longest x1 18.9 us: on_device(): lax.all_to_all(tails.reshape(2 * slabs, slab, width), 'pencil', 0, 1, til...]
    pallas_call x0 -> x3, Pallas kernels: none -> 16.1 us  [the longest x1 8.9 us: on_device(): pl.pallas_call(moments_kernel, out_shape=jax.ShapeDtypeStruct((1, LANES),...]
    unnamed x31 -> x0, other arithmetic: 14 us -> none
    dot_general x10 -> x0, matrix products: 8.82 us -> none  [the longest x3 3.4 us: on_device(): jnp.einsum('xab,bz->xaz', field, z, precision=HIGHEST)]
    reduce_sum x5 -> x1, other arithmetic: 8.51 us -> 0.02 us  [on_device(): jnp.sum(lax.all_to_all(table, 'pencil', 0, 0, tiled=True), axis=0, keepdi...]
  transfers between devices with their start and end apart: 2 -> 5, of which waited for: 1 -> 4; matrix products, arithmetic and copies ran while one was open for 1% -> 0% of each run, Pallas kernels for 0% -> 0%
where the time goes in v2:
time: 65.5 us; the launch traced here: 65 us
  blocking collectives  27.5 us (42%)
  Pallas kernels  16.1 us (25%)
  local copies, waits for them, and re-layouts  7.39 us (11%)
  waiting for transfers between devices  6.54 us (10%)
  starting transfers between devices  5.79 us (9%)
  between operations  1.4 us (2%)
    all_to_all x1, blocking collectives, on_device(): lax.all_to_all(jnp.broadcast_to(table, (groups, LANES)), 'macro', 0, 0, t...  19.2 us
    pallas_call x1, Pallas kernels, on_device(): pl.pallas_call(moments_kernel, out_shape=jax.ShapeDtypeStruct((1, LANES),...  8.9 us
    all_to_all x1, blocking collectives, on_device(): lax.all_to_all(table, 'pencil', 0, 0, tiled=True)  8.28 us
    unnamed x38, local copies, waits for them, and re-layouts  7.37 us
    ppermute x3, waiting for transfers between devices, from_chip(): return lax.ppermute(array, 'pencil', perm)  5.74 us
    pallas_call x1, Pallas kernels, on_device(): pl.pallas_call(analyse_kernel, out_shape=(block, block, plane, plane), in...  4.56 us
    ppermute x1, starting transfers between devices, on_device(): chip = lax.ppermute(give, 'pencil', swap) + step * keep  3.32 us
    pallas_call x1, Pallas kernels, on_device(): pl.pallas_call(lambda *refs: close_kernel(own_nodes, volume, *refs), out_...  2.65 us
  transfers between devices with their start and end apart: 5, of which 4 were waited for; matrix products, arithmetic and copies ran while one was open for 0% of the time, Pallas kernels for 0%

profile of v2, /device:TPU:1, one launch (start us, length us, event | category | flops | bytes accessed | tf_op | source)
XLA Modules:
  0.0 65.0 jit_solution(14830820408549129839)
XLA Ops:
  0.6 1.2 %copy-done = s32[1,16,128,128]{3,2,1,0:T(8,128)S(1)} copy-done((s32[1,16,128,128]{3,2,1,0:T(8,128)S(1)}, s32[1,16,128,128]{3,2,1,0:T(8,128)}, u32[]{:S(2)}) %copy-start) | copy-done | bytes 1048600
  1.9 1.2 %copy-done.1 = f32[1,16,128,128]{3,2,1,0:T(8,128)S(1)} copy-done((f32[1,16,128,128]{3,2,1,0:T(8,128)S(1)}, f32[1,16,128,128]{3,2,1,0:T(8,128)}, u32[]{:S(2)}) %copy-start.1) | copy-done | bytes 1048600
  3.1 0.8 %copy-done.2 = f32[128,128]{1,0:T(8,128)S(1)} copy-done((f32[128,128]{1,0:T(8,128)S(1)}, f32[128,128]{1,0:T(8,128)}, u32[]{:S(2)}) %copy-start.2) | copy-done | bytes 65560
  3.9 0.9 %copy-done.8 = bf16[256,256]{1,0:T(8,128)(2,1)S(1)} copy-done((bf16[256,256]{1,0:T(8,128)(2,1)S(1)}, bf16[256,256]{1,0:T(8,128)(2,1)}, u32[]{:S(2)}) %copy-start.8) | copy-done | bytes 131096
  4.8 0.9 %copy-done.9 = bf16[256,256]{1,0:T(8,128)(2,1)S(1)} copy-done((bf16[256,256]{1,0:T(8,128)(2,1)S(1)}, bf16[256,256]{1,0:T(8,128)(2,1)}, u32[]{:S(2)}) %copy-start.9) | copy-done | bytes 131096
  5.7 0.8 %copy-done.10 = f32[128,128]{1,0:T(8,128)S(1)} copy-done((f32[128,128]{1,0:T(8,128)S(1)}, f32[128,128]{1,0:T(8,128)}, u32[]{:S(2)}) %copy-start.10) | copy-done | bytes 65560
  6.6 0.7 %copy-done.11 = f32[1,3]{1,0:T(1,128)S(1)} copy-done((f32[1,3]{1,0:T(1,128)S(1)}, f32[1,3]{1,0:T(1,128)}, u32[]{:S(2)}) %copy-start.11) | copy-done | bytes 36
  7.2 4.6 %analyse.1 = (f32[16,128,128]{2,1,0:T(8,128)S(1)}, f32[16,128,128]{2,1,0:T(8,128)S(1)}, f32[128,128]{1,0:T(8,128)S(1)}, f32[128,128]{1,0:T(8,128)S(1)}) custom-call(f32[1,3]{1,0:T(1,128)S(1)} %copy-done.11, s32[1,16,128,128]{3,2,1,0:T(8,128)S(1)} %copy-done, f32[1,16,128,128]{3,2,1,0:T(8,128)S(1)} %copy-done.1, bf16[256,256]{1,0:T(8,128)(2,1)S(1)} %copy-done.8, ...), custom_call_target="tpu_custom_call" | custom-call | tf_op jit(solution)/shard_map/analyse/pallas_call | solution.py:329
  11.8 0.0 copy-start.17
  11.8 3.3 %collective-permute-start = (f32[128,128]{1,0:T(8,128)S(1)}, f32[128,128]{1,0:T(8,128)S(1)}, u32[]{:S(2)}, u32[]{:S(2)}) collective-permute-start(f32[128,128]{1,0:T(8,128)S(1)} %get-tuple-element.10), channel_id=1, source_target_pairs={{0,1},{1,0},{2,3},{3,2},{4,5},{5,4},{6,7},{7,6},{8,9},{9,8},{10,11... | collective-permute-start | bytes 196616 | tf_op jit(solution)/shard_map/ppermute | solution.py:354
  15.8 0.6 copy-done.18
  16.5 0.0 copy-start.13
  16.5 0.0 copy-start.14
  16.5 0.8 %collective-permute-start.1 = (f32[128,128]{1,0:T(8,128)S(1)}, f32[128,128]{1,0:T(8,128)S(1)}, u32[]{:S(2)}, u32[]{:S(2)}) collective-permute-start(f32[128,128]{1,0:T(8,128)S(1)} %multiply_add_fusion.2), channel_id=1, source_target_pairs={{0,2},{1,7},{2,4},{3,1},{4,6},{5,3},{6,0},{7,5},{8,10},{9,15},{10,... | collective-permute-start | bytes 196616 | tf_op jit(solution)/shard_map/ppermute | solution.py:351
  17.3 0.5 collective-permute-start.2
  17.8 0.6 collective-permute-start.3
  18.5 1.2 %collective-permute-done.1 = f32[128,128]{1,0:T(8,128)S(1)} collective-permute-done((f32[128,128]{1,0:T(8,128)S(1)}, f32[128,128]{1,0:T(8,128)S(1)}, u32[]{:S(2)}, u32[]{:S(2)}) %collective-permute-start.1) | collective-permute-done | bytes 65568 | tf_op jit(solution)/shard_map/ppermute | solution.py:351
  19.7 3.0 %collective-permute-done.2 = f32[128,128]{1,0:T(8,128)S(1)} collective-permute-done((f32[128,128]{1,0:T(8,128)S(1)}, f32[128,128]{1,0:T(8,128)S(1)}, u32[]{:S(2)}, u32[]{:S(2)}) %collective-permute-start.2) | collective-permute-done | bytes 65568 | tf_op jit(solution)/shard_map/ppermute | solution.py:351
  22.7 1.5 %collective-permute-done.3 = f32[128,128]{1,0:T(8,128)S(1)} collective-permute-done((f32[128,128]{1,0:T(8,128)S(1)}, f32[128,128]{1,0:T(8,128)S(1)}, u32[]{:S(2)}, u32[]{:S(2)}) %collective-permute-start.3) | collective-permute-done | bytes 65568 | tf_op jit(solution)/shard_map/ppermute | solution.py:351
  24.2 0.0 copy-start.6
  24.2 0.0 copy-start.7
  24.3 0.1 multiply_add_fusion
  24.3 0.0 copy-start.4
  24.4 0.5 collective-permute-start.4
  24.9 0.0 copy-done.16
  24.9 0.1 fusion.extra_ref
  25.0 0.8 %collective-permute-done.4.other_ref = f32[128,128]{1,0:T(8,128)S(1)} collective-permute-done((f32[128,128]{1,0:T(8,128)S(1)}, f32[128,128]{1,0:T(8,128)S(1)}, u32[]{:S(2)}, u32[]{:S(2)}) %collective-permute-start.4) | collective-permute-done | bytes 65568 | tf_op jit(solution)/shard_map/ppermute | solution.py:361
  25.8 0.1 copy-done.3
  25.9 8.9 %moments.1 = f32[1,128]{1,0:T(1,128)S(1)} custom-call(f32[16,128,128]{2,1,0:T(8,128)S(1)} %get-tuple-element.8.conduct_ref, f32[16,128,128]{2,1,0:T(8,128)S(1)} %get-tuple-element.9.modes_ref, f32[128,128]{1,0:T(8,128)S(1)} %mul.22.own_ref, f32[128,128]{1,0:T(8,128)S(1)} %collective-permute-done.4.other_ref, f32[1,128]{1,0:T(1,128)S(1)} %fusion.extra_ref, ...), custom_call_target="tpu_custom_call" | custom-call | tf_op jit(solution)/shard_map/moments/pallas_call | solution.py:365
  34.8 8.3 %all_to_all.14 = f32[8,1,128]{2,1,0:T(1,128)S(1)} all-to-all(f32[8,1,128]{2,1,0:T(1,128)S(1)} %broadcast_in_dim.16), channel_id=1, replica_groups=mesh['macro'=32,'pencil'=8] {'pencil'}, dimensions={0} | all-to-all | bytes 8192 | tf_op jit(solution)/shard_map/all_to_all | solution.py:387
  43.1 19.2 %all_to_all.15 = f32[32,1,128]{2,1,0:T(1,128)} all-to-all(f32[32,1,128]{2,1,0:T(1,128)S(1)} %broadcast_in_dim.17), channel_id=1, replica_groups=mesh['macro'=32,'pencil'=8] {'macro'}, dimensions={0} | all-to-all | bytes 32768 | tf_op jit(solution)/shard_map/all_to_all | solution.py:388
  62.3 2.7 %close.1 = (f32[1,3]{1,0:T(1,128)}, f32[1,4]{1,0:T(1,128)}) custom-call(f32[32,128]{1,0:T(8,128)} %bitcast.9), custom_call_target="tpu_custom_call" | custom-call | tf_op jit(solution)/shard_map/close/pallas_call | solution.py:389
  (31 shorter events, 0.1 us)
Async XLA Ops:
  0.6 1.2 %copy-start = (s32[1,16,128,128]{3,2,1,0:T(8,128)S(1)}, s32[1,16,128,128]{3,2,1,0:T(8,128)}, u32[]{:S(2)}) copy-start(s32[1,16,128,128]{3,2,1,0:T(8,128)} %ids_ref.1) | copy-start | bytes 3145732
  1.9 1.2 %copy-start.1 = (f32[1,16,128,128]{3,2,1,0:T(8,128)S(1)}, f32[1,16,128,128]{3,2,1,0:T(8,128)}, u32[]{:S(2)}) copy-start(f32[1,16,128,128]{3,2,1,0:T(8,128)} %fiber_ref.1) | copy-start | bytes 3145732
  3.1 0.8 %copy-start.2 = (f32[128,128]{1,0:T(8,128)S(1)}, f32[128,128]{1,0:T(8,128)}, u32[]{:S(2)}) copy-start(f32[128,128]{1,0:T(8,128)} %constant.31.clone.rho_ref) | copy-start | bytes 196612
  3.9 0.9 %copy-start.8 = (bf16[256,256]{1,0:T(8,128)(2,1)S(1)}, bf16[256,256]{1,0:T(8,128)(2,1)}, u32[]{:S(2)}) copy-start(bf16[256,256]{1,0:T(8,128)(2,1)} %constant.28.clone.right_ref) | copy-start | bytes 393220
  4.8 0.9 %copy-start.9 = (bf16[256,256]{1,0:T(8,128)(2,1)S(1)}, bf16[256,256]{1,0:T(8,128)(2,1)}, u32[]{:S(2)}) copy-start(bf16[256,256]{1,0:T(8,128)(2,1)} %constant.29.clone.left_ref) | copy-start | bytes 393220
  5.7 0.8 %copy-start.10 = (f32[128,128]{1,0:T(8,128)S(1)}, f32[128,128]{1,0:T(8,128)}, u32[]{:S(2)}) copy-start(f32[128,128]{1,0:T(8,128)} %constant.30.clone.norm_ref) | copy-start | bytes 196612
  6.6 0.7 %copy-start.11 = (f32[1,3]{1,0:T(1,128)S(1)}, f32[1,3]{1,0:T(1,128)}, u32[]{:S(2)}) copy-start(f32[1,3]{1,0:T(1,128)} %material_ref.1) | copy-start | bytes 40
  7.2 9.2 %copy-start.15 = (f32[128,128]{1,0:T(8,128)S(1)}, f32[128,128]{1,0:T(8,128)}, u32[]{:S(2)}) copy-start(f32[128,128]{1,0:T(8,128)} %constant.32.clone) | copy-start | bytes 196612
  11.8 3.3 %copy-start.17 = (s32[1,8]{1,0:T(1,128)S(1)}, s32[1,8]{1,0:T(1,128)}, u32[]{:S(2)}) copy-start(s32[1,8]{1,0:T(1,128)} %param.22) | copy-start | bytes 100
  11.8 4.6 %collective-permute-start = (f32[128,128]{1,0:T(8,128)S(1)}, f32[128,128]{1,0:T(8,128)S(1)}, u32[]{:S(2)}, u32[]{:S(2)}) collective-permute-start(f32[128,128]{1,0:T(8,128)S(1)} %get-tuple-element.10), channel_id=1, source_target_pairs={{0,1},{1,0},{2,3},{3,2},{4,5},{5,4},{6,7},{7,6},{8,9},{9,8},{10,11... | collective-permute-start | bytes 196616 | tf_op jit(solution)/shard_map/ppermute | solution.py:354
  15.8 0.7 %copy-start.18 = (s32[4]{0:T(128)S(1)}, s32[4]{0:T(128)}, u32[]{:S(2)}) copy-start(s32[4]{0:T(128)} %param.23) | copy-start | bytes 52
  16.5 7.8 %copy-start.13 = (f32[128,128]{1,0:T(8,128)S(1)}, f32[128,128]{1,0:T(8,128)}, u32[]{:S(2)}) copy-start(f32[128,128]{1,0:T(8,128)} %constant.48) | copy-start | bytes 196612
  16.5 7.7 %copy-start.14 = (f32[128,128]{1,0:T(8,128)S(1)}, f32[128,128]{1,0:T(8,128)}, u32[]{:S(2)}) copy-start(f32[128,128]{1,0:T(8,128)} %constant.33.clone) | copy-start | bytes 196612
  16.5 3.2 %collective-permute-start.1 = (f32[128,128]{1,0:T(8,128)S(1)}, f32[128,128]{1,0:T(8,128)S(1)}, u32[]{:S(2)}, u32[]{:S(2)}) collective-permute-start(f32[128,128]{1,0:T(8,128)S(1)} %multiply_add_fusion.2), channel_id=1, source_target_pairs={{0,2},{1,7},{2,4},{3,1},{4,6},{5,3},{6,0},{7,5},{8,10},{9,15},{10,... | collective-permute-start | bytes 196616 | tf_op jit(solution)/shard_map/ppermute | solution.py:351
  17.3 5.4 %collective-permute-start.2 = (f32[128,128]{1,0:T(8,128)S(1)}, f32[128,128]{1,0:T(8,128)S(1)}, u32[]{:S(2)}, u32[]{:S(2)}) collective-permute-start(f32[128,128]{1,0:T(8,128)S(1)} %multiply_add_fusion.2), channel_id=1, source_target_pairs={{0,4},{1,5},{2,6},{3,7},{4,0},{5,1},{6,2},{7,3},{8,12},{9,13},{10,... | collective-permute-start | bytes 196616 | tf_op jit(solution)/shard_map/ppermute | solution.py:351
  17.8 6.4 %collective-permute-start.3 = (f32[128,128]{1,0:T(8,128)S(1)}, f32[128,128]{1,0:T(8,128)S(1)}, u32[]{:S(2)}, u32[]{:S(2)}) collective-permute-start(f32[128,128]{1,0:T(8,128)S(1)} %multiply_add_fusion.2), channel_id=1, source_target_pairs={{0,6},{1,3},{2,0},{3,5},{4,2},{5,7},{6,4},{7,1},{8,14},{9,11},{10,... | collective-permute-start | bytes 196616 | tf_op jit(solution)/shard_map/ppermute | solution.py:351
  18.5 6.5 %copy-start.12 = (f32[128,128]{1,0:T(8,128)S(1)}, f32[128,128]{1,0:T(8,128)}, u32[]{:S(2)}) copy-start(f32[128,128]{1,0:T(8,128)} %constant.34.clone) | copy-start | bytes 196612
  24.2 0.7 %copy-start.16 = (f32[4]{0:T(128)S(1)}, f32[4]{0:T(128)}, u32[]{:S(2)}) copy-start(f32[4]{0:T(128)} %param.21) | copy-start | bytes 52
  24.2 1.6 %copy-start.5 = (bf16[256,256]{1,0:T(8,128)(2,1)S(1)}, bf16[256,256]{1,0:T(8,128)(2,1)}, u32[]{:S(2)}) copy-start(bf16[256,256]{1,0:T(8,128)(2,1)} %constant.36.clone.right_slope_ref) | copy-start | bytes 393220
  24.2 1.6 %copy-start.6 = (bf16[256,256]{1,0:T(8,128)(2,1)S(1)}, bf16[256,256]{1,0:T(8,128)(2,1)}, u32[]{:S(2)}) copy-start(bf16[256,256]{1,0:T(8,128)(2,1)} %constant.37.clone.left_basis_ref) | copy-start | bytes 393220
  24.2 1.5 %copy-start.7 = (bf16[256,256]{1,0:T(8,128)(2,1)S(1)}, bf16[256,256]{1,0:T(8,128)(2,1)}, u32[]{:S(2)}) copy-start(bf16[256,256]{1,0:T(8,128)(2,1)} %constant.38.clone.left_slope_ref) | copy-start | bytes 393220
  24.3 1.4 %copy-start.4 = (bf16[256,256]{1,0:T(8,128)(2,1)S(1)}, bf16[256,256]{1,0:T(8,128)(2,1)}, u32[]{:S(2)}) copy-start(bf16[256,256]{1,0:T(8,128)(2,1)} %constant.35.clone.right_basis_ref) | copy-start | bytes 393220
  24.4 1.4 %collective-permute-start.4 = (f32[128,128]{1,0:T(8,128)S(1)}, f32[128,128]{1,0:T(8,128)S(1)}, u32[]{:S(2)}, u32[]{:S(2)}) collective-permute-start(f32[128,128]{1,0:T(8,128)S(1)} %get-tuple-element.14), channel_id=1, source_target_pairs={{0,1},{1,0},{2,3},{3,2},{4,5},{5,4},{6,7},{7,6},{8,9},{9,8},{10,11... | collective-permute-start | bytes 196616 | tf_op jit(solution)/shard_map/ppermute | solution.py:361
  25.0 0.9 %copy-start.3 = (f32[128,128]{1,0:T(8,128)S(1)}, f32[128,128]{1,0:T(8,128)}, u32[]{:S(2)}) copy-start(f32[128,128]{1,0:T(8,128)} %constant.31.clone.rho_ref) | copy-start | bytes 196612

commit v3 on v2

--- a/solution.py
+++ b/solution.py
@@ -12,7 +12,9 @@
 PHASES = 3
 LANES = 128
 ROWS = 8
+PIECES = 4
 VMEM_BYTES = 48 * 1024 * 1024
+HBM_INPUTS_BYTES = 56 * 1024 * 1024
 
 HIGHEST = lax.Precision.HIGHEST
 
@@ -86,123 +88,166 @@
 
 
 def analyse_kernel(
-    material_ref, ids_ref, fiber_ref, right_ref, left_ref, norm_ref, rho_ref,
-    conduct_ref, modes_ref, keep_ref, give_ref, sums_ref,
+    material_hbm, ids_hbm, fiber_hbm, right_hbm, left_hbm, norm_hbm, rho_hbm,
+    conduct_hbm, modes_hbm, keep_ref, give_ref,
+    conduct_ref, modes_ref, sums_ref, material_ref, ids_ref, fiber_ref, right_ref, left_ref, norm_ref, rho_ref,
+    table_sems, ids_sems, fiber_sems, conduct_sems, modes_sems,
 ):
-    slab, width = fiber_ref.shape[1], fiber_ref.shape[3]
+    slab, width = fiber_ref.shape[0], fiber_ref.shape[2]
+    group = slab // PIECES
     odd = lax.rem(lax.axis_index("pencil"), 2) == 1
+
+    def ids_copy(piece):
+        at = pl.ds(piece * group, group)
+        return pltpu.make_async_copy(ids_hbm.at[0, at], ids_ref.at[at], ids_sems.at[piece])
+
+    def fiber_copy(piece):
+        at = pl.ds(piece * group, group)
+        return pltpu.make_async_copy(fiber_hbm.at[0, at], fiber_ref.at[at], fiber_sems.at[piece])
+
+    def conduct_copy(piece):
+        at = pl.ds(piece * group, group)
+        return pltpu.make_async_copy(conduct_ref.at[at], conduct_hbm.at[at], conduct_sems.at[piece])
+
+    def modes_copy(piece):
+        at = pl.ds(piece * group, group)
+        return pltpu.make_async_copy(modes_ref.at[at], modes_hbm.at[at], modes_sems.at[piece])
+
+    tables = [
+        pltpu.make_async_copy(source, target, table_sems.at[index])
+        for index, (source, target) in enumerate(
+            (
+                (material_hbm, material_ref),
+                (right_hbm, right_ref),
+                (left_hbm, left_ref),
+                (norm_hbm, norm_ref),
+                (rho_hbm, rho_ref),
+            )
+        )
+    ]
+    tables[0].start()
+    ids_copy(0).start()
+    fiber_copy(0).start()
+    for copy in tables[1:]:
+        copy.start()
+    for piece in range(1, PIECES):
+        ids_copy(piece).start()
+        fiber_copy(piece).start()
     sums_ref[...] = jnp.zeros_like(sums_ref)
-
-    def pair(step, carry):
+    for copy in tables:
+        copy.wait()
+
+    def few(piece, carry):
+        ids_copy(piece).wait()
+        fiber_copy(piece).wait()
         planes = []
-        for part in range(2):
-            x = 2 * step + part
-            ids = ids_ref[0, x]
-            conduct = jnp.zeros((width, width), jnp.float32)
-            for phase in range(PHASES):
-                conduct = jnp.where(ids == phase, material_ref[0, phase], conduct)
-            conduct = conduct * fiber_ref[0, x]
+        for part in range(group):
+            x = group * piece + part
+            ids = ids_ref[x]
+            conduct = jnp.where(
+                ids == 0, material_ref[0, 0], jnp.where(ids == 1, material_ref[0, 1], material_ref[0, 2])
+            )
+            conduct = conduct * fiber_ref[x]
             conduct_ref[x] = conduct
             tiles = conduct.reshape(width // ROWS, ROWS, width)
             sums_ref[0] += jnp.sum(tiles, axis=0)
             sums_ref[1] += jnp.sum(tiles * tiles, axis=0)
             planes.append(beside(conduct))
+        conduct_copy(piece).start()
         lines = product(jnp.concatenate(planes, axis=0), right_ref[...])
         lines = lines[:, :width] + lines[:, width:]
-        lines = jnp.concatenate([lines[:width], lines[width:]], axis=1)
-        modes = product(left_ref[...], stacked(lines))
-        modes = modes[:width] + modes[width:]
         norm = norm_ref[...]
-        modes_ref[2 * step] = modes[:, :width] * norm
-        modes_ref[2 * step + 1] = modes[:, width:] * norm
+        for part in range(0, group, 2):
+            pair = jnp.concatenate(
+                [lines[part * width : (part + 1) * width], lines[(part + 1) * width : (part + 2) * width]], axis=1
+            )
+            modes = product(left_ref[...], stacked(pair))
+            modes = modes[:width] + modes[width:]
+            modes_ref[group * piece + part] = modes[:, :width] * norm
+            modes_ref[group * piece + part + 1] = modes[:, width:] * norm
+        modes_copy(piece).start()
         return carry
 
-    lax.fori_loop(0, slab // 2, pair, 0)
+    lax.fori_loop(0, PIECES, few, 0)
     total = jnp.sum(sums_ref[0])
     total_square = jnp.sum(sums_ref[1])
-
-    def chunk(index, carry):
-        at = pl.ds(pl.multiple_of(index * ROWS, ROWS), ROWS)
-        rho = rho_ref[at]
-        right = modes_ref[0, at]
-        left = modes_ref[slab - 1, at]
-        for x in range(1, slab):
-            right = modes_ref[x, at] + rho * right
-            left = modes_ref[slab - 1 - x, at] + rho * left
-        corner = corner_mask(right.shape) & (index == 0)
-        right = jnp.where(corner, total, right)
-        left = jnp.where(corner, total_square, left)
-        keep_ref[at] = jnp.where(odd, left, right)
-        give_ref[at] = jnp.where(odd, right, left)
-        return carry
-
-    lax.fori_loop(0, width // ROWS, chunk, 0)
+    rho = rho_ref[...]
+    right = modes_ref[0]
+    left = modes_ref[slab - 1]
+    for x in range(1, slab):
+        right = modes_ref[x] + rho * right
+        left = modes_ref[slab - 1 - x] + rho * left
+    corner = corner_mask(right.shape)
+    right = jnp.where(corner, total, right)
+    left = jnp.where(corner, total_square, left)
+    keep_ref[...] = jnp.where(odd, left, right)
+    give_ref[...] = jnp.where(odd, right, left)
+    for piece in range(PIECES):
+        conduct_copy(piece).wait()
+        modes_copy(piece).wait()
 
 
 def moments_kernel(
     conduct_ref, modes_ref, own_ref, other_ref, extra_ref, rho_ref,
     right_basis_ref, right_slope_ref, left_basis_ref, left_slope_ref,
-    out_ref, potential_ref, rise_ref, px_ref, py_ref, pz_ref,
+    out_ref, potential_ref, rise_ref, px_ref, py_ref, pz_ref, lines_ref,
 ):
     slab, width = conduct_ref.shape[0], conduct_ref.shape[2]
     volume = float(width**3)
     pencil = lax.axis_index("pencil")
     odd = lax.rem(pencil, 2) == 1
 
-    def sweep(index, carry):
-        at = pl.ds(pl.multiple_of(index * ROWS, ROWS), ROWS)
-        rho = rho_ref[at]
-        corner = corner_mask(rho.shape) & (index == 0)
-        own, other = own_ref[at], other_ref[at]
-        before = jnp.where(corner, 0.0, jnp.where(odd, other, own))
-        after = jnp.where(corner, 0.0, jnp.where(odd, own, other))
-        behind = [after, rho * after]
-        for x in range(slab - 1, -1, -1):
-            behind.append(rho * (modes_ref[x, at] + behind[-1]))
-        behind = behind[::-1]
-        ahead = before
-        last = ahead + behind[0]
-        for x in range(slab + 1):
-            ahead = rho * ahead
-            if x < slab:
-                ahead = ahead + modes_ref[x, at]
-            here = ahead + behind[x + 1]
-            potential_ref[x, at] = here
-            rise_ref[x, at] = here - last
-            last = here
-        return carry
-
-    lax.fori_loop(0, width // ROWS, sweep, 0)
+    corner = corner_mask((width, width))
+    first_plane = jnp.where(odd, other_ref[...], own_ref[...])
+    second_plane = jnp.where(odd, own_ref[...], other_ref[...])
+    first = jnp.sum(jnp.where(corner, first_plane, 0.0)[:ROWS])
+    second = jnp.sum(jnp.where(corner, second_plane, 0.0)[:ROWS])
+    mean = first / volume
+    rho = rho_ref[...]
+    behind = jnp.where(corner, 0.0, second_plane)
+    potential_ref[slab] = behind
+    behind = rho * behind
+    potential_ref[slab - 1] = behind
+    for x in range(slab - 2, -1, -1):
+        behind = rho * (modes_ref[x + 1] + behind)
+        potential_ref[x] = behind
+    ahead = jnp.where(corner, 0.0, first_plane)
+    last = ahead + rho * (modes_ref[0] + behind)
+    for x in range(slab + 1):
+        ahead = rho * ahead
+        if x < slab:
+            ahead = ahead + modes_ref[x]
+        here = ahead + potential_ref[x]
+        potential_ref[x] = here
+        rise_ref[x] = here - last
+        last = here
 
     def put(ref, x, plane):
         ref[x, :width] = plane
         ref[x, width:] = plane[:ROWS]
 
-    def synthesise(x):
+    def along_z(x):
         along = beside(potential_ref[x])
         rise = product(beside(rise_ref[x]), right_basis_ref[...])
         slope = product(along, right_slope_ref[...])
         plain = product(along, right_basis_ref[...])
-        rise = rise[:, :width] + rise[:, width:]
-        slope = slope[:, :width] + slope[:, width:]
-        plain = plain[:, :width] + plain[:, width:]
-        both = product(left_basis_ref[...], stacked(jnp.concatenate([slope, rise], axis=1)))
+        for place, lines in enumerate((slope, rise, plain)):
+            high, low = halves(lines[:, :width] + lines[:, width:])
+            lanes = pl.ds(place * width, width)
+            lines_ref[:width, lanes] = high
+            lines_ref[width:, lanes] = low
+
+    def along_y(x):
+        both = product(left_basis_ref[...], lines_ref[:, : 2 * width])
         both = both[:width] + both[width:]
-        third = product(left_slope_ref[...], stacked(plain))
+        third = product(left_slope_ref[...], lines_ref[:, 2 * width :])
         third = third[:width] + third[width:]
         put(pz_ref, x, both[:, :width])
         put(px_ref, x, both[:, width:])
         put(py_ref, x, third)
 
-    corner = corner_mask((ROWS, width))
-    own = jnp.sum(jnp.where(corner, own_ref[:ROWS], 0.0))
-    other = jnp.sum(jnp.where(corner, other_ref[:ROWS], 0.0))
-    first = jnp.where(odd, other, own)
-    second = jnp.where(odd, own, other)
-    mean = first / volume
-
     def plane(step, totals):
-        x = jnp.maximum(step - 2, 0)
+        x = jnp.maximum(step - 3, 0)
         totals = list(totals)
         for chunk in range(width // ROWS):
             at = pl.ds(chunk * ROWS, ROWS)
@@ -222,11 +267,12 @@
                     totals[at_entry] = totals[at_entry] + term
                     totals[6 + at_entry] = totals[6 + at_entry] + conduct * term
                     at_entry += 1
-        synthesise(jnp.minimum(step, slab))
-        return tuple(jnp.where(step < 2, 0.0, total) for total in totals)
+        along_y(jnp.clip(step - 1, 0, slab))
+        along_z(jnp.minimum(step, slab))
+        return tuple(jnp.where(step < 3, 0.0, total) for total in totals)
 
     nothing = jnp.zeros((ROWS, width), jnp.float32)
-    totals = lax.fori_loop(0, slab + 2, plane, (nothing,) * 12)
+    totals = lax.fori_loop(0, slab + 3, plane, (nothing,) * 12)
     lines = [jnp.sum(total, axis=0, keepdims=True) for total in totals]
     lines = jnp.concatenate(lines + [jnp.zeros((4, width), jnp.float32)], axis=0)
     column = jnp.sum(lines, axis=1, keepdims=True)
@@ -245,20 +291,22 @@
     row = lax.broadcasted_iota(jnp.int32, (points, LANES), 0)
     column = lambda index: table[:, index : index + 1]
 
-    def along_lanes(start):
-        spread = jnp.zeros((points, LANES), jnp.float32)
-        for node in range(nodes_own):
-            spread = jnp.where(lane == row * nodes_own + node, column(start + node), spread)
-        return jnp.sum(spread, axis=0, keepdims=True)
-
-    temperature = along_lanes(16)
-    entry = along_lanes(16 + nodes_own)
+    temperature = jnp.zeros((points, LANES), jnp.float32)
+    node_of = jnp.zeros((points, LANES), jnp.float32)
+    mine = (macro * nodes_own + lane).astype(jnp.float32)
+    for node in range(nodes_own):
+        at = row * nodes_own + node
+        temperature = jnp.where(lane == at, column(16 + node), temperature)
+        node_of = jnp.where(column(16 + nodes_own + node) == mine, at.astype(jnp.float32), node_of)
+    temperature = jnp.sum(temperature, axis=0, keepdims=True)
+    node_of = jnp.sum(node_of, axis=0, keepdims=True)
+    node_of = jnp.where(lane[:1] < nodes_own, node_of, -1.0)
     assign = column(16 + 2 * nodes_own)
-    theta, rows = [], []
+    corners = [column(17 + 2 * nodes_own + corner) for corner in range(8)]
+    theta = []
     for corner in range(8):
-        pick = lane.astype(jnp.float32) == column(17 + 2 * nodes_own + corner)
+        pick = lane.astype(jnp.float32) == corners[corner]
         theta.append(jnp.sum(jnp.where(pick, temperature, 0.0), axis=1, keepdims=True))
-        rows.append(jnp.sum(jnp.where(pick, entry, 0.0), axis=1, keepdims=True))
     sign = lambda corner, axis: 2.0 * (corner >> axis & 1) - 1.0
     gradient = [sum(sign(a, d) * theta[a] for a in range(8)) / 4.0 for d in range(3)]
     heat = sum(theta) / 8.0
@@ -283,13 +331,11 @@
     spread = jnp.zeros((points, LANES), jnp.float32)
     for d in range(3):
         spread = jnp.where(lane == d, flux[d], spread)
-    mine = jnp.sum(jnp.where(row == macro, spread, 0.0), axis=0, keepdims=True)
-    flux_ref[...] = mine[:, :3]
+    flux_ref[...] = jnp.sum(jnp.where(row == macro, spread, 0.0), axis=0, keepdims=True)[:, :3]
     assembled = jnp.zeros((points, LANES), jnp.float32)
     for corner in range(8):
         residual = sum(sign(corner, d) * flux[d] for d in range(3)) / 4.0
-        hit = lane.astype(jnp.float32) == rows[corner] - (macro * nodes_own).astype(jnp.float32)
-        assembled = assembled + jnp.where(hit, residual, 0.0)
+        assembled = assembled + jnp.where(corners[corner] == node_of, residual, 0.0)
     nodal_ref[...] = jnp.sum(assembled, axis=0, keepdims=True)[:, :nodes_own]
 
 
@@ -314,25 +360,31 @@
     block = jax.ShapeDtypeStruct((slab, width, width), jnp.float32)
     params = pltpu.CompilerParams(vmem_limit_bytes=VMEM_BYTES)
     vmem = pl.BlockSpec(memory_space=pltpu.VMEM)
-    smem = pl.BlockSpec(memory_space=pltpu.SMEM)
-
-    extra = jnp.concatenate(
-        [
-            mesh_point_thermal_state,
-            global_entry_position.astype(jnp.float32),
-            sample_choice_per_point.astype(jnp.float32),
-            element_corner_ids.reshape(-1).astype(jnp.float32),
-        ]
-    )
-    extra = jnp.pad(extra, (16, LANES - 16 - extra.shape[0])).reshape(1, LANES)
+    hbm = pl.BlockSpec(memory_space=pltpu.HBM)
 
     conduct, modes, keep, give = pl.pallas_call(
         analyse_kernel,
         out_shape=(block, block, plane, plane),
-        in_specs=[smem] + [vmem] * 6,
-        out_specs=(vmem,) * 4,
-        scratch_shapes=[pltpu.VMEM((2, ROWS, width), jnp.float32)],
-        compiler_params=params,
+        in_specs=[hbm] * 7,
+        out_specs=(hbm, hbm, vmem, vmem),
+        scratch_shapes=[
+            pltpu.VMEM((slab, width, width), jnp.float32),
+            pltpu.VMEM((slab, width, width), jnp.float32),
+            pltpu.VMEM((2, ROWS, width), jnp.float32),
+            pltpu.SMEM((1, PHASES), jnp.float32),
+            pltpu.VMEM((slab, width, width), jnp.int32),
+            pltpu.VMEM((slab, width, width), jnp.float32),
+            pltpu.VMEM((2 * width, 2 * width), jnp.bfloat16),
+            pltpu.VMEM((2 * width, 2 * width), jnp.bfloat16),
+            pltpu.VMEM((width, width), jnp.float32),
+            pltpu.VMEM((width, width), jnp.float32),
+            pltpu.SemaphoreType.DMA((5,)),
+            pltpu.SemaphoreType.DMA((PIECES,)),
+            pltpu.SemaphoreType.DMA((PIECES,)),
+            pltpu.SemaphoreType.DMA((PIECES,)),
+            pltpu.SemaphoreType.DMA((PIECES,)),
+        ],
+        compiler_params=pltpu.CompilerParams(vmem_limit_bytes=HBM_INPUTS_BYTES),
         name="analyse",
     )(
         material_matrix_diffusivity,
@@ -352,6 +404,18 @@
 
     step, chip_step, scale = tables["step"], tables["chip_step"], tables["scale"]
     chip = lax.ppermute(give, "pencil", swap) + step * keep
+    chip, temperature, entry, assign, corners = lax.optimization_barrier(
+        (chip, mesh_point_thermal_state, global_entry_position, sample_choice_per_point, element_corner_ids)
+    )
+    extra = jnp.concatenate(
+        [
+            temperature,
+            entry.astype(jnp.float32),
+            assign.astype(jnp.float32),
+            corners.reshape(-1).astype(jnp.float32),
+        ]
+    )
+    extra = jnp.pad(extra, (16, LANES - 16 - extra.shape[0])).reshape(1, LANES)
     coming = [from_chip(chip, away) for away in range(1, chips)] + [chip]
     own = coming[-1]
     for tail in coming[-2::-1]:
@@ -367,7 +431,8 @@
         out_shape=jax.ShapeDtypeStruct((1, LANES), jnp.float32),
         in_specs=[vmem] * 10,
         out_specs=vmem,
-        scratch_shapes=[pltpu.VMEM(s, jnp.float32) for s in (field, field, padded, padded, padded)],
+        scratch_shapes=[pltpu.VMEM(s, jnp.float32) for s in (field, field, padded, padded, padded)]
+        + [pltpu.VMEM((2 * width, 3 * width), jnp.bfloat16)],
         compiler_params=params,
         name="moments",
     )(

time: 65.5 us -> 59.3 us (0.905)
  local copies, waits for them, and re-layouts: 7.39 us -> 1.32 us
  Pallas kernels: 16.1 us -> 14.1 us
  other arithmetic: 0.22 us -> 1.89 us
    unnamed x38 -> x28, local copies, waits for them, and re-layouts: 7.37 us -> 1.3 us
    pallas_call x1, Pallas kernels: 8.9 us -> 6.77 us  [on_device(): pl.pallas_call(moments_kernel, out_shape=jax.ShapeDtypeStruct((1, LANES),...]
    add x1, other arithmetic: 0.01 us -> 0.85 us  [on_device(): chip = lax.ppermute(give, 'pencil', swap) + step * keep]
    add x1, other arithmetic: 0.09 us -> 0.93 us  [on_device(): jnp.where(corner, 0.0, keep) + step * own]
  transfers between devices with their start and end apart: 5 -> 5, of which waited for: 4 -> 5; matrix products, arithmetic and copies ran while one was open for 0% -> 0% of each run, Pallas kernels for 0% -> 0%
where the time goes in v3:
time: 59.3 us; the launch traced here: 59 us
  blocking collectives  27.8 us (47%)
  Pallas kernels  14.1 us (24%)
  waiting for transfers between devices  6.61 us (11%)
  starting transfers between devices  5.74 us (10%)
  other arithmetic  1.89 us (3%)
  between operations  1.45 us (2%)
  local copies, waits for them, and re-layouts  1.32 us (2%)
    all_to_all x1, blocking collectives, on_device(): lax.all_to_all(jnp.broadcast_to(table, (groups, LANES)), 'macro', 0, 0, t...  19.4 us
    all_to_all x1, blocking collectives, on_device(): lax.all_to_all(table, 'pencil', 0, 0, tiled=True)  8.43 us
    pallas_call x1, Pallas kernels, on_device(): pl.pallas_call(moments_kernel, out_shape=jax.ShapeDtypeStruct((1, LANES),...  6.77 us
    ppermute x3, waiting for transfers between devices, from_chip(): return lax.ppermute(array, 'pencil', perm)  5.36 us
    pallas_call x1, Pallas kernels, on_device(): pl.pallas_call(analyse_kernel, out_shape=(block, block, plane, plane), in...  5.12 us
    ppermute x1, starting transfers between devices, on_device(): chip = lax.ppermute(give, 'pencil', swap) + step * keep  3.33 us
    pallas_call x1, Pallas kernels, on_device(): pl.pallas_call(lambda *refs: close_kernel(own_nodes, volume, *refs), out_...  2.24 us
    ppermute x3, starting transfers between devices, from_chip(): return lax.ppermute(array, 'pencil', perm)  1.95 us
  transfers between devices with their start and end apart: 5, of which 5 were waited for; matrix products, arithmetic and copies ran while one was open for 0% of the time, Pallas kernels for 0%

profile of v3, /device:TPU:1, one launch (start us, length us, event | category | flops | bytes accessed | tf_op | source)
XLA Modules:
  0.0 59.0 jit_solution(16210838224591193921)
XLA Ops:
  0.6 0.0 copy-start.10
  0.7 0.0 copy-start.8
  0.7 0.0 copy-start.9
  0.7 0.0 copy-start.11
  0.7 0.0 copy-start.7
  0.7 0.0 copy-start.2
  0.7 0.0 copy-start.3
  0.7 0.0 copy-start.4
  0.8 0.0 copy-start.5
  0.8 0.0 copy-start.6
  0.8 5.1 %analyse.1 = (f32[16,128,128]{2,1,0:T(8,128)}, f32[16,128,128]{2,1,0:T(8,128)}, f32[128,128]{1,0:T(8,128)}, f32[128,128]{1,0:T(8,128)}) custom-call(f32[1,3]{1,0:T(1,128)} %material_hbm.1, s32[1,16,128,128]{3,2,1,0:T(8,128)} %ids_hbm.1, f32[1,16,128,128]{3,2,1,0:T(8,128)} %fiber_hbm.1, bf16[256,256]{1,0:T(8,128)(2,1)} %constant.28.clone.right_hbm, ...), custom_call_target="tpu_custom_call" | custom-call | tf_op jit(solution)/shard_map/analyse/pallas_call | solution.py:365
  5.9 3.3 %collective-permute-start = (f32[128,128]{1,0:T(8,128)}, f32[128,128]{1,0:T(8,128)S(1)}, u32[]{:S(2)}, u32[]{:S(2)}) collective-permute-start(f32[128,128]{1,0:T(8,128)} %get-tuple-element.15), channel_id=1, source_target_pairs={{0,1},{1,0},{2,3},{3,2},{4,5},{5,4},{6,7},{7,6},{8,9},{9,8},{10,11... | collective-permute-start | bytes 196616 | tf_op jit(solution)/shard_map/ppermute | solution.py:406
  9.9 0.4 collective-permute-done
  10.4 0.9 %multiply_add_fusion.2 = f32[128,128]{1,0:T(8,128)S(1)} fusion(f32[128,128]{1,0:T(8,128)S(1)} %collective-permute-done, f32[128,128]{1,0:T(8,128)S(1)} %copy-done.10, f32[128,128]{1,0:T(8,128)} %get-tuple-element.16), kind=kLoop, calls=%fused_computation.2 | loop fusion | flops 32768 | bytes 262144 | tf_op jit(solution)/shard_map/add | solution.py:406
  11.2 0.8 %collective-permute-start.1 = (f32[128,128]{1,0:T(8,128)S(1)}, f32[128,128]{1,0:T(8,128)S(1)}, u32[]{:S(2)}, u32[]{:S(2)}) collective-permute-start(f32[128,128]{1,0:T(8,128)S(1)} %multiply_add_fusion.2), channel_id=1, source_target_pairs={{0,2},{1,7},{2,4},{3,1},{4,6},{5,3},{6,0},{7,5},{8,10},{9,15},{10,... | collective-permute-start | bytes 196616 | tf_op jit(solution)/shard_map/ppermute | solution.py:403
  12.0 0.5 collective-permute-start.2
  12.6 0.6 %collective-permute-start.3 = (f32[128,128]{1,0:T(8,128)S(1)}, f32[128,128]{1,0:T(8,128)S(1)}, u32[]{:S(2)}, u32[]{:S(2)}) collective-permute-start(f32[128,128]{1,0:T(8,128)S(1)} %multiply_add_fusion.2), channel_id=1, source_target_pairs={{0,6},{1,3},{2,0},{3,5},{4,2},{5,7},{6,4},{7,1},{8,14},{9,11},{10,... | collective-permute-start | bytes 196616 | tf_op jit(solution)/shard_map/ppermute | solution.py:403
  13.2 0.0 copy-done.12
  13.2 1.2 %collective-permute-done.1 = f32[128,128]{1,0:T(8,128)S(1)} collective-permute-done((f32[128,128]{1,0:T(8,128)S(1)}, f32[128,128]{1,0:T(8,128)S(1)}, u32[]{:S(2)}, u32[]{:S(2)}) %collective-permute-start.1) | collective-permute-done | bytes 65568 | tf_op jit(solution)/shard_map/ppermute | solution.py:403
  14.4 3.1 %collective-permute-done.2 = f32[128,128]{1,0:T(8,128)S(1)} collective-permute-done((f32[128,128]{1,0:T(8,128)S(1)}, f32[128,128]{1,0:T(8,128)S(1)}, u32[]{:S(2)}, u32[]{:S(2)}) %collective-permute-start.2) | collective-permute-done | bytes 65568 | tf_op jit(solution)/shard_map/ppermute | solution.py:403
  17.5 1.0 %collective-permute-done.3 = f32[128,128]{1,0:T(8,128)S(1)} collective-permute-done((f32[128,128]{1,0:T(8,128)S(1)}, f32[128,128]{1,0:T(8,128)S(1)}, u32[]{:S(2)}, u32[]{:S(2)}) %collective-permute-start.3) | collective-permute-done | bytes 65568 | tf_op jit(solution)/shard_map/ppermute | solution.py:403
  18.5 0.0 copy-done.9
  18.5 0.9 %multiply_add_fusion = (f32[128,128]{1,0:T(8,128)S(1)}, f32[128,128]{1,0:T(8,128)S(1)}) fusion(f32[128,128]{1,0:T(8,128)S(1)} %copy-done.8, f32[128,128]{1,0:T(8,128)} %get-tuple-element.16, pred[128]{0:T(512)(128)(4,1)S(1)} %iota_compare_fusion, f32[128,128]{1,0:T(8,128)S(1)} %collective-permute-done.1, f32[128,128]{1,0:T(8,128)S(1)} %copy-done.9, ...), kind=kLoop, calls=%fused_computation | loop fusion | flops 163840 | bytes 589952 | tf_op jit(solution)/shard_map/add | solution.py:425
  19.5 0.5 collective-permute-start.4
  19.9 0.1 fusion.extra_ref
  20.0 0.8 %collective-permute-done.4.other_ref = f32[128,128]{1,0:T(8,128)S(1)} collective-permute-done((f32[128,128]{1,0:T(8,128)S(1)}, f32[128,128]{1,0:T(8,128)S(1)}, u32[]{:S(2)}, u32[]{:S(2)}) %collective-permute-start.4) | collective-permute-done | bytes 65568 | tf_op jit(solution)/shard_map/ppermute | solution.py:425
  20.8 0.0 copy-done.2
  20.9 1.2 %copy-done.1 = f32[16,128,128]{2,1,0:T(8,128)S(1)} copy-done((f32[16,128,128]{2,1,0:T(8,128)S(1)}, f32[16,128,128]{2,1,0:T(8,128)}, u32[]{:S(2)}) %copy-start.1) | copy-done | bytes 1048600
  22.1 6.8 %moments.1 = f32[1,128]{1,0:T(1,128)S(1)} custom-call(f32[16,128,128]{2,1,0:T(8,128)S(1)} %copy-done, f32[16,128,128]{2,1,0:T(8,128)S(1)} %copy-done.1, f32[128,128]{1,0:T(8,128)S(1)} %mul.22.own_ref, f32[128,128]{1,0:T(8,128)S(1)} %collective-permute-done.4.other_ref, f32[1,128]{1,0:T(1,128)S(1)} %fusion.extra_ref, f32[128,128]{1,0:T(8,128)S(1)} %copy-done.2, ...), custom_call_target="tpu_custom_call" | custom-call | tf_op jit(solution)/shard_map/moments/pallas_call | solution.py:429
  28.9 8.4 %all_to_all.14 = f32[8,1,128]{2,1,0:T(1,128)S(1)} all-to-all(f32[8,1,128]{2,1,0:T(1,128)S(1)} %broadcast_in_dim.16), channel_id=1, replica_groups=mesh['macro'=32,'pencil'=8] {'pencil'}, dimensions={0} | all-to-all | bytes 8192 | tf_op jit(solution)/shard_map/all_to_all | solution.py:452
  37.3 19.4 %all_to_all.15 = f32[32,1,128]{2,1,0:T(1,128)} all-to-all(f32[32,1,128]{2,1,0:T(1,128)S(1)} %broadcast_in_dim.17), channel_id=1, replica_groups=mesh['macro'=32,'pencil'=8] {'macro'}, dimensions={0} | all-to-all | bytes 32768 | tf_op jit(solution)/shard_map/all_to_all | solution.py:453
  56.7 2.2 %close.1 = (f32[1,3]{1,0:T(1,128)}, f32[1,4]{1,0:T(1,128)}) custom-call(f32[32,128]{1,0:T(8,128)} %bitcast.9), custom_call_target="tpu_custom_call" | custom-call | tf_op jit(solution)/shard_map/close/pallas_call | solution.py:454
  (21 shorter events, 0.1 us)
Async XLA Ops:
  0.6 9.7 %copy-start.10 = (f32[128,128]{1,0:T(8,128)S(1)}, f32[128,128]{1,0:T(8,128)}, u32[]{:S(2)}) copy-start(f32[128,128]{1,0:T(8,128)} %constant.32.clone) | copy-start | bytes 196612
  0.6 12.5 %copy-start.12 = (s32[1,8]{1,0:T(1,128)S(1)}, s32[1,8]{1,0:T(1,128)}, u32[]{:S(2)}) copy-start(s32[1,8]{1,0:T(1,128)} %param.22) | copy-start | bytes 100
  0.7 12.5 %copy-start.13 = (s32[4]{0:T(128)S(1)}, s32[4]{0:T(128)}, u32[]{:S(2)}) copy-start(s32[4]{0:T(128)} %param.23) | copy-start | bytes 52
  0.7 17.9 %copy-start.8 = (f32[128,128]{1,0:T(8,128)S(1)}, f32[128,128]{1,0:T(8,128)}, u32[]{:S(2)}) copy-start(f32[128,128]{1,0:T(8,128)} %constant.48) | copy-start | bytes 196612
  0.7 17.9 %copy-start.9 = (f32[128,128]{1,0:T(8,128)S(1)}, f32[128,128]{1,0:T(8,128)}, u32[]{:S(2)}) copy-start(f32[128,128]{1,0:T(8,128)} %constant.33.clone) | copy-start | bytes 196612
  0.7 19.3 %copy-start.11 = (f32[4]{0:T(128)S(1)}, f32[4]{0:T(128)}, u32[]{:S(2)}) copy-start(f32[4]{0:T(128)} %param.21) | copy-start | bytes 52
  0.7 19.3 %copy-start.7 = (f32[128,128]{1,0:T(8,128)S(1)}, f32[128,128]{1,0:T(8,128)}, u32[]{:S(2)}) copy-start(f32[128,128]{1,0:T(8,128)} %constant.34.clone) | copy-start | bytes 196612
  0.7 20.1 %copy-start.2 = (f32[128,128]{1,0:T(8,128)S(1)}, f32[128,128]{1,0:T(8,128)}, u32[]{:S(2)}) copy-start(f32[128,128]{1,0:T(8,128)} %constant.31.clone.rho_hbm.rho_ref) | copy-start | bytes 196612
  0.7 20.1 %copy-start.3 = (bf16[256,256]{1,0:T(8,128)(2,1)S(1)}, bf16[256,256]{1,0:T(8,128)(2,1)}, u32[]{:S(2)}) copy-start(bf16[256,256]{1,0:T(8,128)(2,1)} %constant.35.clone.right_basis_ref) | copy-start | bytes 393220
  0.7 20.1 %copy-start.4 = (bf16[256,256]{1,0:T(8,128)(2,1)S(1)}, bf16[256,256]{1,0:T(8,128)(2,1)}, u32[]{:S(2)}) copy-start(bf16[256,256]{1,0:T(8,128)(2,1)} %constant.36.clone.right_slope_ref) | copy-start | bytes 393220
  0.8 20.1 %copy-start.5 = (bf16[256,256]{1,0:T(8,128)(2,1)S(1)}, bf16[256,256]{1,0:T(8,128)(2,1)}, u32[]{:S(2)}) copy-start(bf16[256,256]{1,0:T(8,128)(2,1)} %constant.37.clone.left_basis_ref) | copy-start | bytes 393220
  0.8 20.1 %copy-start.6 = (bf16[256,256]{1,0:T(8,128)(2,1)S(1)}, bf16[256,256]{1,0:T(8,128)(2,1)}, u32[]{:S(2)}) copy-start(bf16[256,256]{1,0:T(8,128)(2,1)} %constant.38.clone.left_slope_ref) | copy-start | bytes 393220
  5.9 15.0 %copy-start = (f32[16,128,128]{2,1,0:T(8,128)S(1)}, f32[16,128,128]{2,1,0:T(8,128)}, u32[]{:S(2)}) copy-start(f32[16,128,128]{2,1,0:T(8,128)} %get-tuple-element.13.conduct_ref) | copy-start | bytes 3145732
  5.9 4.4 %collective-permute-start = (f32[128,128]{1,0:T(8,128)}, f32[128,128]{1,0:T(8,128)S(1)}, u32[]{:S(2)}, u32[]{:S(2)}) collective-permute-start(f32[128,128]{1,0:T(8,128)} %get-tuple-element.15), channel_id=1, source_target_pairs={{0,1},{1,0},{2,3},{3,2},{4,5},{5,4},{6,7},{7,6},{8,9},{9,8},{10,11... | collective-permute-start | bytes 196616 | tf_op jit(solution)/shard_map/ppermute | solution.py:406
  11.2 3.2 %collective-permute-start.1 = (f32[128,128]{1,0:T(8,128)S(1)}, f32[128,128]{1,0:T(8,128)S(1)}, u32[]{:S(2)}, u32[]{:S(2)}) collective-permute-start(f32[128,128]{1,0:T(8,128)S(1)} %multiply_add_fusion.2), channel_id=1, source_target_pairs={{0,2},{1,7},{2,4},{3,1},{4,6},{5,3},{6,0},{7,5},{8,10},{9,15},{10,... | collective-permute-start | bytes 196616 | tf_op jit(solution)/shard_map/ppermute | solution.py:403
  12.0 5.5 %collective-permute-start.2 = (f32[128,128]{1,0:T(8,128)S(1)}, f32[128,128]{1,0:T(8,128)S(1)}, u32[]{:S(2)}, u32[]{:S(2)}) collective-permute-start(f32[128,128]{1,0:T(8,128)S(1)} %multiply_add_fusion.2), channel_id=1, source_target_pairs={{0,4},{1,5},{2,6},{3,7},{4,0},{5,1},{6,2},{7,3},{8,12},{9,13},{10,... | collective-permute-start | bytes 196616 | tf_op jit(solution)/shard_map/ppermute | solution.py:403
  12.6 6.0 %collective-permute-start.3 = (f32[128,128]{1,0:T(8,128)S(1)}, f32[128,128]{1,0:T(8,128)S(1)}, u32[]{:S(2)}, u32[]{:S(2)}) collective-permute-start(f32[128,128]{1,0:T(8,128)S(1)} %multiply_add_fusion.2), channel_id=1, source_target_pairs={{0,6},{1,3},{2,0},{3,5},{4,2},{5,7},{6,4},{7,1},{8,14},{9,11},{10,... | collective-permute-start | bytes 196616 | tf_op jit(solution)/shard_map/ppermute | solution.py:403
  19.5 1.4 %collective-permute-start.4 = (f32[128,128]{1,0:T(8,128)S(1)}, f32[128,128]{1,0:T(8,128)S(1)}, u32[]{:S(2)}, u32[]{:S(2)}) collective-permute-start(f32[128,128]{1,0:T(8,128)S(1)} %get-tuple-element.24), channel_id=1, source_target_pairs={{0,1},{1,0},{2,3},{3,2},{4,5},{5,4},{6,7},{7,6},{8,9},{9,8},{10,11... | collective-permute-start | bytes 196616 | tf_op jit(solution)/shard_map/ppermute | solution.py:425
  20.9 1.2 %copy-start.1 = (f32[16,128,128]{2,1,0:T(8,128)S(1)}, f32[16,128,128]{2,1,0:T(8,128)}, u32[]{:S(2)}) copy-start(f32[16,128,128]{2,1,0:T(8,128)} %get-tuple-element.14.modes_ref) | copy-start | bytes 3145732

commit v4 on v3

--- a/solution.py
+++ b/solution.py
@@ -137,7 +137,7 @@
     for copy in tables:
         copy.wait()
 
-    def few(piece, carry):
+    def along_z(piece):
         ids_copy(piece).wait()
         fiber_copy(piece).wait()
         planes = []
@@ -155,20 +155,25 @@
             planes.append(beside(conduct))
         conduct_copy(piece).start()
         lines = product(jnp.concatenate(planes, axis=0), right_ref[...])
-        lines = lines[:, :width] + lines[:, width:]
-        norm = norm_ref[...]
+        return lines[:, :width] + lines[:, width:]
+
+    def along_y(piece, lines):
         for part in range(0, group, 2):
             pair = jnp.concatenate(
                 [lines[part * width : (part + 1) * width], lines[(part + 1) * width : (part + 2) * width]], axis=1
             )
             modes = product(left_ref[...], stacked(pair))
             modes = modes[:width] + modes[width:]
-            modes_ref[group * piece + part] = modes[:, :width] * norm
-            modes_ref[group * piece + part + 1] = modes[:, width:] * norm
+            modes_ref[group * piece + part] = modes[:, :width]
+            modes_ref[group * piece + part + 1] = modes[:, width:]
         modes_copy(piece).start()
-        return carry
-
-    lax.fori_loop(0, PIECES, few, 0)
+
+    lines = along_z(0)
+    for piece in range(1, PIECES):
+        ahead = along_z(piece)
+        along_y(piece - 1, lines)
+        lines = ahead
+    along_y(PIECES - 1, lines)
     total = jnp.sum(sums_ref[0])
     total_square = jnp.sum(sums_ref[1])
     rho = rho_ref[...]
@@ -178,8 +183,9 @@
         right = modes_ref[x] + rho * right
         left = modes_ref[slab - 1 - x] + rho * left
     corner = corner_mask(right.shape)
-    right = jnp.where(corner, total, right)
-    left = jnp.where(corner, total_square, left)
+    norm = norm_ref[...]
+    right = jnp.where(corner, total, right * norm)
+    left = jnp.where(corner, total_square, left * norm)
     keep_ref[...] = jnp.where(odd, left, right)
     give_ref[...] = jnp.where(odd, right, left)
     for piece in range(PIECES):
@@ -221,35 +227,49 @@
         potential_ref[x] = here
         rise_ref[x] = here - last
         last = here
+    potential_ref[slab + 1] = last
+    rise_ref[slab + 1] = last
 
     def put(ref, x, plane):
         ref[x, :width] = plane
         ref[x, width:] = plane[:ROWS]
 
-    def along_z(x):
-        along = beside(potential_ref[x])
-        rise = product(beside(rise_ref[x]), right_basis_ref[...])
+    def along_z(pair):
+        planes = [2 * pair, 2 * pair + 1]
+        along = jnp.concatenate([beside(potential_ref[x]) for x in planes], axis=0)
+        rise = product(jnp.concatenate([beside(rise_ref[x]) for x in planes], axis=0), right_basis_ref[...])
         slope = product(along, right_slope_ref[...])
         plain = product(along, right_basis_ref[...])
         for place, lines in enumerate((slope, rise, plain)):
             high, low = halves(lines[:, :width] + lines[:, width:])
-            lanes = pl.ds(place * width, width)
-            lines_ref[:width, lanes] = high
-            lines_ref[width:, lanes] = low
-
-    def along_y(x):
-        both = product(left_basis_ref[...], lines_ref[:, : 2 * width])
-        both = both[:width] + both[width:]
-        third = product(left_slope_ref[...], lines_ref[:, 2 * width :])
+            for part in range(2):
+                rows = slice(part * width, (part + 1) * width)
+                lanes = pl.ds((2 * part + place if place < 2 else 4 + part) * width, width)
+                lines_ref[:width, lanes] = high[rows]
+                lines_ref[width:, lanes] = low[rows]
+
+    def along_y(pair):
+        third = product(left_slope_ref[...], lines_ref[:, 4 * width :])
         third = third[:width] + third[width:]
-        put(pz_ref, x, both[:, :width])
-        put(px_ref, x, both[:, width:])
-        put(py_ref, x, third)
+        for part in range(2):
+            both = product(left_basis_ref[...], lines_ref[:, 2 * part * width : 2 * (part + 1) * width])
+            both = both[:width] + both[width:]
+            put(pz_ref, 2 * pair + part, both[:, :width])
+            put(px_ref, 2 * pair + part, both[:, width:])
+            put(py_ref, 2 * pair + part, third[:, part * width : (part + 1) * width])
+
+    pairs = slab // 2 + 1
+
+    def warm(step, carry):
+        along_y(jnp.maximum(step - 1, 0))
+        along_z(step)
+        return carry
 
     def plane(step, totals):
-        x = jnp.maximum(step - 3, 0)
         totals = list(totals)
-        for chunk in range(width // ROWS):
+        for place in range(2 * (width // ROWS)):
+            x = 2 * (step - 3) + place // (width // ROWS)
+            chunk = place % (width // ROWS)
             at = pl.ds(chunk * ROWS, ROWS)
             down = pl.ds(chunk * ROWS + 1, ROWS)
             conduct = conduct_ref[x, at]
@@ -267,12 +287,13 @@
                     totals[at_entry] = totals[at_entry] + term
                     totals[6 + at_entry] = totals[6 + at_entry] + conduct * term
                     at_entry += 1
-        along_y(jnp.clip(step - 1, 0, slab))
-        along_z(jnp.minimum(step, slab))
-        return tuple(jnp.where(step < 3, 0.0, total) for total in totals)
+        along_y(jnp.minimum(step - 1, pairs - 1))
+        along_z(jnp.minimum(step, pairs - 1))
+        return tuple(totals)
 
     nothing = jnp.zeros((ROWS, width), jnp.float32)
-    totals = lax.fori_loop(0, slab + 3, plane, (nothing,) * 12)
+    lax.fori_loop(0, 3, warm, 0)
+    totals = lax.fori_loop(3, pairs + 2, plane, (nothing,) * 12)
     lines = [jnp.sum(total, axis=0, keepdims=True) for total in totals]
     lines = jnp.concatenate(lines + [jnp.zeros((4, width), jnp.float32)], axis=0)
     column = jnp.sum(lines, axis=1, keepdims=True)
@@ -403,10 +424,12 @@
         return lax.ppermute(array, "pencil", perm)
 
     step, chip_step, scale = tables["step"], tables["chip_step"], tables["scale"]
-    chip = lax.ppermute(give, "pencil", swap) + step * keep
-    chip, temperature, entry, assign, corners = lax.optimization_barrier(
-        (chip, mesh_point_thermal_state, global_entry_position, sample_choice_per_point, element_corner_ids)
-    )
+    chip = lax.ppermute(give, "pencil", swap) + lax.optimization_barrier(step * keep)
+    chip, keep, modes, temperature, entry, assign, corners = lax.optimization_barrier(
+        (chip, keep, modes, mesh_point_thermal_state, global_entry_position, sample_choice_per_point, element_corner_ids)
+    )
+    modes = lax.optimization_barrier(modes * tables["norm"])
+    kept = lax.optimization_barrier(jnp.where(corner_mask((width, width)), 0.0, keep))
     extra = jnp.concatenate(
         [
             temperature,
@@ -421,18 +444,17 @@
     for tail in coming[-2::-1]:
         own = tail + chip_step * own
     own = own * scale
-    corner = corner_mask((width, width))
-    other = lax.ppermute(jnp.where(corner, 0.0, keep) + step * own, "pencil", swap)
-
-    field = (slab + 1, width, width)
-    padded = (slab + 1, width + ROWS, width)
+    other = lax.ppermute(kept + step * own, "pencil", swap)
+
+    field = (slab + 2, width, width)
+    padded = (slab + 2, width + ROWS, width)
     moments = pl.pallas_call(
         moments_kernel,
         out_shape=jax.ShapeDtypeStruct((1, LANES), jnp.float32),
         in_specs=[vmem] * 10,
         out_specs=vmem,
         scratch_shapes=[pltpu.VMEM(s, jnp.float32) for s in (field, field, padded, padded, padded)]
-        + [pltpu.VMEM((2 * width, 3 * width), jnp.bfloat16)],
+        + [pltpu.VMEM((2 * width, 6 * width), jnp.bfloat16)],
         compiler_params=params,
         name="moments",
     )(

time: 59.3 us -> 55.2 us (0.931)
  waiting for transfers between devices: 6.61 us -> 3.08 us
  Pallas kernels: 14.1 us -> 12.8 us
    ppermute x3, waiting for transfers between devices: 5.36 us -> 2.41 us  [from_chip(): return lax.ppermute(array, 'pencil', perm)]
    mul x0 -> x2, other arithmetic: none -> 2.15 us  [the longest x1 1.3 us: on_device(): modes = lax.optimization_barrier(modes * tables['norm'])]
    add x2, other arithmetic: 1.78 us -> 0.05 us  [the longest x1 0.04 us: on_device(): other = lax.ppermute(kept + step * own, 'pencil', swap)]
    pallas_call x1, Pallas kernels: 5.12 us -> 4.47 us  [on_device(): pl.pallas_call(analyse_kernel, out_shape=(block, block, plane, plane), in...]
    pallas_call x1, Pallas kernels: 6.77 us -> 6.13 us  [on_device(): pl.pallas_call(moments_kernel, out_shape=jax.ShapeDtypeStruct((1, LANES),...]
    unnamed x28 -> x30, local copies, waits for them, and re-layouts: 1.3 us -> 1.65 us
  transfers between devices with their start and end apart: 5 -> 5, of which waited for: 5 -> 3; matrix products, arithmetic and copies ran while one was open for 0% -> 4% of each run, Pallas kernels for 0% -> 0%
where the time goes in v4:
time: 55.2 us; the launch traced here: 54.7 us
  blocking collectives  27.7 us (50%)
  Pallas kernels  12.8 us (23%)
  starting transfers between devices  5.62 us (10%)
  waiting for transfers between devices  3.08 us (6%)
  other arithmetic  2.4 us (4%)
  local copies, waits for them, and re-layouts  1.67 us (3%)
  between operations  1.46 us (3%)
    all_to_all x1, blocking collectives, on_device(): lax.all_to_all(jnp.broadcast_to(table, (groups, LANES)), 'macro', 0, 0, t...  19.2 us
    all_to_all x1, blocking collectives, on_device(): lax.all_to_all(table, 'pencil', 0, 0, tiled=True)  8.45 us
    pallas_call x1, Pallas kernels, on_device(): pl.pallas_call(moments_kernel, out_shape=jax.ShapeDtypeStruct((1, LANES),...  6.13 us
    pallas_call x1, Pallas kernels, on_device(): pl.pallas_call(analyse_kernel, out_shape=(block, block, plane, plane), in...  4.47 us
    ppermute x1, starting transfers between devices, on_device(): lax.ppermute(give, 'pencil', swap) + lax.optimization_barrier(step * keep)  3.33 us
    ppermute x3, waiting for transfers between devices, from_chip(): return lax.ppermute(array, 'pencil', perm)  2.41 us
    pallas_call x1, Pallas kernels, on_device(): pl.pallas_call(lambda *refs: close_kernel(own_nodes, volume, *refs), out_...  2.24 us
    ppermute x3, starting transfers between devices, from_chip(): return lax.ppermute(array, 'pencil', perm)  1.94 us
  transfers between devices with their start and end apart: 5, of which 3 were waited for; matrix products, arithmetic and copies ran while one was open for 4% of the time, Pallas kernels for 0%

profile of v4, /device:TPU:1, one launch (start us, length us, event | category | flops | bytes accessed | tf_op | source)
XLA Modules:
  0.0 54.7 jit_solution(8228064789930721272)
XLA Ops:
  0.6 0.0 copy-start.11
  0.6 4.5 %analyse.1 = (f32[16,128,128]{2,1,0:T(8,128)}, f32[16,128,128]{2,1,0:T(8,128)}, f32[128,128]{1,0:T(8,128)}, f32[128,128]{1,0:T(8,128)}) custom-call(f32[1,3]{1,0:T(1,128)} %material_hbm.1, s32[1,16,128,128]{3,2,1,0:T(8,128)} %ids_hbm.1, f32[1,16,128,128]{3,2,1,0:T(8,128)} %fiber_hbm.1, bf16[256,256]{1,0:T(8,128)(2,1)} %constant.28.clone.right_hbm, ...), custom_call_target="tpu_custom_call" | custom-call | tf_op jit(solution)/shard_map/analyse/pallas_call | solution.py:386
  5.1 3.3 %collective-permute-start = (f32[128,128]{1,0:T(8,128)}, f32[128,128]{1,0:T(8,128)S(1)}, u32[]{:S(2)}, u32[]{:S(2)}) collective-permute-start(f32[128,128]{1,0:T(8,128)} %get-tuple-element.16), channel_id=1, source_target_pairs={{0,1},{1,0},{2,3},{3,2},{4,5},{5,4},{6,7},{7,6},{8,9},{9,8},{10,11... | collective-permute-start | bytes 196616 | tf_op jit(solution)/shard_map/ppermute | solution.py:427
  8.5 0.8 %mul.26 = f32[128,128]{1,0:T(8,128)S(1)} multiply(f32[128,128]{1,0:T(8,128)S(1)} %copy-done.11, f32[128,128]{1,0:T(8,128)} %get-tuple-element.21) | non-fusion elementwise | flops 16384 | bytes 196608 | tf_op jit(solution)/shard_map/mul | solution.py:427
  10.0 0.0 copy-start.6
  10.0 0.0 collective-permute-done
  10.0 0.8 %collective-permute-start.1 = (f32[128,128]{1,0:T(8,128)S(1)}, f32[128,128]{1,0:T(8,128)S(1)}, u32[]{:S(2)}, u32[]{:S(2)}) collective-permute-start(f32[128,128]{1,0:T(8,128)S(1)} %add.17), channel_id=1, source_target_pairs={{0,2},{1,7},{2,4},{3,1},{4,6},{5,3},{6,0},{7,5},{8,10},{9,15},{10,... | collective-permute-start | bytes 196616 | tf_op jit(solution)/shard_map/ppermute | solution.py:424
  10.8 0.5 collective-permute-start.2
  11.4 0.6 %collective-permute-start.3 = (f32[128,128]{1,0:T(8,128)S(1)}, f32[128,128]{1,0:T(8,128)S(1)}, u32[]{:S(2)}, u32[]{:S(2)}) collective-permute-start(f32[128,128]{1,0:T(8,128)S(1)} %add.17), channel_id=1, source_target_pairs={{0,6},{1,3},{2,0},{3,5},{4,2},{5,7},{6,4},{7,1},{8,14},{9,11},{10,... | collective-permute-start | bytes 196616 | tf_op jit(solution)/shard_map/ppermute | solution.py:424
  12.0 0.0 copy-done.6
  12.0 1.3 %broadcast_multiply_fusion.modes_ref = f32[16,128,128]{2,1,0:T(8,128)S(1)} fusion(f32[16,128,128]{2,1,0:T(8,128)} %get-tuple-element.19, f32[128,128]{1,0:T(8,128)S(1)} %copy-done.6), kind=kLoop, calls=%fused_computation | loop fusion | flops 262144 | bytes 2162688 | tf_op jit(solution)/shard_map/mul | solution.py:431
  13.3 0.0 copy-start.13
  13.3 0.0 copy-start.9
  13.3 0.0 copy-start.10
  13.3 0.1 and_select_fusion
  13.4 0.5 copy-done.13
  14.0 0.7 %copy-done.14 = s32[4]{0:T(128)S(1)} copy-done((s32[4]{0:T(128)S(1)}, s32[4]{0:T(128)}, u32[]{:S(2)}) %copy-start.14) | copy-done | bytes 40
  14.6 0.0 collective-permute-done.1
  14.6 1.6 %collective-permute-done.2 = f32[128,128]{1,0:T(8,128)S(1)} collective-permute-done((f32[128,128]{1,0:T(8,128)S(1)}, f32[128,128]{1,0:T(8,128)S(1)}, u32[]{:S(2)}, u32[]{:S(2)}) %collective-permute-start.2) | collective-permute-done | bytes 65568 | tf_op jit(solution)/shard_map/ppermute | solution.py:424
  16.2 0.8 %collective-permute-done.3 = f32[128,128]{1,0:T(8,128)S(1)} collective-permute-done((f32[128,128]{1,0:T(8,128)S(1)}, f32[128,128]{1,0:T(8,128)S(1)}, u32[]{:S(2)}, u32[]{:S(2)}) %collective-permute-start.3) | collective-permute-done | bytes 65568 | tf_op jit(solution)/shard_map/ppermute | solution.py:424
  17.0 0.0 copy-start.4
  17.0 0.0 copy-start.5
  17.1 0.0 copy-start.2
  17.1 0.3 collective-permute-start.4
  17.5 0.2 copy-done.12
  17.7 0.1 fusion.extra_ref
  17.8 0.7 %collective-permute-done.4.other_ref = f32[128,128]{1,0:T(8,128)S(1)} collective-permute-done((f32[128,128]{1,0:T(8,128)S(1)}, f32[128,128]{1,0:T(8,128)S(1)}, u32[]{:S(2)}, u32[]{:S(2)}) %collective-permute-start.4) | collective-permute-done | bytes 65568 | tf_op jit(solution)/shard_map/ppermute | solution.py:447
  18.5 0.2 copy-done.1
  18.7 6.1 %moments.1 = f32[1,128]{1,0:T(1,128)S(1)} custom-call(f32[16,128,128]{2,1,0:T(8,128)S(1)} %copy-done, f32[16,128,128]{2,1,0:T(8,128)S(1)} %broadcast_multiply_fusion.modes_ref, f32[128,128]{1,0:T(8,128)S(1)} %mul.32.own_ref, f32[128,128]{1,0:T(8,128)S(1)} %collective-permute-done.4.other_ref, f32[1,128]{1,0:T(1,128)S(1)} %fusion.extra_ref, ...), custom_call_target="tpu_custom_call" | custom-call | tf_op jit(solution)/shard_map/moments/pallas_call | solution.py:451
  24.8 8.4 %all_to_all.14 = f32[8,1,128]{2,1,0:T(1,128)S(1)} all-to-all(f32[8,1,128]{2,1,0:T(1,128)S(1)} %broadcast_in_dim.9), channel_id=1, replica_groups=mesh['macro'=32,'pencil'=8] {'pencil'}, dimensions={0} | all-to-all | bytes 8192 | tf_op jit(solution)/shard_map/all_to_all | solution.py:474
  33.3 19.2 %all_to_all.15 = f32[32,1,128]{2,1,0:T(1,128)} all-to-all(f32[32,1,128]{2,1,0:T(1,128)S(1)} %broadcast_in_dim.18), channel_id=1, replica_groups=mesh['macro'=32,'pencil'=8] {'macro'}, dimensions={0} | all-to-all | bytes 32768 | tf_op jit(solution)/shard_map/all_to_all | solution.py:475
  52.5 2.2 %close.1 = (f32[1,3]{1,0:T(1,128)}, f32[1,4]{1,0:T(1,128)}) custom-call(f32[32,128]{1,0:T(8,128)} %bitcast.9), custom_call_target="tpu_custom_call" | custom-call | tf_op jit(solution)/shard_map/close/pallas_call | solution.py:476
  (26 shorter events, 0.1 us)
Async XLA Ops:
  0.6 7.8 %copy-start.11 = (f32[128,128]{1,0:T(8,128)S(1)}, f32[128,128]{1,0:T(8,128)}, u32[]{:S(2)}) copy-start(f32[128,128]{1,0:T(8,128)} %constant.32.clone) | copy-start | bytes 196612
  5.1 4.9 %collective-permute-start = (f32[128,128]{1,0:T(8,128)}, f32[128,128]{1,0:T(8,128)S(1)}, u32[]{:S(2)}, u32[]{:S(2)}) collective-permute-start(f32[128,128]{1,0:T(8,128)} %get-tuple-element.16), channel_id=1, source_target_pairs={{0,1},{1,0},{2,3},{3,2},{4,5},{5,4},{6,7},{7,6},{8,9},{9,8},{10,11... | collective-permute-start | bytes 196616 | tf_op jit(solution)/shard_map/ppermute | solution.py:427
  10.0 2.0 %copy-start.6 = (f32[128,128]{1,0:T(8,128)S(1)}, f32[128,128]{1,0:T(8,128)}, u32[]{:S(2)}) copy-start(f32[128,128]{1,0:T(8,128)} %constant.30.clone.norm_hbm) | copy-start | bytes 196612
  10.0 3.3 %copy-start.7 = (f32[128,128]{1,0:T(8,128)S(1)}, f32[128,128]{1,0:T(8,128)}, u32[]{:S(2)}) copy-start(f32[128,128]{1,0:T(8,128)} %get-tuple-element.21) | copy-start | bytes 196612
  10.0 8.4 %copy-start = (f32[16,128,128]{2,1,0:T(8,128)S(1)}, f32[16,128,128]{2,1,0:T(8,128)}, u32[]{:S(2)}) copy-start(f32[16,128,128]{2,1,0:T(8,128)} %get-tuple-element.15.conduct_ref) | copy-start | bytes 3145732
  10.0 4.6 %collective-permute-start.1 = (f32[128,128]{1,0:T(8,128)S(1)}, f32[128,128]{1,0:T(8,128)S(1)}, u32[]{:S(2)}, u32[]{:S(2)}) collective-permute-start(f32[128,128]{1,0:T(8,128)S(1)} %add.17), channel_id=1, source_target_pairs={{0,2},{1,7},{2,4},{3,1},{4,6},{5,3},{6,0},{7,5},{8,10},{9,15},{10,... | collective-permute-start | bytes 196616 | tf_op jit(solution)/shard_map/ppermute | solution.py:424
  10.8 5.4 %collective-permute-start.2 = (f32[128,128]{1,0:T(8,128)S(1)}, f32[128,128]{1,0:T(8,128)S(1)}, u32[]{:S(2)}, u32[]{:S(2)}) collective-permute-start(f32[128,128]{1,0:T(8,128)S(1)} %add.17), channel_id=1, source_target_pairs={{0,4},{1,5},{2,6},{3,7},{4,0},{5,1},{6,2},{7,3},{8,12},{9,13},{10,... | collective-permute-start | bytes 196616 | tf_op jit(solution)/shard_map/ppermute | solution.py:424
  11.4 5.7 %collective-permute-start.3 = (f32[128,128]{1,0:T(8,128)S(1)}, f32[128,128]{1,0:T(8,128)S(1)}, u32[]{:S(2)}, u32[]{:S(2)}) collective-permute-start(f32[128,128]{1,0:T(8,128)S(1)} %add.17), channel_id=1, source_target_pairs={{0,6},{1,3},{2,0},{3,5},{4,2},{5,7},{6,4},{7,1},{8,14},{9,11},{10,... | collective-permute-start | bytes 196616 | tf_op jit(solution)/shard_map/ppermute | solution.py:424
  13.3 0.7 %copy-start.13 = (s32[1,8]{1,0:T(1,128)S(1)}, s32[1,8]{1,0:T(1,128)}, u32[]{:S(2)}) copy-start(s32[1,8]{1,0:T(1,128)} %param.22) | copy-start | bytes 100
  13.3 3.7 %copy-start.9 = (f32[128,128]{1,0:T(8,128)S(1)}, f32[128,128]{1,0:T(8,128)}, u32[]{:S(2)}) copy-start(f32[128,128]{1,0:T(8,128)} %constant.48) | copy-start | bytes 196612
  13.3 3.7 %copy-start.10 = (f32[128,128]{1,0:T(8,128)S(1)}, f32[128,128]{1,0:T(8,128)}, u32[]{:S(2)}) copy-start(f32[128,128]{1,0:T(8,128)} %constant.33.clone) | copy-start | bytes 196612
  14.0 0.7 %copy-start.14 = (s32[4]{0:T(128)S(1)}, s32[4]{0:T(128)}, u32[]{:S(2)}) copy-start(s32[4]{0:T(128)} %param.23) | copy-start | bytes 52
  14.6 3.2 %copy-start.8 = (f32[128,128]{1,0:T(8,128)S(1)}, f32[128,128]{1,0:T(8,128)}, u32[]{:S(2)}) copy-start(f32[128,128]{1,0:T(8,128)} %constant.34.clone) | copy-start | bytes 196612
  17.0 0.7 %copy-start.12 = (f32[4]{0:T(128)S(1)}, f32[4]{0:T(128)}, u32[]{:S(2)}) copy-start(f32[4]{0:T(128)} %param.21) | copy-start | bytes 52
  17.0 1.4 %copy-start.3 = (bf16[256,256]{1,0:T(8,128)(2,1)S(1)}, bf16[256,256]{1,0:T(8,128)(2,1)}, u32[]{:S(2)}) copy-start(bf16[256,256]{1,0:T(8,128)(2,1)} %constant.36.clone.right_slope_ref) | copy-start | bytes 393220
  17.0 1.4 %copy-start.4 = (bf16[256,256]{1,0:T(8,128)(2,1)S(1)}, bf16[256,256]{1,0:T(8,128)(2,1)}, u32[]{:S(2)}) copy-start(bf16[256,256]{1,0:T(8,128)(2,1)} %constant.37.clone.left_basis_ref) | copy-start | bytes 393220
  17.0 1.4 %copy-start.5 = (bf16[256,256]{1,0:T(8,128)(2,1)S(1)}, bf16[256,256]{1,0:T(8,128)(2,1)}, u32[]{:S(2)}) copy-start(bf16[256,256]{1,0:T(8,128)(2,1)} %constant.38.clone.left_slope_ref) | copy-start | bytes 393220
  17.1 1.4 %copy-start.2 = (bf16[256,256]{1,0:T(8,128)(2,1)S(1)}, bf16[256,256]{1,0:T(8,128)(2,1)}, u32[]{:S(2)}) copy-start(bf16[256,256]{1,0:T(8,128)(2,1)} %constant.35.clone.right_basis_ref) | copy-start | bytes 393220
  17.1 1.3 %collective-permute-start.4 = (f32[128,128]{1,0:T(8,128)S(1)}, f32[128,128]{1,0:T(8,128)S(1)}, u32[]{:S(2)}, u32[]{:S(2)}) collective-permute-start(f32[128,128]{1,0:T(8,128)S(1)} %get-tuple-element.28), channel_id=1, source_target_pairs={{0,1},{1,0},{2,3},{3,2},{4,5},{5,4},{6,7},{7,6},{8,9},{9,8},{10,11... | collective-permute-start | bytes 196616 | tf_op jit(solution)/shard_map/ppermute | solution.py:447
  17.8 0.9 %copy-start.1 = (f32[128,128]{1,0:T(8,128)S(1)}, f32[128,128]{1,0:T(8,128)}, u32[]{:S(2)}) copy-start(f32[128,128]{1,0:T(8,128)} %constant.31.clone.rho_hbm.rho_ref) | copy-start | bytes 196612

commit v5 on v4

--- a/solution.py
+++ b/solution.py
@@ -15,8 +15,6 @@
 PIECES = 4
 VMEM_BYTES = 48 * 1024 * 1024
 HBM_INPUTS_BYTES = 56 * 1024 * 1024
-
-HIGHEST = lax.Precision.HIGHEST
 
 
 def split_table(table):
@@ -89,9 +87,9 @@
 
 def analyse_kernel(
     material_hbm, ids_hbm, fiber_hbm, right_hbm, left_hbm, norm_hbm, rho_hbm,
-    conduct_hbm, modes_hbm, keep_ref, give_ref,
-    conduct_ref, modes_ref, sums_ref, material_ref, ids_ref, fiber_ref, right_ref, left_ref, norm_ref, rho_ref,
-    table_sems, ids_sems, fiber_sems, conduct_sems, modes_sems,
+    conduct_hbm, modes_hbm, keep_hbm, give_hbm,
+    conduct_ref, modes_ref, keep_ref, give_ref, sums_ref, material_ref, ids_ref, fiber_ref, right_ref, left_ref, norm_ref, rho_ref,
+    table_sems, ids_sems, fiber_sems, conduct_sems, modes_sems, tail_sems,
 ):
     slab, width = fiber_ref.shape[0], fiber_ref.shape[2]
     group = slab // PIECES
@@ -186,8 +184,16 @@
     norm = norm_ref[...]
     right = jnp.where(corner, total, right * norm)
     left = jnp.where(corner, total_square, left * norm)
+    tails = [
+        pltpu.make_async_copy(give_ref, give_hbm, tail_sems.at[0]),
+        pltpu.make_async_copy(keep_ref, keep_hbm, tail_sems.at[1]),
+    ]
+    give_ref[...] = jnp.where(odd, right, left)
+    tails[0].start()
     keep_ref[...] = jnp.where(odd, left, right)
-    give_ref[...] = jnp.where(odd, right, left)
+    tails[1].start()
+    for copy in tails:
+        copy.wait()
     for piece in range(PIECES):
         conduct_copy(piece).wait()
         modes_copy(piece).wait()
@@ -260,12 +266,16 @@
 
     pairs = slab // 2 + 1
 
-    def warm(step, carry):
-        along_y(jnp.maximum(step - 1, 0))
+    def lines_only(step, carry):
         along_z(step)
         return carry
 
-    def plane(step, totals):
+    def warm(step, carry):
+        along_y(step - 1)
+        along_z(step)
+        return carry
+
+    def plane(step, totals, products=2):
         totals = list(totals)
         for place in range(2 * (width // ROWS)):
             x = 2 * (step - 3) + place // (width // ROWS)
@@ -287,13 +297,18 @@
                     totals[at_entry] = totals[at_entry] + term
                     totals[6 + at_entry] = totals[6 + at_entry] + conduct * term
                     at_entry += 1
-        along_y(jnp.minimum(step - 1, pairs - 1))
-        along_z(jnp.minimum(step, pairs - 1))
+        if products > 0:
+            along_y(step - 1)
+        if products > 1:
+            along_z(step)
         return tuple(totals)
 
     nothing = jnp.zeros((ROWS, width), jnp.float32)
-    lax.fori_loop(0, 3, warm, 0)
-    totals = lax.fori_loop(3, pairs + 2, plane, (nothing,) * 12)
+    lax.fori_loop(0, 1, lines_only, 0)
+    lax.fori_loop(1, 3, warm, 0)
+    totals = lax.fori_loop(3, pairs, plane, (nothing,) * 12)
+    totals = lax.fori_loop(pairs, pairs + 1, lambda step, t: plane(step, t, 1), totals)
+    totals = lax.fori_loop(pairs + 1, pairs + 2, lambda step, t: plane(step, t, 0), totals)
     lines = [jnp.sum(total, axis=0, keepdims=True) for total in totals]
     lines = jnp.concatenate(lines + [jnp.zeros((4, width), jnp.float32)], axis=0)
     column = jnp.sum(lines, axis=1, keepdims=True)
@@ -334,7 +349,10 @@
     chosen = jnp.where(
         lax.broadcasted_iota(jnp.int32, (points, points), 1).astype(jnp.float32) == assign, 1.0, 0.0
     )
-    moments = jnp.dot(chosen, table, precision=HIGHEST, preferred_element_type=jnp.float32) / volume
+    high, rest = halves(table)
+    low = (table - high.astype(jnp.float32) - rest.astype(jnp.float32)).astype(jnp.bfloat16)
+    picked = product(chosen.astype(jnp.bfloat16), jnp.concatenate([high, rest, low], axis=1))
+    moments = (picked[:, :LANES] + (picked[:, LANES : 2 * LANES] + picked[:, 2 * LANES :])) * (1.0 / volume)
     moment = lambda index: moments[:, index : index + 1]
     mean, mean_square = moment(12), moment(13)
     radiative = heat * heat * heat
@@ -387,10 +405,12 @@
         analyse_kernel,
         out_shape=(block, block, plane, plane),
         in_specs=[hbm] * 7,
-        out_specs=(hbm, hbm, vmem, vmem),
+        out_specs=(hbm,) * 4,
         scratch_shapes=[
             pltpu.VMEM((slab, width, width), jnp.float32),
             pltpu.VMEM((slab, width, width), jnp.float32),
+            pltpu.VMEM((width, width), jnp.float32),
+            pltpu.VMEM((width, width), jnp.float32),
             pltpu.VMEM((2, ROWS, width), jnp.float32),
             pltpu.SMEM((1, PHASES), jnp.float32),
             pltpu.VMEM((slab, width, width), jnp.int32),
@@ -404,6 +424,7 @@
             pltpu.SemaphoreType.DMA((PIECES,)),
             pltpu.SemaphoreType.DMA((PIECES,)),
             pltpu.SemaphoreType.DMA((PIECES,)),
+            pltpu.SemaphoreType.DMA((2,)),
         ],
         compiler_params=pltpu.CompilerParams(vmem_limit_bytes=HBM_INPUTS_BYTES),
         name="analyse",
@@ -423,7 +444,7 @@
         perm = [(i, (i + (2 * away if i % 2 == 0 else -2 * away)) % pencils) for i in range(pencils)]
         return lax.ppermute(array, "pencil", perm)
 
-    step, chip_step, scale = tables["step"], tables["chip_step"], tables["scale"]
+    step, chip_step = tables["step"], tables["chip_step"]
     chip = lax.ppermute(give, "pencil", swap) + lax.optimization_barrier(step * keep)
     chip, keep, modes, temperature, entry, assign, corners = lax.optimization_barrier(
         (chip, keep, modes, mesh_point_thermal_state, global_entry_position, sample_choice_per_point, element_corner_ids)
@@ -439,11 +460,14 @@
         ]
     )
     extra = jnp.pad(extra, (16, LANES - 16 - extra.shape[0])).reshape(1, LANES)
-    coming = [from_chip(chip, away) for away in range(1, chips)] + [chip]
-    own = coming[-1]
-    for tail in coming[-2::-1]:
-        own = tail + chip_step * own
-    own = own * scale
+    half = chips // 2
+    powers = [tables["scale"], tables["scale"] * chip_step]
+    while len(powers) < chips:
+        powers.append(powers[-1] * chip_step)
+    own = lax.optimization_barrier(powers[half - 1] * from_chip(chip, half) + powers[-1] * chip)
+    for away in range(1, chips):
+        if away != half:
+            own = own + powers[away - 1] * from_chip(chip, away)
     other = lax.ppermute(kept + step * own, "pencil", swap)
 
     field = (slab + 2, width, width)

time: 55.2 us -> 53.1 us (0.962)
  starting transfers between devices: 5.62 us -> 8.08 us
  local copies, waits for them, and re-layouts: 1.67 us -> 0.11 us
  Pallas kernels: 12.8 us -> 11.6 us
  waiting for transfers between devices: 3.08 us -> 1.93 us
  blocking collectives: 27.7 us -> 26.9 us
    unnamed x30 -> x32, local copies, waits for them, and re-layouts: 1.65 us -> 0.09 us
    ppermute x3, waiting for transfers between devices: 2.41 us -> 1.11 us  [from_chip(): return lax.ppermute(array, 'pencil', perm)]
    ppermute x1, starting transfers between devices: 0.35 us -> 1.61 us  [on_device(): other = lax.ppermute(kept + step * own, 'pencil', swap)]
    ppermute x3, starting transfers between devices: 1.94 us -> 3.15 us  [from_chip(): return lax.ppermute(array, 'pencil', perm)]
    all_to_all x1, blocking collectives: 8.45 us -> 7.47 us  [on_device(): lax.all_to_all(table, 'pencil', 0, 0, tiled=True)]
    pallas_call x1, Pallas kernels: 6.13 us -> 5.42 us  [on_device(): pl.pallas_call(moments_kernel, out_shape=jax.ShapeDtypeStruct((1, LANES),...]
    pallas_call x1, Pallas kernels: 4.47 us -> 3.88 us  [on_device(): pl.pallas_call(analyse_kernel, out_shape=(block, block, plane, plane), in...]
  transfers between devices with their start and end apart: 5 -> 5, of which waited for: 3 -> 3; matrix products, arithmetic and copies ran while one was open for 4% -> 5% of each run, Pallas kernels for 0% -> 0%
where the time goes in v5:
time: 53.1 us; the launch traced here: 52.8 us
  blocking collectives  26.9 us (51%)
  Pallas kernels  11.6 us (22%)
  starting transfers between devices  8.08 us (15%)
  other arithmetic  2.57 us (5%)
  waiting for transfers between devices  1.93 us (4%)
  between operations  1.55 us (3%)
    all_to_all x1, blocking collectives, on_device(): lax.all_to_all(jnp.broadcast_to(table, (groups, LANES)), 'macro', 0, 0, t...  19.5 us
    all_to_all x1, blocking collectives, on_device(): lax.all_to_all(table, 'pencil', 0, 0, tiled=True)  7.47 us
    pallas_call x1, Pallas kernels, on_device(): pl.pallas_call(moments_kernel, out_shape=jax.ShapeDtypeStruct((1, LANES),...  5.42 us
    pallas_call x1, Pallas kernels, on_device(): pl.pallas_call(analyse_kernel, out_shape=(block, block, plane, plane), in...  3.88 us
    ppermute x1, starting transfers between devices, on_device(): lax.ppermute(give, 'pencil', swap) + lax.optimization_barrier(step * keep)  3.32 us
    ppermute x3, starting transfers between devices, from_chip(): return lax.ppermute(array, 'pencil', perm)  3.15 us
    pallas_call x1, Pallas kernels, on_device(): pl.pallas_call(lambda *refs: close_kernel(own_nodes, volume, *refs), out_...  2.29 us
    ppermute x1, starting transfers between devices, on_device(): other = lax.ppermute(kept + step * own, 'pencil', swap)  1.61 us
  transfers between devices with their start and end apart: 5, of which 3 were waited for; matrix products, arithmetic and copies ran while one was open for 5% of the time, Pallas kernels for 0%

profile of v5, /device:TPU:1, one launch (start us, length us, event | category | flops | bytes accessed | tf_op | source)
XLA Modules:
  0.0 52.8 jit_solution(15219228572267213644)
XLA Ops:
  0.6 0.0 copy-start.6
  0.6 3.9 %analyse.1 = (f32[16,128,128]{2,1,0:T(8,128)}, f32[16,128,128]{2,1,0:T(8,128)}, f32[128,128]{1,0:T(8,128)}, f32[128,128]{1,0:T(8,128)}) custom-call(f32[1,3]{1,0:T(1,128)} %material_hbm.1, s32[1,16,128,128]{3,2,1,0:T(8,128)} %ids_hbm.1, f32[1,16,128,128]{3,2,1,0:T(8,128)} %fiber_hbm.1, bf16[256,256]{1,0:T(8,128)(2,1)} %constant.32.clone.right_hbm, ...), custom_call_target="tpu_custom_call" | custom-call | tf_op jit(solution)/shard_map/analyse/pallas_call | solution.py:404
  4.5 3.3 %collective-permute-start = (f32[128,128]{1,0:T(8,128)}, f32[128,128]{1,0:T(8,128)S(1)}, u32[]{:S(2)}, u32[]{:S(2)}) collective-permute-start(f32[128,128]{1,0:T(8,128)} %get-tuple-element.16), channel_id=1, source_target_pairs={{0,1},{1,0},{2,3},{3,2},{4,5},{5,4},{6,7},{7,6},{8,9},{9,8},{10,11... | collective-permute-start | bytes 196616 | tf_op jit(solution)/shard_map/ppermute | solution.py:448
  7.9 0.0 copy-done.6
  7.9 0.8 %mul.26 = f32[128,128]{1,0:T(8,128)S(1)} multiply(f32[128,128]{1,0:T(8,128)S(1)} %copy-done.6, f32[128,128]{1,0:T(8,128)} %get-tuple-element.21) | non-fusion elementwise | flops 16384 | bytes 196608 | tf_op jit(solution)/shard_map/mul | solution.py:448
  9.4 0.0 copy-start.7
  9.4 0.0 collective-permute-done
  9.4 0.1 collective-permute-start.3
  9.5 1.9 %collective-permute-start.1 = (f32[128,128]{1,0:T(8,128)S(1)}, f32[128,128]{1,0:T(8,128)S(1)}, u32[]{:S(2)}, u32[]{:S(2)}) collective-permute-start(f32[128,128]{1,0:T(8,128)S(1)} %add.17), channel_id=1, source_target_pairs={{0,4},{1,5},{2,6},{3,7},{4,0},{5,1},{6,2},{7,3},{8,12},{9,13},{10,... | collective-permute-start | bytes 196616 | tf_op jit(solution)/shard_map/ppermute | solution.py:445
  11.4 1.2 %collective-permute-start.2 = (f32[128,128]{1,0:T(8,128)S(1)}, f32[128,128]{1,0:T(8,128)S(1)}, u32[]{:S(2)}, u32[]{:S(2)}) collective-permute-start(f32[128,128]{1,0:T(8,128)S(1)} %add.17), channel_id=1, source_target_pairs={{0,2},{1,7},{2,4},{3,1},{4,6},{5,3},{6,0},{7,5},{8,10},{9,15},{10,... | collective-permute-start | bytes 196616 | tf_op jit(solution)/shard_map/ppermute | solution.py:445
  12.6 0.0 copy-start.12
  12.6 0.0 copy-start.9
  12.6 0.0 copy-start.10
  12.6 0.0 copy-start.1
  12.6 0.0 copy-start.2
  12.7 0.0 copy-start.3
  12.7 0.0 copy-start.4
  12.7 0.0 copy-start.5
  12.7 1.5 %broadcast_multiply_fusion.modes_ref = f32[16,128,128]{2,1,0:T(8,128)S(1)} fusion(f32[16,128,128]{2,1,0:T(8,128)} %get-tuple-element.19, f32[128,128]{1,0:T(8,128)S(1)} %copy-done.7), kind=kLoop, calls=%fused_computation | loop fusion | flops 262144 | bytes 2162688 | tf_op jit(solution)/shard_map/mul | solution.py:452
  14.2 0.0 copy-done.8
  14.2 0.1 and_select_fusion
  14.3 0.0 collective-permute-done.1
  14.4 0.1 collective-permute-done.3
  14.5 1.0 %collective-permute-done.2 = f32[128,128]{1,0:T(8,128)S(1)} collective-permute-done((f32[128,128]{1,0:T(8,128)S(1)}, f32[128,128]{1,0:T(8,128)S(1)}, u32[]{:S(2)}, u32[]{:S(2)}) %collective-permute-start.2) | collective-permute-done | bytes 65568 | tf_op jit(solution)/shard_map/ppermute | solution.py:445
  15.5 0.0 copy-start.13
  15.5 1.6 %collective-permute-start.4 = (f32[128,128]{1,0:T(8,128)S(1)}, f32[128,128]{1,0:T(8,128)S(1)}, u32[]{:S(2)}, u32[]{:S(2)}) collective-permute-start(f32[128,128]{1,0:T(8,128)S(1)} %get-tuple-element.28), channel_id=1, source_target_pairs={{0,1},{1,0},{2,3},{3,2},{4,5},{5,4},{6,7},{7,6},{8,9},{9,8},{10,11... | collective-permute-start | bytes 196616 | tf_op jit(solution)/shard_map/ppermute | solution.py:471
  17.2 0.1 fusion.extra_ref
  17.2 0.8 %collective-permute-done.4.other_ref = f32[128,128]{1,0:T(8,128)S(1)} collective-permute-done((f32[128,128]{1,0:T(8,128)S(1)}, f32[128,128]{1,0:T(8,128)S(1)}, u32[]{:S(2)}, u32[]{:S(2)}) %collective-permute-start.4) | collective-permute-done | bytes 65568 | tf_op jit(solution)/shard_map/ppermute | solution.py:471
  18.1 5.4 %moments.1 = f32[1,128]{1,0:T(1,128)S(1)} custom-call(f32[16,128,128]{2,1,0:T(8,128)S(1)} %copy-done, f32[16,128,128]{2,1,0:T(8,128)S(1)} %broadcast_multiply_fusion.modes_ref, f32[128,128]{1,0:T(8,128)S(1)} %get-tuple-element.29.own_ref, f32[128,128]{1,0:T(8,128)S(1)} %collective-permute-done.4.other_ref, f32[1,128]{1,0:T(1,128)S(1)} %fusion.extra_ref, ...), custom_call_target="tpu_custom_call" | custom-call | tf_op jit(solution)/shard_map/moments/pallas_call | solution.py:475
  23.5 7.5 %all_to_all.14 = f32[8,1,128]{2,1,0:T(1,128)S(1)} all-to-all(f32[8,1,128]{2,1,0:T(1,128)S(1)} %broadcast_in_dim.9), channel_id=1, replica_groups=mesh['macro'=32,'pencil'=8] {'pencil'}, dimensions={0} | all-to-all | bytes 8192 | tf_op jit(solution)/shard_map/all_to_all | solution.py:498
  31.0 19.5 %all_to_all.15 = f32[32,1,128]{2,1,0:T(1,128)} all-to-all(f32[32,1,128]{2,1,0:T(1,128)S(1)} %broadcast_in_dim.18), channel_id=1, replica_groups=mesh['macro'=32,'pencil'=8] {'macro'}, dimensions={0} | all-to-all | bytes 32768 | tf_op jit(solution)/shard_map/all_to_all | solution.py:499
  50.5 2.3 %close.1 = (f32[1,3]{1,0:T(1,128)}, f32[1,4]{1,0:T(1,128)}) custom-call(f32[32,128]{1,0:T(8,128)} %bitcast.9), custom_call_target="tpu_custom_call" | custom-call | tf_op jit(solution)/shard_map/close/pallas_call | solution.py:500
  (28 shorter events, 0.1 us)
Async XLA Ops:
  0.6 7.2 %copy-start.6 = (f32[128,128]{1,0:T(8,128)S(1)}, f32[128,128]{1,0:T(8,128)}, u32[]{:S(2)}) copy-start(f32[128,128]{1,0:T(8,128)} %constant.36.clone) | copy-start | bytes 196612
  4.5 4.9 %collective-permute-start = (f32[128,128]{1,0:T(8,128)}, f32[128,128]{1,0:T(8,128)S(1)}, u32[]{:S(2)}, u32[]{:S(2)}) collective-permute-start(f32[128,128]{1,0:T(8,128)} %get-tuple-element.16), channel_id=1, source_target_pairs={{0,1},{1,0},{2,3},{3,2},{4,5},{5,4},{6,7},{7,6},{8,9},{9,8},{10,11... | collective-permute-start | bytes 196616 | tf_op jit(solution)/shard_map/ppermute | solution.py:448
  9.4 3.2 %copy-start.7 = (f32[128,128]{1,0:T(8,128)S(1)}, f32[128,128]{1,0:T(8,128)}, u32[]{:S(2)}) copy-start(f32[128,128]{1,0:T(8,128)} %constant.34.clone.norm_hbm) | copy-start | bytes 196612
  9.4 4.8 %copy-start.8 = (f32[128,128]{1,0:T(8,128)S(1)}, f32[128,128]{1,0:T(8,128)}, u32[]{:S(2)}) copy-start(f32[128,128]{1,0:T(8,128)} %get-tuple-element.21) | copy-start | bytes 196612
  9.4 5.1 %collective-permute-start.3 = (f32[128,128]{1,0:T(8,128)S(1)}, f32[128,128]{1,0:T(8,128)S(1)}, u32[]{:S(2)}, u32[]{:S(2)}) collective-permute-start(f32[128,128]{1,0:T(8,128)S(1)} %add.17), channel_id=1, source_target_pairs={{0,6},{1,3},{2,0},{3,5},{4,2},{5,7},{6,4},{7,1},{8,14},{9,11},{10,... | collective-permute-start | bytes 196616 | tf_op jit(solution)/shard_map/ppermute | solution.py:445
  9.5 4.8 %collective-permute-start.1 = (f32[128,128]{1,0:T(8,128)S(1)}, f32[128,128]{1,0:T(8,128)S(1)}, u32[]{:S(2)}, u32[]{:S(2)}) collective-permute-start(f32[128,128]{1,0:T(8,128)S(1)} %add.17), channel_id=1, source_target_pairs={{0,4},{1,5},{2,6},{3,7},{4,0},{5,1},{6,2},{7,3},{8,12},{9,13},{10,... | collective-permute-start | bytes 196616 | tf_op jit(solution)/shard_map/ppermute | solution.py:445
  11.4 4.1 %collective-permute-start.2 = (f32[128,128]{1,0:T(8,128)S(1)}, f32[128,128]{1,0:T(8,128)S(1)}, u32[]{:S(2)}, u32[]{:S(2)}) collective-permute-start(f32[128,128]{1,0:T(8,128)S(1)} %add.17), channel_id=1, source_target_pairs={{0,2},{1,7},{2,4},{3,1},{4,6},{5,3},{6,0},{7,5},{8,10},{9,15},{10,... | collective-permute-start | bytes 196616 | tf_op jit(solution)/shard_map/ppermute | solution.py:445
  12.6 1.7 %copy-start.14 = (s32[1,8]{1,0:T(1,128)S(1)}, s32[1,8]{1,0:T(1,128)}, u32[]{:S(2)}) copy-start(s32[1,8]{1,0:T(1,128)} %param.24) | copy-start | bytes 100
  12.6 1.7 %copy-start.15 = (s32[4]{0:T(128)S(1)}, s32[4]{0:T(128)}, u32[]{:S(2)}) copy-start(s32[4]{0:T(128)} %param.25) | copy-start | bytes 52
  12.6 1.8 %copy-start.11 = (f32[128,128]{1,0:T(8,128)S(1)}, f32[128,128]{1,0:T(8,128)}, u32[]{:S(2)}) copy-start(f32[128,128]{1,0:T(8,128)} %constant.38.clone) | copy-start | bytes 196612
  12.6 1.8 %copy-start.12 = (f32[128,128]{1,0:T(8,128)S(1)}, f32[128,128]{1,0:T(8,128)}, u32[]{:S(2)}) copy-start(f32[128,128]{1,0:T(8,128)} %constant.37.clone) | copy-start | bytes 196612
  12.6 2.9 %copy-start.9 = (f32[128,128]{1,0:T(8,128)S(1)}, f32[128,128]{1,0:T(8,128)}, u32[]{:S(2)}) copy-start(f32[128,128]{1,0:T(8,128)} %constant.40.clone) | copy-start | bytes 196612
  12.6 2.9 %copy-start.10 = (f32[128,128]{1,0:T(8,128)S(1)}, f32[128,128]{1,0:T(8,128)}, u32[]{:S(2)}) copy-start(f32[128,128]{1,0:T(8,128)} %constant.39.clone) | copy-start | bytes 196612
  12.6 5.4 %copy-start.1 = (f32[128,128]{1,0:T(8,128)S(1)}, f32[128,128]{1,0:T(8,128)}, u32[]{:S(2)}) copy-start(f32[128,128]{1,0:T(8,128)} %constant.35.clone.rho_hbm.rho_ref) | copy-start | bytes 196612
  12.6 5.4 %copy-start.2 = (bf16[256,256]{1,0:T(8,128)(2,1)S(1)}, bf16[256,256]{1,0:T(8,128)(2,1)}, u32[]{:S(2)}) copy-start(bf16[256,256]{1,0:T(8,128)(2,1)} %constant.41.clone.right_basis_ref) | copy-start | bytes 393220
  12.7 5.4 %copy-start.3 = (bf16[256,256]{1,0:T(8,128)(2,1)S(1)}, bf16[256,256]{1,0:T(8,128)(2,1)}, u32[]{:S(2)}) copy-start(bf16[256,256]{1,0:T(8,128)(2,1)} %constant.42.clone.right_slope_ref) | copy-start | bytes 393220
  12.7 5.4 %copy-start.4 = (bf16[256,256]{1,0:T(8,128)(2,1)S(1)}, bf16[256,256]{1,0:T(8,128)(2,1)}, u32[]{:S(2)}) copy-start(bf16[256,256]{1,0:T(8,128)(2,1)} %constant.43.clone.left_basis_ref) | copy-start | bytes 393220
  12.7 5.4 %copy-start.5 = (bf16[256,256]{1,0:T(8,128)(2,1)S(1)}, bf16[256,256]{1,0:T(8,128)(2,1)}, u32[]{:S(2)}) copy-start(bf16[256,256]{1,0:T(8,128)(2,1)} %constant.44.clone.left_slope_ref) | copy-start | bytes 393220
  14.2 3.9 %copy-start = (f32[16,128,128]{2,1,0:T(8,128)S(1)}, f32[16,128,128]{2,1,0:T(8,128)}, u32[]{:S(2)}) copy-start(f32[16,128,128]{2,1,0:T(8,128)} %get-tuple-element.15.conduct_ref) | copy-start | bytes 3145732
  15.5 1.6 %copy-start.13 = (f32[4]{0:T(128)S(1)}, f32[4]{0:T(128)}, u32[]{:S(2)}) copy-start(f32[4]{0:T(128)} %param.23) | copy-start | bytes 52
  15.5 2.5 %collective-permute-start.4 = (f32[128,128]{1,0:T(8,128)S(1)}, f32[128,128]{1,0:T(8,128)S(1)}, u32[]{:S(2)}, u32[]{:S(2)}) collective-permute-start(f32[128,128]{1,0:T(8,128)S(1)} %get-tuple-element.28), channel_id=1, source_target_pairs={{0,1},{1,0},{2,3},{3,2},{4,5},{5,4},{6,7},{7,6},{8,9},{9,8},{10,11... | collective-permute-start | bytes 196616 | tf_op jit(solution)/shard_map/ppermute | solution.py:471

commit v6 on v5

--- a/solution.py
+++ b/solution.py
@@ -132,12 +132,15 @@
         ids_copy(piece).start()
         fiber_copy(piece).start()
     sums_ref[...] = jnp.zeros_like(sums_ref)
-    for copy in tables:
-        copy.wait()
+    tables[0].wait()
 
     def along_z(piece):
-        ids_copy(piece).wait()
-        fiber_copy(piece).wait()
+        if piece == 0:
+            for each in range(PIECES):
+                ids_copy(each).wait()
+                fiber_copy(each).wait()
+            for copy in tables[1:]:
+                copy.wait()
         planes = []
         for part in range(group):
             x = group * piece + part
@@ -266,19 +269,10 @@
 
     pairs = slab // 2 + 1
 
-    def lines_only(step, carry):
-        along_z(step)
-        return carry
-
-    def warm(step, carry):
-        along_y(step - 1)
-        along_z(step)
-        return carry
-
-    def plane(step, totals, products=2):
+    def differences(pair, totals):
         totals = list(totals)
         for place in range(2 * (width // ROWS)):
-            x = 2 * (step - 3) + place // (width // ROWS)
+            x = 2 * pair + place // (width // ROWS)
             chunk = place % (width // ROWS)
             at = pl.ds(chunk * ROWS, ROWS)
             down = pl.ds(chunk * ROWS + 1, ROWS)
@@ -297,18 +291,17 @@
                     totals[at_entry] = totals[at_entry] + term
                     totals[6 + at_entry] = totals[6 + at_entry] + conduct * term
                     at_entry += 1
-        if products > 0:
+        return tuple(totals)
+
+    nothing = jnp.zeros((ROWS, width), jnp.float32)
+    totals = (nothing,) * 12
+    for step in range(pairs + 2):
+        if step >= 3:
+            totals = differences(step - 3, totals)
+        if 1 <= step <= pairs:
             along_y(step - 1)
-        if products > 1:
+        if step < pairs:
             along_z(step)
-        return tuple(totals)
-
-    nothing = jnp.zeros((ROWS, width), jnp.float32)
-    lax.fori_loop(0, 1, lines_only, 0)
-    lax.fori_loop(1, 3, warm, 0)
-    totals = lax.fori_loop(3, pairs, plane, (nothing,) * 12)
-    totals = lax.fori_loop(pairs, pairs + 1, lambda step, t: plane(step, t, 1), totals)
-    totals = lax.fori_loop(pairs + 1, pairs + 2, lambda step, t: plane(step, t, 0), totals)
     lines = [jnp.sum(total, axis=0, keepdims=True) for total in totals]
     lines = jnp.concatenate(lines + [jnp.zeros((4, width), jnp.float32)], axis=0)
     column = jnp.sum(lines, axis=1, keepdims=True)
@@ -505,6 +498,7 @@
         ),
         in_specs=[vmem],
         out_specs=(vmem, vmem),
+        compiler_params=params,
         name="close",
     )(table)
     return (flux, nodal.reshape(own_nodes))

time: 53.1 us -> 51.9 us (0.977)
  Pallas kernels: 11.6 us -> 10.4 us
    pallas_call x1, Pallas kernels: 2.29 us -> 1.65 us  [on_device(): pl.pallas_call(lambda *refs: close_kernel(own_nodes, volume, *refs), out_...]
where the time goes in v6:
time: 51.9 us; the launch traced here: 51.6 us
  blocking collectives  27 us (52%)
  Pallas kernels  10.4 us (20%)
  starting transfers between devices  8.08 us (16%)
  other arithmetic  2.57 us (5%)
  waiting for transfers between devices  1.94 us (4%)
  between operations  1.55 us (3%)
    all_to_all x1, blocking collectives, on_device(): lax.all_to_all(jnp.broadcast_to(table, (groups, LANES)), 'macro', 0, 0, t...  19.5 us
    all_to_all x1, blocking collectives, on_device(): lax.all_to_all(table, 'pencil', 0, 0, tiled=True)  7.48 us
    pallas_call x1, Pallas kernels, on_device(): pl.pallas_call(moments_kernel, out_shape=jax.ShapeDtypeStruct((1, LANES),...  4.94 us
    pallas_call x1, Pallas kernels, on_device(): pl.pallas_call(analyse_kernel, out_shape=(block, block, plane, plane), in...  3.81 us
    ppermute x1, starting transfers between devices, on_device(): lax.ppermute(give, 'pencil', swap) + lax.optimization_barrier(step * keep)  3.33 us
    ppermute x3, starting transfers between devices, from_chip(): return lax.ppermute(array, 'pencil', perm)  3.15 us
    pallas_call x1, Pallas kernels, on_device(): pl.pallas_call(lambda *refs: close_kernel(own_nodes, volume, *refs), out_...  1.65 us
    ppermute x1, starting transfers between devices, on_device(): other = lax.ppermute(kept + step * own, 'pencil', swap)  1.6 us
  transfers between devices with their start and end apart: 5, of which 3 were waited for; matrix products, arithmetic and copies ran while one was open for 5% of the time, Pallas kernels for 0%

profile of v6, /device:TPU:1, one launch (start us, length us, event | category | flops | bytes accessed | tf_op | source)
XLA Modules:
  0.0 51.6 jit_solution(18108571561602925406)
XLA Ops:
  0.6 0.0 copy-start.6
  0.6 3.8 %analyse.1 = (f32[16,128,128]{2,1,0:T(8,128)}, f32[16,128,128]{2,1,0:T(8,128)}, f32[128,128]{1,0:T(8,128)}, f32[128,128]{1,0:T(8,128)}) custom-call(f32[1,3]{1,0:T(1,128)} %material_hbm.1, s32[1,16,128,128]{3,2,1,0:T(8,128)} %ids_hbm.1, f32[1,16,128,128]{3,2,1,0:T(8,128)} %fiber_hbm.1, bf16[256,256]{1,0:T(8,128)(2,1)} %constant.32.clone.right_hbm, ...), custom_call_target="tpu_custom_call" | custom-call | tf_op jit(solution)/shard_map/analyse/pallas_call | solution.py:397
  4.5 3.3 %collective-permute-start = (f32[128,128]{1,0:T(8,128)}, f32[128,128]{1,0:T(8,128)S(1)}, u32[]{:S(2)}, u32[]{:S(2)}) collective-permute-start(f32[128,128]{1,0:T(8,128)} %get-tuple-element.16), channel_id=1, source_target_pairs={{0,1},{1,0},{2,3},{3,2},{4,5},{5,4},{6,7},{7,6},{8,9},{9,8},{10,11... | collective-permute-start | bytes 196616 | tf_op jit(solution)/shard_map/ppermute | solution.py:441
  7.8 0.0 copy-done.6
  7.8 0.8 %mul.26 = f32[128,128]{1,0:T(8,128)S(1)} multiply(f32[128,128]{1,0:T(8,128)S(1)} %copy-done.6, f32[128,128]{1,0:T(8,128)} %get-tuple-element.21) | non-fusion elementwise | flops 16384 | bytes 196608 | tf_op jit(solution)/shard_map/mul | solution.py:441
  9.3 0.0 copy-start.7
  9.3 0.0 collective-permute-done
  9.3 0.0 copy-start.8
  9.4 0.1 collective-permute-start.3
  9.4 1.9 %collective-permute-start.1 = (f32[128,128]{1,0:T(8,128)S(1)}, f32[128,128]{1,0:T(8,128)S(1)}, u32[]{:S(2)}, u32[]{:S(2)}) collective-permute-start(f32[128,128]{1,0:T(8,128)S(1)} %add.17), channel_id=1, source_target_pairs={{0,4},{1,5},{2,6},{3,7},{4,0},{5,1},{6,2},{7,3},{8,12},{9,13},{10,... | collective-permute-start | bytes 196616 | tf_op jit(solution)/shard_map/ppermute | solution.py:438
  11.4 1.2 %collective-permute-start.2 = (f32[128,128]{1,0:T(8,128)S(1)}, f32[128,128]{1,0:T(8,128)S(1)}, u32[]{:S(2)}, u32[]{:S(2)}) collective-permute-start(f32[128,128]{1,0:T(8,128)S(1)} %add.17), channel_id=1, source_target_pairs={{0,2},{1,7},{2,4},{3,1},{4,6},{5,3},{6,0},{7,5},{8,10},{9,15},{10,... | collective-permute-start | bytes 196616 | tf_op jit(solution)/shard_map/ppermute | solution.py:438
  12.5 0.0 copy-start.12
  12.5 0.0 copy-start.9
  12.6 0.0 copy-start.10
  12.6 0.0 copy-start.1
  12.6 0.0 copy-start.2
  12.6 0.0 copy-start.3
  12.6 0.0 copy-start.4
  12.6 0.0 copy-start.5
  12.6 1.5 %broadcast_multiply_fusion.modes_ref = f32[16,128,128]{2,1,0:T(8,128)S(1)} fusion(f32[16,128,128]{2,1,0:T(8,128)} %get-tuple-element.19, f32[128,128]{1,0:T(8,128)S(1)} %copy-done.7), kind=kLoop, calls=%fused_computation | loop fusion | flops 262144 | bytes 2162688 | tf_op jit(solution)/shard_map/mul | solution.py:445
  14.1 0.1 and_select_fusion
  14.3 0.0 collective-permute-done.1
  14.3 0.1 collective-permute-done.3
  14.5 1.0 %collective-permute-done.2 = f32[128,128]{1,0:T(8,128)S(1)} collective-permute-done((f32[128,128]{1,0:T(8,128)S(1)}, f32[128,128]{1,0:T(8,128)S(1)}, u32[]{:S(2)}, u32[]{:S(2)}) %collective-permute-start.2) | collective-permute-done | bytes 65568 | tf_op jit(solution)/shard_map/ppermute | solution.py:438
  15.5 0.0 copy-start.13
  15.5 1.6 %collective-permute-start.4 = (f32[128,128]{1,0:T(8,128)S(1)}, f32[128,128]{1,0:T(8,128)S(1)}, u32[]{:S(2)}, u32[]{:S(2)}) collective-permute-start(f32[128,128]{1,0:T(8,128)S(1)} %get-tuple-element.28), channel_id=1, source_target_pairs={{0,1},{1,0},{2,3},{3,2},{4,5},{5,4},{6,7},{7,6},{8,9},{9,8},{10,11... | collective-permute-start | bytes 196616 | tf_op jit(solution)/shard_map/ppermute | solution.py:464
  17.1 0.1 fusion.extra_ref
  17.2 0.8 %collective-permute-done.4.other_ref = f32[128,128]{1,0:T(8,128)S(1)} collective-permute-done((f32[128,128]{1,0:T(8,128)S(1)}, f32[128,128]{1,0:T(8,128)S(1)}, u32[]{:S(2)}, u32[]{:S(2)}) %collective-permute-start.4) | collective-permute-done | bytes 65568 | tf_op jit(solution)/shard_map/ppermute | solution.py:464
  18.0 4.9 %moments.1 = f32[1,128]{1,0:T(1,128)S(1)} custom-call(f32[16,128,128]{2,1,0:T(8,128)S(1)} %copy-done, f32[16,128,128]{2,1,0:T(8,128)S(1)} %broadcast_multiply_fusion.modes_ref, f32[128,128]{1,0:T(8,128)S(1)} %get-tuple-element.29.own_ref, f32[128,128]{1,0:T(8,128)S(1)} %collective-permute-done.4.other_ref, f32[1,128]{1,0:T(1,128)S(1)} %fusion.extra_ref, ...), custom_call_target="tpu_custom_call" | custom-call | tf_op jit(solution)/shard_map/moments/pallas_call | solution.py:468
  23.0 7.5 %all_to_all.14 = f32[8,1,128]{2,1,0:T(1,128)S(1)} all-to-all(f32[8,1,128]{2,1,0:T(1,128)S(1)} %broadcast_in_dim.9), channel_id=1, replica_groups=mesh['macro'=32,'pencil'=8] {'pencil'}, dimensions={0} | all-to-all | bytes 8192 | tf_op jit(solution)/shard_map/all_to_all | solution.py:491
  30.5 19.5 %all_to_all.15 = f32[32,1,128]{2,1,0:T(1,128)S(1)} all-to-all(f32[32,1,128]{2,1,0:T(1,128)S(1)} %broadcast_in_dim.18), channel_id=1, replica_groups=mesh['macro'=32,'pencil'=8] {'macro'}, dimensions={0} | all-to-all | bytes 32768 | tf_op jit(solution)/shard_map/all_to_all | solution.py:492
  50.0 1.6 %close.1 = (f32[1,3]{1,0:T(1,128)}, f32[1,4]{1,0:T(1,128)}) custom-call(f32[32,128]{1,0:T(8,128)S(1)} %bitcast.8), custom_call_target="tpu_custom_call" | custom-call | tf_op jit(solution)/shard_map/close/pallas_call | solution.py:493
  (28 shorter events, 0.1 us)
Async XLA Ops:
  0.6 7.2 %copy-start.6 = (f32[128,128]{1,0:T(8,128)S(1)}, f32[128,128]{1,0:T(8,128)}, u32[]{:S(2)}) copy-start(f32[128,128]{1,0:T(8,128)} %constant.36.clone) | copy-start | bytes 196612
  4.5 4.9 %collective-permute-start = (f32[128,128]{1,0:T(8,128)}, f32[128,128]{1,0:T(8,128)S(1)}, u32[]{:S(2)}, u32[]{:S(2)}) collective-permute-start(f32[128,128]{1,0:T(8,128)} %get-tuple-element.16), channel_id=1, source_target_pairs={{0,1},{1,0},{2,3},{3,2},{4,5},{5,4},{6,7},{7,6},{8,9},{9,8},{10,11... | collective-permute-start | bytes 196616 | tf_op jit(solution)/shard_map/ppermute | solution.py:441
  9.3 3.2 %copy-start.7 = (f32[128,128]{1,0:T(8,128)S(1)}, f32[128,128]{1,0:T(8,128)}, u32[]{:S(2)}) copy-start(f32[128,128]{1,0:T(8,128)} %constant.34.clone.norm_hbm) | copy-start | bytes 196612
  9.3 4.8 %copy-start.8 = (f32[128,128]{1,0:T(8,128)S(1)}, f32[128,128]{1,0:T(8,128)}, u32[]{:S(2)}) copy-start(f32[128,128]{1,0:T(8,128)} %get-tuple-element.21) | copy-start | bytes 196612
  9.4 5.1 %collective-permute-start.3 = (f32[128,128]{1,0:T(8,128)S(1)}, f32[128,128]{1,0:T(8,128)S(1)}, u32[]{:S(2)}, u32[]{:S(2)}) collective-permute-start(f32[128,128]{1,0:T(8,128)S(1)} %add.17), channel_id=1, source_target_pairs={{0,6},{1,3},{2,0},{3,5},{4,2},{5,7},{6,4},{7,1},{8,14},{9,11},{10,... | collective-permute-start | bytes 196616 | tf_op jit(solution)/shard_map/ppermute | solution.py:438
  9.4 4.8 %collective-permute-start.1 = (f32[128,128]{1,0:T(8,128)S(1)}, f32[128,128]{1,0:T(8,128)S(1)}, u32[]{:S(2)}, u32[]{:S(2)}) collective-permute-start(f32[128,128]{1,0:T(8,128)S(1)} %add.17), channel_id=1, source_target_pairs={{0,4},{1,5},{2,6},{3,7},{4,0},{5,1},{6,2},{7,3},{8,12},{9,13},{10,... | collective-permute-start | bytes 196616 | tf_op jit(solution)/shard_map/ppermute | solution.py:438
  11.4 4.1 %collective-permute-start.2 = (f32[128,128]{1,0:T(8,128)S(1)}, f32[128,128]{1,0:T(8,128)S(1)}, u32[]{:S(2)}, u32[]{:S(2)}) collective-permute-start(f32[128,128]{1,0:T(8,128)S(1)} %add.17), channel_id=1, source_target_pairs={{0,2},{1,7},{2,4},{3,1},{4,6},{5,3},{6,0},{7,5},{8,10},{9,15},{10,... | collective-permute-start | bytes 196616 | tf_op jit(solution)/shard_map/ppermute | solution.py:438
  12.5 1.7 %copy-start.14 = (s32[1,8]{1,0:T(1,128)S(1)}, s32[1,8]{1,0:T(1,128)}, u32[]{:S(2)}) copy-start(s32[1,8]{1,0:T(1,128)} %param.24) | copy-start | bytes 100
  12.5 1.7 %copy-start.15 = (s32[4]{0:T(128)S(1)}, s32[4]{0:T(128)}, u32[]{:S(2)}) copy-start(s32[4]{0:T(128)} %param.25) | copy-start | bytes 52
  12.5 1.8 %copy-start.11 = (f32[128,128]{1,0:T(8,128)S(1)}, f32[128,128]{1,0:T(8,128)}, u32[]{:S(2)}) copy-start(f32[128,128]{1,0:T(8,128)} %constant.38.clone) | copy-start | bytes 196612
  12.5 1.8 %copy-start.12 = (f32[128,128]{1,0:T(8,128)S(1)}, f32[128,128]{1,0:T(8,128)}, u32[]{:S(2)}) copy-start(f32[128,128]{1,0:T(8,128)} %constant.37.clone) | copy-start | bytes 196612
  12.5 2.9 %copy-start.9 = (f32[128,128]{1,0:T(8,128)S(1)}, f32[128,128]{1,0:T(8,128)}, u32[]{:S(2)}) copy-start(f32[128,128]{1,0:T(8,128)} %constant.40.clone) | copy-start | bytes 196612
  12.6 2.9 %copy-start.10 = (f32[128,128]{1,0:T(8,128)S(1)}, f32[128,128]{1,0:T(8,128)}, u32[]{:S(2)}) copy-start(f32[128,128]{1,0:T(8,128)} %constant.39.clone) | copy-start | bytes 196612
  12.6 5.4 %copy-start.1 = (f32[128,128]{1,0:T(8,128)S(1)}, f32[128,128]{1,0:T(8,128)}, u32[]{:S(2)}) copy-start(f32[128,128]{1,0:T(8,128)} %constant.35.clone.rho_hbm.rho_ref) | copy-start | bytes 196612
  12.6 5.4 %copy-start.2 = (bf16[256,256]{1,0:T(8,128)(2,1)S(1)}, bf16[256,256]{1,0:T(8,128)(2,1)}, u32[]{:S(2)}) copy-start(bf16[256,256]{1,0:T(8,128)(2,1)} %constant.41.clone.right_basis_ref) | copy-start | bytes 393220
  12.6 5.4 %copy-start.3 = (bf16[256,256]{1,0:T(8,128)(2,1)S(1)}, bf16[256,256]{1,0:T(8,128)(2,1)}, u32[]{:S(2)}) copy-start(bf16[256,256]{1,0:T(8,128)(2,1)} %constant.42.clone.right_slope_ref) | copy-start | bytes 393220
  12.6 5.4 %copy-start.4 = (bf16[256,256]{1,0:T(8,128)(2,1)S(1)}, bf16[256,256]{1,0:T(8,128)(2,1)}, u32[]{:S(2)}) copy-start(bf16[256,256]{1,0:T(8,128)(2,1)} %constant.43.clone.left_basis_ref) | copy-start | bytes 393220
  12.6 5.4 %copy-start.5 = (bf16[256,256]{1,0:T(8,128)(2,1)S(1)}, bf16[256,256]{1,0:T(8,128)(2,1)}, u32[]{:S(2)}) copy-start(bf16[256,256]{1,0:T(8,128)(2,1)} %constant.44.clone.left_slope_ref) | copy-start | bytes 393220
  14.1 3.9 %copy-start = (f32[16,128,128]{2,1,0:T(8,128)S(1)}, f32[16,128,128]{2,1,0:T(8,128)}, u32[]{:S(2)}) copy-start(f32[16,128,128]{2,1,0:T(8,128)} %get-tuple-element.15.conduct_ref) | copy-start | bytes 3145732
  15.5 1.6 %copy-start.13 = (f32[4]{0:T(128)S(1)}, f32[4]{0:T(128)}, u32[]{:S(2)}) copy-start(f32[4]{0:T(128)} %param.23) | copy-start | bytes 52
  15.5 2.5 %collective-permute-start.4 = (f32[128,128]{1,0:T(8,128)S(1)}, f32[128,128]{1,0:T(8,128)S(1)}, u32[]{:S(2)}, u32[]{:S(2)}) collective-permute-start(f32[128,128]{1,0:T(8,128)S(1)} %get-tuple-element.28), channel_id=1, source_target_pairs={{0,1},{1,0},{2,3},{3,2},{4,5},{5,4},{6,7},{7,6},{8,9},{9,8},{10,11... | collective-permute-start | bytes 196616 | tf_op jit(solution)/shard_map/ppermute | solution.py:464

commit v7 on v6

--- a/solution.py
+++ b/solution.py
@@ -269,11 +269,9 @@
 
     pairs = slab // 2 + 1
 
-    def differences(pair, totals):
+    def differences(x, totals):
         totals = list(totals)
-        for place in range(2 * (width // ROWS)):
-            x = 2 * pair + place // (width // ROWS)
-            chunk = place % (width // ROWS)
+        for chunk in range(width // ROWS):
             at = pl.ds(chunk * ROWS, ROWS)
             down = pl.ds(chunk * ROWS + 1, ROWS)
             conduct = conduct_ref[x, at]
@@ -297,9 +295,11 @@
     totals = (nothing,) * 12
     for step in range(pairs + 2):
         if step >= 3:
-            totals = differences(step - 3, totals)
+            totals = differences(2 * (step - 3), totals)
         if 1 <= step <= pairs:
             along_y(step - 1)
+        if step >= 3:
+            totals = differences(2 * (step - 3) + 1, totals)
         if step < pairs:
             along_z(step)
     lines = [jnp.sum(total, axis=0, keepdims=True) for total in totals]
@@ -460,7 +460,7 @@
     own = lax.optimization_barrier(powers[half - 1] * from_chip(chip, half) + powers[-1] * chip)
     for away in range(1, chips):
         if away != half:
-            own = own + powers[away - 1] * from_chip(chip, away)
+            own = lax.optimization_barrier(own + powers[away - 1] * from_chip(chip, away))
     other = lax.ppermute(kept + step * own, "pencil", swap)
 
     field = (slab + 2, width, width)

time: 51.9 us -> 53 us (1.021)
  starting transfers between devices: 8.08 us -> 6.41 us
  waiting for transfers between devices: 1.94 us -> 3.51 us
  blocking collectives: 27 us -> 28.2 us
    ppermute x3, waiting for transfers between devices: 1.12 us -> 2.76 us  [from_chip(): return lax.ppermute(array, 'pencil', perm)]
    all_to_all x1, blocking collectives: 7.48 us -> 8.6 us  [on_device(): lax.all_to_all(table, 'pencil', 0, 0, tiled=True)]
    ppermute x1, starting transfers between devices: 1.6 us -> 0.52 us  [on_device(): other = lax.ppermute(kept + step * own, 'pencil', swap)]
    ppermute x3, starting transfers between devices: 3.15 us -> 2.56 us  [from_chip(): return lax.ppermute(array, 'pencil', perm)]
where the time goes in v7:
time: 53 us; the launch traced here: 52.8 us
  blocking collectives  28.2 us (53%)
  Pallas kernels  10.4 us (20%)
  starting transfers between devices  6.41 us (12%)
  waiting for transfers between devices  3.51 us (7%)
  other arithmetic  2.55 us (5%)
  between operations  1.54 us (3%)
    all_to_all x1, blocking collectives, on_device(): lax.all_to_all(jnp.broadcast_to(table, (groups, LANES)), 'macro', 0, 0, t...  19.6 us
    all_to_all x1, blocking collectives, on_device(): lax.all_to_all(table, 'pencil', 0, 0, tiled=True)  8.6 us
    pallas_call x1, Pallas kernels, on_device(): pl.pallas_call(moments_kernel, out_shape=jax.ShapeDtypeStruct((1, LANES),...  4.91 us
    pallas_call x1, Pallas kernels, on_device(): pl.pallas_call(analyse_kernel, out_shape=(block, block, plane, plane), in...  3.82 us
    ppermute x1, starting transfers between devices, on_device(): lax.ppermute(give, 'pencil', swap) + lax.optimization_barrier(step * keep)  3.33 us
    ppermute x3, waiting for transfers between devices, from_chip(): return lax.ppermute(array, 'pencil', perm)  2.76 us
    ppermute x3, starting transfers between devices, from_chip(): return lax.ppermute(array, 'pencil', perm)  2.56 us
    pallas_call x1, Pallas kernels, on_device(): pl.pallas_call(lambda *refs: close_kernel(own_nodes, volume, *refs), out_...  1.65 us
  transfers between devices with their start and end apart: 5, of which 3 were waited for; matrix products, arithmetic and copies ran while one was open for 5% of the time, Pallas kernels for 0%

profile of v7, /device:TPU:1, one launch (start us, length us, event | category | flops | bytes accessed | tf_op | source)
XLA Modules:
  0.0 52.8 jit_solution(9259793262361138249)
XLA Ops:
  0.6 0.0 copy-start.8
  0.6 3.8 %analyse.1 = (f32[16,128,128]{2,1,0:T(8,128)}, f32[16,128,128]{2,1,0:T(8,128)}, f32[128,128]{1,0:T(8,128)}, f32[128,128]{1,0:T(8,128)}) custom-call(f32[1,3]{1,0:T(1,128)} %material_hbm.1, s32[1,16,128,128]{3,2,1,0:T(8,128)} %ids_hbm.1, f32[1,16,128,128]{3,2,1,0:T(8,128)} %fiber_hbm.1, bf16[256,256]{1,0:T(8,128)(2,1)} %constant.32.clone.right_hbm, ...), custom_call_target="tpu_custom_call" | custom-call | tf_op jit(solution)/shard_map/analyse/pallas_call | solution.py:397
  4.5 3.3 %collective-permute-start = (f32[128,128]{1,0:T(8,128)}, f32[128,128]{1,0:T(8,128)S(1)}, u32[]{:S(2)}, u32[]{:S(2)}) collective-permute-start(f32[128,128]{1,0:T(8,128)} %get-tuple-element.16), channel_id=1, source_target_pairs={{0,1},{1,0},{2,3},{3,2},{4,5},{5,4},{6,7},{7,6},{8,9},{9,8},{10,11... | collective-permute-start | bytes 196616 | tf_op jit(solution)/shard_map/ppermute | solution.py:441
  7.8 0.8 %mul.26 = f32[128,128]{1,0:T(8,128)S(1)} multiply(f32[128,128]{1,0:T(8,128)S(1)} %copy-done.8, f32[128,128]{1,0:T(8,128)} %get-tuple-element.21) | non-fusion elementwise | flops 16384 | bytes 196608 | tf_op jit(solution)/shard_map/mul | solution.py:441
  9.3 0.0 copy-start.6
  9.3 0.0 collective-permute-done
  9.4 0.0 copy-start.7
  9.4 1.1 %collective-permute-start.1 = (f32[128,128]{1,0:T(8,128)S(1)}, f32[128,128]{1,0:T(8,128)S(1)}, u32[]{:S(2)}, u32[]{:S(2)}) collective-permute-start(f32[128,128]{1,0:T(8,128)S(1)} %add.17), channel_id=1, source_target_pairs={{0,4},{1,5},{2,6},{3,7},{4,0},{5,1},{6,2},{7,3},{8,12},{9,13},{10,... | collective-permute-start | bytes 196616 | tf_op jit(solution)/shard_map/ppermute | solution.py:438
  10.5 0.9 %collective-permute-start.2 = (f32[128,128]{1,0:T(8,128)S(1)}, f32[128,128]{1,0:T(8,128)S(1)}, u32[]{:S(2)}, u32[]{:S(2)}) collective-permute-start(f32[128,128]{1,0:T(8,128)S(1)} %add.17), channel_id=1, source_target_pairs={{0,2},{1,7},{2,4},{3,1},{4,6},{5,3},{6,0},{7,5},{8,10},{9,15},{10,... | collective-permute-start | bytes 196616 | tf_op jit(solution)/shard_map/ppermute | solution.py:438
  11.3 0.6 %collective-permute-start.3 = (f32[128,128]{1,0:T(8,128)S(1)}, f32[128,128]{1,0:T(8,128)S(1)}, u32[]{:S(2)}, u32[]{:S(2)}) collective-permute-start(f32[128,128]{1,0:T(8,128)S(1)} %add.17), channel_id=1, source_target_pairs={{0,6},{1,3},{2,0},{3,5},{4,2},{5,7},{6,4},{7,1},{8,14},{9,11},{10,... | collective-permute-start | bytes 196616 | tf_op jit(solution)/shard_map/ppermute | solution.py:438
  11.9 0.0 copy-start.10
  11.9 0.0 copy-start.12
  12.0 0.0 copy-start.11
  12.0 0.0 copy-start.3
  12.0 0.0 copy-start.4
  12.0 0.0 copy-start.5
  12.0 1.4 %broadcast_multiply_fusion.modes_ref = f32[16,128,128]{2,1,0:T(8,128)S(1)} fusion(f32[16,128,128]{2,1,0:T(8,128)} %get-tuple-element.19, f32[128,128]{1,0:T(8,128)S(1)} %copy-done.6), kind=kLoop, calls=%fused_computation | loop fusion | flops 262144 | bytes 2162688 | tf_op jit(solution)/shard_map/mul | solution.py:445
  13.5 0.1 and_select_fusion
  13.6 1.0 %collective-permute-done.1 = f32[128,128]{1,0:T(8,128)S(1)} collective-permute-done((f32[128,128]{1,0:T(8,128)S(1)}, f32[128,128]{1,0:T(8,128)S(1)}, u32[]{:S(2)}, u32[]{:S(2)}) %collective-permute-start.1) | collective-permute-done | bytes 65568 | tf_op jit(solution)/shard_map/ppermute | solution.py:438
  14.7 0.0 collective-permute-done.2
  14.7 1.7 %collective-permute-done.3 = f32[128,128]{1,0:T(8,128)S(1)} collective-permute-done((f32[128,128]{1,0:T(8,128)S(1)}, f32[128,128]{1,0:T(8,128)S(1)}, u32[]{:S(2)}, u32[]{:S(2)}) %collective-permute-start.3) | collective-permute-done | bytes 65568 | tf_op jit(solution)/shard_map/ppermute | solution.py:438
  16.5 0.0 copy-start.13
  16.5 0.0 copy-start.1
  16.5 0.0 copy-start.2
  16.5 0.5 collective-permute-start.4
  17.0 0.1 copy-done.13
  17.1 0.1 fusion.extra_ref
  17.2 0.7 %collective-permute-done.4.other_ref = f32[128,128]{1,0:T(8,128)S(1)} collective-permute-done((f32[128,128]{1,0:T(8,128)S(1)}, f32[128,128]{1,0:T(8,128)S(1)}, u32[]{:S(2)}, u32[]{:S(2)}) %collective-permute-start.4) | collective-permute-done | bytes 65568 | tf_op jit(solution)/shard_map/ppermute | solution.py:464
  18.0 4.9 %moments.1 = f32[1,128]{1,0:T(1,128)S(1)} custom-call(f32[16,128,128]{2,1,0:T(8,128)S(1)} %copy-done, f32[16,128,128]{2,1,0:T(8,128)S(1)} %broadcast_multiply_fusion.modes_ref, f32[128,128]{1,0:T(8,128)S(1)} %multiply_add_fusion.1.own_ref, f32[128,128]{1,0:T(8,128)S(1)} %collective-permute-done.4.other_ref, f32[1,128]{1,0:T(1,128)S(1)} %fusion.extra_ref, ...), custom_call_target="tpu_custom_call" | custom-call | tf_op jit(solution)/shard_map/moments/pallas_call | solution.py:468
  22.9 8.6 %all_to_all.14 = f32[8,1,128]{2,1,0:T(1,128)S(1)} all-to-all(f32[8,1,128]{2,1,0:T(1,128)S(1)} %broadcast_in_dim.9), channel_id=1, replica_groups=mesh['macro'=32,'pencil'=8] {'pencil'}, dimensions={0} | all-to-all | bytes 8192 | tf_op jit(solution)/shard_map/all_to_all | solution.py:491
  31.5 19.6 %all_to_all.15 = f32[32,1,128]{2,1,0:T(1,128)S(1)} all-to-all(f32[32,1,128]{2,1,0:T(1,128)S(1)} %broadcast_in_dim.18), channel_id=1, replica_groups=mesh['macro'=32,'pencil'=8] {'macro'}, dimensions={0} | all-to-all | bytes 32768 | tf_op jit(solution)/shard_map/all_to_all | solution.py:492
  51.1 1.6 %close.1 = (f32[1,3]{1,0:T(1,128)}, f32[1,4]{1,0:T(1,128)}) custom-call(f32[32,128]{1,0:T(8,128)S(1)} %bitcast.8), custom_call_target="tpu_custom_call" | custom-call | tf_op jit(solution)/shard_map/close/pallas_call | solution.py:493
  (30 shorter events, 0.2 us)
Async XLA Ops:
  0.6 7.2 %copy-start.8 = (f32[128,128]{1,0:T(8,128)S(1)}, f32[128,128]{1,0:T(8,128)}, u32[]{:S(2)}) copy-start(f32[128,128]{1,0:T(8,128)} %constant.36.clone) | copy-start | bytes 196612
  4.5 4.9 %collective-permute-start = (f32[128,128]{1,0:T(8,128)}, f32[128,128]{1,0:T(8,128)S(1)}, u32[]{:S(2)}, u32[]{:S(2)}) collective-permute-start(f32[128,128]{1,0:T(8,128)} %get-tuple-element.16), channel_id=1, source_target_pairs={{0,1},{1,0},{2,3},{3,2},{4,5},{5,4},{6,7},{7,6},{8,9},{9,8},{10,11... | collective-permute-start | bytes 196616 | tf_op jit(solution)/shard_map/ppermute | solution.py:441
  9.3 2.6 %copy-start.6 = (f32[128,128]{1,0:T(8,128)S(1)}, f32[128,128]{1,0:T(8,128)}, u32[]{:S(2)}) copy-start(f32[128,128]{1,0:T(8,128)} %constant.34.clone.norm_hbm) | copy-start | bytes 196612
  9.4 4.1 %copy-start.7 = (f32[128,128]{1,0:T(8,128)S(1)}, f32[128,128]{1,0:T(8,128)}, u32[]{:S(2)}) copy-start(f32[128,128]{1,0:T(8,128)} %get-tuple-element.21) | copy-start | bytes 196612
  9.4 5.3 %collective-permute-start.1 = (f32[128,128]{1,0:T(8,128)S(1)}, f32[128,128]{1,0:T(8,128)S(1)}, u32[]{:S(2)}, u32[]{:S(2)}) collective-permute-start(f32[128,128]{1,0:T(8,128)S(1)} %add.17), channel_id=1, source_target_pairs={{0,4},{1,5},{2,6},{3,7},{4,0},{5,1},{6,2},{7,3},{8,12},{9,13},{10,... | collective-permute-start | bytes 196616 | tf_op jit(solution)/shard_map/ppermute | solution.py:438
  10.5 4.2 %collective-permute-start.2 = (f32[128,128]{1,0:T(8,128)S(1)}, f32[128,128]{1,0:T(8,128)S(1)}, u32[]{:S(2)}, u32[]{:S(2)}) collective-permute-start(f32[128,128]{1,0:T(8,128)S(1)} %add.17), channel_id=1, source_target_pairs={{0,2},{1,7},{2,4},{3,1},{4,6},{5,3},{6,0},{7,5},{8,10},{9,15},{10,... | collective-permute-start | bytes 196616 | tf_op jit(solution)/shard_map/ppermute | solution.py:438
  11.3 5.1 %collective-permute-start.3 = (f32[128,128]{1,0:T(8,128)S(1)}, f32[128,128]{1,0:T(8,128)S(1)}, u32[]{:S(2)}, u32[]{:S(2)}) collective-permute-start(f32[128,128]{1,0:T(8,128)S(1)} %add.17), channel_id=1, source_target_pairs={{0,6},{1,3},{2,0},{3,5},{4,2},{5,7},{6,4},{7,1},{8,14},{9,11},{10,... | collective-permute-start | bytes 196616 | tf_op jit(solution)/shard_map/ppermute | solution.py:438
  11.9 1.6 %copy-start.14 = (s32[1,8]{1,0:T(1,128)S(1)}, s32[1,8]{1,0:T(1,128)}, u32[]{:S(2)}) copy-start(s32[1,8]{1,0:T(1,128)} %param.24) | copy-start | bytes 100
  11.9 1.7 %copy-start.15 = (s32[4]{0:T(128)S(1)}, s32[4]{0:T(128)}, u32[]{:S(2)}) copy-start(s32[4]{0:T(128)} %param.25) | copy-start | bytes 52
  11.9 2.7 %copy-start.9 = (f32[128,128]{1,0:T(8,128)S(1)}, f32[128,128]{1,0:T(8,128)}, u32[]{:S(2)}) copy-start(f32[128,128]{1,0:T(8,128)} %constant.38.clone) | copy-start | bytes 196612
  11.9 2.7 %copy-start.10 = (f32[128,128]{1,0:T(8,128)S(1)}, f32[128,128]{1,0:T(8,128)}, u32[]{:S(2)}) copy-start(f32[128,128]{1,0:T(8,128)} %constant.37.clone) | copy-start | bytes 196612
  11.9 2.8 %copy-start.12 = (f32[128,128]{1,0:T(8,128)S(1)}, f32[128,128]{1,0:T(8,128)}, u32[]{:S(2)}) copy-start(f32[128,128]{1,0:T(8,128)} %constant.39.clone) | copy-start | bytes 196612
  12.0 4.5 %copy-start.11 = (f32[128,128]{1,0:T(8,128)S(1)}, f32[128,128]{1,0:T(8,128)}, u32[]{:S(2)}) copy-start(f32[128,128]{1,0:T(8,128)} %constant.40.clone) | copy-start | bytes 196612
  12.0 6.0 %copy-start.3 = (bf16[256,256]{1,0:T(8,128)(2,1)S(1)}, bf16[256,256]{1,0:T(8,128)(2,1)}, u32[]{:S(2)}) copy-start(bf16[256,256]{1,0:T(8,128)(2,1)} %constant.42.clone.right_slope_ref) | copy-start | bytes 393220
  12.0 6.0 %copy-start.4 = (bf16[256,256]{1,0:T(8,128)(2,1)S(1)}, bf16[256,256]{1,0:T(8,128)(2,1)}, u32[]{:S(2)}) copy-start(bf16[256,256]{1,0:T(8,128)(2,1)} %constant.43.clone.left_basis_ref) | copy-start | bytes 393220
  12.0 6.0 %copy-start.5 = (bf16[256,256]{1,0:T(8,128)(2,1)S(1)}, bf16[256,256]{1,0:T(8,128)(2,1)}, u32[]{:S(2)}) copy-start(bf16[256,256]{1,0:T(8,128)(2,1)} %constant.44.clone.left_slope_ref) | copy-start | bytes 393220
  13.5 4.5 %copy-start = (f32[16,128,128]{2,1,0:T(8,128)S(1)}, f32[16,128,128]{2,1,0:T(8,128)}, u32[]{:S(2)}) copy-start(f32[16,128,128]{2,1,0:T(8,128)} %get-tuple-element.15.conduct_ref) | copy-start | bytes 3145732
  16.5 0.7 %copy-start.13 = (f32[4]{0:T(128)S(1)}, f32[4]{0:T(128)}, u32[]{:S(2)}) copy-start(f32[4]{0:T(128)} %param.23) | copy-start | bytes 52
  16.5 1.5 %copy-start.1 = (f32[128,128]{1,0:T(8,128)S(1)}, f32[128,128]{1,0:T(8,128)}, u32[]{:S(2)}) copy-start(f32[128,128]{1,0:T(8,128)} %constant.35.clone.rho_hbm.rho_ref) | copy-start | bytes 196612
  16.5 1.5 %copy-start.2 = (bf16[256,256]{1,0:T(8,128)(2,1)S(1)}, bf16[256,256]{1,0:T(8,128)(2,1)}, u32[]{:S(2)}) copy-start(bf16[256,256]{1,0:T(8,128)(2,1)} %constant.41.clone.right_basis_ref) | copy-start | bytes 393220
  16.5 1.4 %collective-permute-start.4 = (f32[128,128]{1,0:T(8,128)S(1)}, f32[128,128]{1,0:T(8,128)S(1)}, u32[]{:S(2)}, u32[]{:S(2)}) collective-permute-start(f32[128,128]{1,0:T(8,128)S(1)} %multiply_add_fusion), channel_id=1, source_target_pairs={{0,1},{1,0},{2,3},{3,2},{4,5},{5,4},{6,7},{7,6},{8,9},{9,8},{10,11... | collective-permute-start | bytes 196616 | tf_op jit(solution)/shard_map/ppermute | solution.py:464

commit v8 on v6

--- a/solution.py
+++ b/solution.py
@@ -296,10 +296,10 @@
     nothing = jnp.zeros((ROWS, width), jnp.float32)
     totals = (nothing,) * 12
     for step in range(pairs + 2):
+        if 1 <= step <= pairs:
+            along_y(step - 1)
         if step >= 3:
             totals = differences(step - 3, totals)
-        if 1 <= step <= pairs:
-            along_y(step - 1)
         if step < pairs:
             along_z(step)
     lines = [jnp.sum(total, axis=0, keepdims=True) for total in totals]

time: 51.9 us -> 51.9 us (level)
  no operation moved by 1% of the time
where the time goes in v8:
time: 51.9 us; the launch traced here: 51.6 us
  blocking collectives  27 us (52%)
  Pallas kernels  10.4 us (20%)
  starting transfers between devices  8.08 us (16%)
  other arithmetic  2.57 us (5%)
  waiting for transfers between devices  1.94 us (4%)
  between operations  1.55 us (3%)
    all_to_all x1, blocking collectives, on_device(): lax.all_to_all(jnp.broadcast_to(table, (groups, LANES)), 'macro', 0, 0, t...  19.5 us
    all_to_all x1, blocking collectives, on_device(): lax.all_to_all(table, 'pencil', 0, 0, tiled=True)  7.47 us
    pallas_call x1, Pallas kernels, on_device(): pl.pallas_call(moments_kernel, out_shape=jax.ShapeDtypeStruct((1, LANES),...  4.9 us
    pallas_call x1, Pallas kernels, on_device(): pl.pallas_call(analyse_kernel, out_shape=(block, block, plane, plane), in...  3.81 us
    ppermute x1, starting transfers between devices, on_device(): lax.ppermute(give, 'pencil', swap) + lax.optimization_barrier(step * keep)  3.33 us
    ppermute x3, starting transfers between devices, from_chip(): return lax.ppermute(array, 'pencil', perm)  3.15 us
    pallas_call x1, Pallas kernels, on_device(): pl.pallas_call(lambda *refs: close_kernel(own_nodes, volume, *refs), out_...  1.65 us
    ppermute x1, starting transfers between devices, on_device(): other = lax.ppermute(kept + step * own, 'pencil', swap)  1.6 us
  transfers between devices with their start and end apart: 5, of which 3 were waited for; matrix products, arithmetic and copies ran while one was open for 5% of the time, Pallas kernels for 0%

profile of v8, /device:TPU:1, one launch (start us, length us, event | category | flops | bytes accessed | tf_op | source)
XLA Modules:
  0.0 51.6 jit_solution(3490236747449340729)
XLA Ops:
  0.6 0.0 copy-start.6
  0.6 3.8 %analyse.1 = (f32[16,128,128]{2,1,0:T(8,128)}, f32[16,128,128]{2,1,0:T(8,128)}, f32[128,128]{1,0:T(8,128)}, f32[128,128]{1,0:T(8,128)}) custom-call(f32[1,3]{1,0:T(1,128)} %material_hbm.1, s32[1,16,128,128]{3,2,1,0:T(8,128)} %ids_hbm.1, f32[1,16,128,128]{3,2,1,0:T(8,128)} %fiber_hbm.1, bf16[256,256]{1,0:T(8,128)(2,1)} %constant.32.clone.right_hbm, ...), custom_call_target="tpu_custom_call" | custom-call | tf_op jit(solution)/shard_map/analyse/pallas_call | solution.py:397
  4.5 3.3 %collective-permute-start = (f32[128,128]{1,0:T(8,128)}, f32[128,128]{1,0:T(8,128)S(1)}, u32[]{:S(2)}, u32[]{:S(2)}) collective-permute-start(f32[128,128]{1,0:T(8,128)} %get-tuple-element.16), channel_id=1, source_target_pairs={{0,1},{1,0},{2,3},{3,2},{4,5},{5,4},{6,7},{7,6},{8,9},{9,8},{10,11... | collective-permute-start | bytes 196616 | tf_op jit(solution)/shard_map/ppermute | solution.py:441
  7.8 0.0 copy-done.6
  7.8 0.8 %mul.26 = f32[128,128]{1,0:T(8,128)S(1)} multiply(f32[128,128]{1,0:T(8,128)S(1)} %copy-done.6, f32[128,128]{1,0:T(8,128)} %get-tuple-element.21) | non-fusion elementwise | flops 16384 | bytes 196608 | tf_op jit(solution)/shard_map/mul | solution.py:441
  9.3 0.0 copy-start.7
  9.3 0.0 collective-permute-done
  9.3 0.0 copy-start.8
  9.4 0.1 collective-permute-start.3
  9.4 1.9 %collective-permute-start.1 = (f32[128,128]{1,0:T(8,128)S(1)}, f32[128,128]{1,0:T(8,128)S(1)}, u32[]{:S(2)}, u32[]{:S(2)}) collective-permute-start(f32[128,128]{1,0:T(8,128)S(1)} %add.17), channel_id=1, source_target_pairs={{0,4},{1,5},{2,6},{3,7},{4,0},{5,1},{6,2},{7,3},{8,12},{9,13},{10,... | collective-permute-start | bytes 196616 | tf_op jit(solution)/shard_map/ppermute | solution.py:438
  11.4 1.2 %collective-permute-start.2 = (f32[128,128]{1,0:T(8,128)S(1)}, f32[128,128]{1,0:T(8,128)S(1)}, u32[]{:S(2)}, u32[]{:S(2)}) collective-permute-start(f32[128,128]{1,0:T(8,128)S(1)} %add.17), channel_id=1, source_target_pairs={{0,2},{1,7},{2,4},{3,1},{4,6},{5,3},{6,0},{7,5},{8,10},{9,15},{10,... | collective-permute-start | bytes 196616 | tf_op jit(solution)/shard_map/ppermute | solution.py:438
  12.5 0.0 copy-start.12
  12.5 0.0 copy-start.9
  12.6 0.0 copy-start.10
  12.6 0.0 copy-start.1
  12.6 0.0 copy-start.2
  12.6 0.0 copy-start.3
  12.6 0.0 copy-start.4
  12.6 0.0 copy-start.5
  12.6 1.5 %broadcast_multiply_fusion.modes_ref = f32[16,128,128]{2,1,0:T(8,128)S(1)} fusion(f32[16,128,128]{2,1,0:T(8,128)} %get-tuple-element.19, f32[128,128]{1,0:T(8,128)S(1)} %copy-done.7), kind=kLoop, calls=%fused_computation | loop fusion | flops 262144 | bytes 2162688 | tf_op jit(solution)/shard_map/mul | solution.py:445
  14.1 0.1 and_select_fusion
  14.3 0.0 collective-permute-done.1
  14.3 0.1 collective-permute-done.3
  14.5 1.0 %collective-permute-done.2 = f32[128,128]{1,0:T(8,128)S(1)} collective-permute-done((f32[128,128]{1,0:T(8,128)S(1)}, f32[128,128]{1,0:T(8,128)S(1)}, u32[]{:S(2)}, u32[]{:S(2)}) %collective-permute-start.2) | collective-permute-done | bytes 65568 | tf_op jit(solution)/shard_map/ppermute | solution.py:438
  15.5 0.0 copy-start.13
  15.5 1.6 %collective-permute-start.4 = (f32[128,128]{1,0:T(8,128)S(1)}, f32[128,128]{1,0:T(8,128)S(1)}, u32[]{:S(2)}, u32[]{:S(2)}) collective-permute-start(f32[128,128]{1,0:T(8,128)S(1)} %get-tuple-element.28), channel_id=1, source_target_pairs={{0,1},{1,0},{2,3},{3,2},{4,5},{5,4},{6,7},{7,6},{8,9},{9,8},{10,11... | collective-permute-start | bytes 196616 | tf_op jit(solution)/shard_map/ppermute | solution.py:464
  17.1 0.1 fusion.extra_ref
  17.2 0.8 %collective-permute-done.4.other_ref = f32[128,128]{1,0:T(8,128)S(1)} collective-permute-done((f32[128,128]{1,0:T(8,128)S(1)}, f32[128,128]{1,0:T(8,128)S(1)}, u32[]{:S(2)}, u32[]{:S(2)}) %collective-permute-start.4) | collective-permute-done | bytes 65568 | tf_op jit(solution)/shard_map/ppermute | solution.py:464
  18.0 4.9 %moments.1 = f32[1,128]{1,0:T(1,128)S(1)} custom-call(f32[16,128,128]{2,1,0:T(8,128)S(1)} %copy-done, f32[16,128,128]{2,1,0:T(8,128)S(1)} %broadcast_multiply_fusion.modes_ref, f32[128,128]{1,0:T(8,128)S(1)} %get-tuple-element.29.own_ref, f32[128,128]{1,0:T(8,128)S(1)} %collective-permute-done.4.other_ref, f32[1,128]{1,0:T(1,128)S(1)} %fusion.extra_ref, ...), custom_call_target="tpu_custom_call" | custom-call | tf_op jit(solution)/shard_map/moments/pallas_call | solution.py:468
  22.9 7.5 %all_to_all.14 = f32[8,1,128]{2,1,0:T(1,128)S(1)} all-to-all(f32[8,1,128]{2,1,0:T(1,128)S(1)} %broadcast_in_dim.9), channel_id=1, replica_groups=mesh['macro'=32,'pencil'=8] {'pencil'}, dimensions={0} | all-to-all | bytes 8192 | tf_op jit(solution)/shard_map/all_to_all | solution.py:491
  30.4 19.5 %all_to_all.15 = f32[32,1,128]{2,1,0:T(1,128)S(1)} all-to-all(f32[32,1,128]{2,1,0:T(1,128)S(1)} %broadcast_in_dim.18), channel_id=1, replica_groups=mesh['macro'=32,'pencil'=8] {'macro'}, dimensions={0} | all-to-all | bytes 32768 | tf_op jit(solution)/shard_map/all_to_all | solution.py:492
  50.0 1.6 %close.1 = (f32[1,3]{1,0:T(1,128)}, f32[1,4]{1,0:T(1,128)}) custom-call(f32[32,128]{1,0:T(8,128)S(1)} %bitcast.8), custom_call_target="tpu_custom_call" | custom-call | tf_op jit(solution)/shard_map/close/pallas_call | solution.py:493
  (28 shorter events, 0.1 us)
Async XLA Ops:
  0.6 7.2 %copy-start.6 = (f32[128,128]{1,0:T(8,128)S(1)}, f32[128,128]{1,0:T(8,128)}, u32[]{:S(2)}) copy-start(f32[128,128]{1,0:T(8,128)} %constant.36.clone) | copy-start | bytes 196612
  4.5 4.9 %collective-permute-start = (f32[128,128]{1,0:T(8,128)}, f32[128,128]{1,0:T(8,128)S(1)}, u32[]{:S(2)}, u32[]{:S(2)}) collective-permute-start(f32[128,128]{1,0:T(8,128)} %get-tuple-element.16), channel_id=1, source_target_pairs={{0,1},{1,0},{2,3},{3,2},{4,5},{5,4},{6,7},{7,6},{8,9},{9,8},{10,11... | collective-permute-start | bytes 196616 | tf_op jit(solution)/shard_map/ppermute | solution.py:441
  9.3 3.2 %copy-start.7 = (f32[128,128]{1,0:T(8,128)S(1)}, f32[128,128]{1,0:T(8,128)}, u32[]{:S(2)}) copy-start(f32[128,128]{1,0:T(8,128)} %constant.34.clone.norm_hbm) | copy-start | bytes 196612
  9.3 4.8 %copy-start.8 = (f32[128,128]{1,0:T(8,128)S(1)}, f32[128,128]{1,0:T(8,128)}, u32[]{:S(2)}) copy-start(f32[128,128]{1,0:T(8,128)} %get-tuple-element.21) | copy-start | bytes 196612
  9.4 5.1 %collective-permute-start.3 = (f32[128,128]{1,0:T(8,128)S(1)}, f32[128,128]{1,0:T(8,128)S(1)}, u32[]{:S(2)}, u32[]{:S(2)}) collective-permute-start(f32[128,128]{1,0:T(8,128)S(1)} %add.17), channel_id=1, source_target_pairs={{0,6},{1,3},{2,0},{3,5},{4,2},{5,7},{6,4},{7,1},{8,14},{9,11},{10,... | collective-permute-start | bytes 196616 | tf_op jit(solution)/shard_map/ppermute | solution.py:438
  9.4 4.8 %collective-permute-start.1 = (f32[128,128]{1,0:T(8,128)S(1)}, f32[128,128]{1,0:T(8,128)S(1)}, u32[]{:S(2)}, u32[]{:S(2)}) collective-permute-start(f32[128,128]{1,0:T(8,128)S(1)} %add.17), channel_id=1, source_target_pairs={{0,4},{1,5},{2,6},{3,7},{4,0},{5,1},{6,2},{7,3},{8,12},{9,13},{10,... | collective-permute-start | bytes 196616 | tf_op jit(solution)/shard_map/ppermute | solution.py:438
  11.4 4.1 %collective-permute-start.2 = (f32[128,128]{1,0:T(8,128)S(1)}, f32[128,128]{1,0:T(8,128)S(1)}, u32[]{:S(2)}, u32[]{:S(2)}) collective-permute-start(f32[128,128]{1,0:T(8,128)S(1)} %add.17), channel_id=1, source_target_pairs={{0,2},{1,7},{2,4},{3,1},{4,6},{5,3},{6,0},{7,5},{8,10},{9,15},{10,... | collective-permute-start | bytes 196616 | tf_op jit(solution)/shard_map/ppermute | solution.py:438
  12.5 1.7 %copy-start.14 = (s32[1,8]{1,0:T(1,128)S(1)}, s32[1,8]{1,0:T(1,128)}, u32[]{:S(2)}) copy-start(s32[1,8]{1,0:T(1,128)} %param.24) | copy-start | bytes 100
  12.5 1.7 %copy-start.15 = (s32[4]{0:T(128)S(1)}, s32[4]{0:T(128)}, u32[]{:S(2)}) copy-start(s32[4]{0:T(128)} %param.25) | copy-start | bytes 52
  12.5 1.8 %copy-start.11 = (f32[128,128]{1,0:T(8,128)S(1)}, f32[128,128]{1,0:T(8,128)}, u32[]{:S(2)}) copy-start(f32[128,128]{1,0:T(8,128)} %constant.38.clone) | copy-start | bytes 196612
  12.5 1.8 %copy-start.12 = (f32[128,128]{1,0:T(8,128)S(1)}, f32[128,128]{1,0:T(8,128)}, u32[]{:S(2)}) copy-start(f32[128,128]{1,0:T(8,128)} %constant.37.clone) | copy-start | bytes 196612
  12.5 2.9 %copy-start.9 = (f32[128,128]{1,0:T(8,128)S(1)}, f32[128,128]{1,0:T(8,128)}, u32[]{:S(2)}) copy-start(f32[128,128]{1,0:T(8,128)} %constant.40.clone) | copy-start | bytes 196612
  12.6 2.9 %copy-start.10 = (f32[128,128]{1,0:T(8,128)S(1)}, f32[128,128]{1,0:T(8,128)}, u32[]{:S(2)}) copy-start(f32[128,128]{1,0:T(8,128)} %constant.39.clone) | copy-start | bytes 196612
  12.6 5.4 %copy-start.1 = (f32[128,128]{1,0:T(8,128)S(1)}, f32[128,128]{1,0:T(8,128)}, u32[]{:S(2)}) copy-start(f32[128,128]{1,0:T(8,128)} %constant.35.clone.rho_hbm.rho_ref) | copy-start | bytes 196612
  12.6 5.4 %copy-start.2 = (bf16[256,256]{1,0:T(8,128)(2,1)S(1)}, bf16[256,256]{1,0:T(8,128)(2,1)}, u32[]{:S(2)}) copy-start(bf16[256,256]{1,0:T(8,128)(2,1)} %constant.41.clone.right_basis_ref) | copy-start | bytes 393220
  12.6 5.4 %copy-start.3 = (bf16[256,256]{1,0:T(8,128)(2,1)S(1)}, bf16[256,256]{1,0:T(8,128)(2,1)}, u32[]{:S(2)}) copy-start(bf16[256,256]{1,0:T(8,128)(2,1)} %constant.42.clone.right_slope_ref) | copy-start | bytes 393220
  12.6 5.4 %copy-start.4 = (bf16[256,256]{1,0:T(8,128)(2,1)S(1)}, bf16[256,256]{1,0:T(8,128)(2,1)}, u32[]{:S(2)}) copy-start(bf16[256,256]{1,0:T(8,128)(2,1)} %constant.43.clone.left_basis_ref) | copy-start | bytes 393220
  12.6 5.4 %copy-start.5 = (bf16[256,256]{1,0:T(8,128)(2,1)S(1)}, bf16[256,256]{1,0:T(8,128)(2,1)}, u32[]{:S(2)}) copy-start(bf16[256,256]{1,0:T(8,128)(2,1)} %constant.44.clone.left_slope_ref) | copy-start | bytes 393220
  14.1 3.9 %copy-start = (f32[16,128,128]{2,1,0:T(8,128)S(1)}, f32[16,128,128]{2,1,0:T(8,128)}, u32[]{:S(2)}) copy-start(f32[16,128,128]{2,1,0:T(8,128)} %get-tuple-element.15.conduct_ref) | copy-start | bytes 3145732
  15.5 1.6 %copy-start.13 = (f32[4]{0:T(128)S(1)}, f32[4]{0:T(128)}, u32[]{:S(2)}) copy-start(f32[4]{0:T(128)} %param.23) | copy-start | bytes 52
  15.5 2.5 %collective-permute-start.4 = (f32[128,128]{1,0:T(8,128)S(1)}, f32[128,128]{1,0:T(8,128)S(1)}, u32[]{:S(2)}, u32[]{:S(2)}) collective-permute-start(f32[128,128]{1,0:T(8,128)S(1)} %get-tuple-element.28), channel_id=1, source_target_pairs={{0,1},{1,0},{2,3},{3,2},{4,5},{5,4},{6,7},{7,6},{8,9},{9,8},{10,11... | collective-permute-start | bytes 196616 | tf_op jit(solution)/shard_map/ppermute | solution.py:464
